TPU v7x, 128 devices: a whole 4x4x4 slice. The times are simulated.
128 devices in a mesh: section: 2 (over core), fsdp: 16 (over x, z), rep: 4 (over y).
Axes of the slice: x: 4, y: 4, z: 4, core: 2. Of those that a mesh axis runs over, the one named last changes fastest.
Arguments:
- layer_in: bfloat16 [2, 64, 64, 768], P(None, ('fsdp', 'rep')), may hold values from -6 to 6
- cotangent: bfloat16 [2, 64, 64, 768], P(None, ('fsdp', 'rep')), may hold values from -6 to 6
- encoder: bfloat16 [2, 64, 256, 768], P(None, ('fsdp', 'rep')), may hold values from -6 to 6
- dec_segments: int32 [2, 64, 64], P(None, ('fsdp', 'rep')), may hold values from 0 to 3, as said below
- enc_segments: int32 [2, 64, 256], P(None, ('fsdp', 'rep')), may hold values from 0 to 3, as said below
- norm_gains: bfloat16 [2, 3, 768], P('section', None, 'fsdp'), may hold values from 0.5 to 1.5
- self_query: bfloat16 [2, 768, 768], P('section', 'fsdp'), may hold values from -0.02734375 to 0.02734375
- self_kv: bfloat16 [2, 768, 2, 768], P('section', 'fsdp'), may hold values from -0.21875 to 0.21875
- self_out: bfloat16 [2, 768, 768], P('section', 'fsdp'), may hold values from -0.875 to 0.875
- rel_bias: bfloat16 [2, 32, 12], P('section', 'fsdp'), may hold values from -6 to 6
- cross_query: bfloat16 [2, 768, 768], P('section', 'fsdp'), may hold values from -0.02734375 to 0.02734375
- cross_kv: bfloat16 [2, 768, 2, 768], P('section', 'fsdp'), may hold values from -0.21875 to 0.21875
- cross_out: bfloat16 [2, 768, 768], P('section', 'fsdp'), may hold values from -1.25 to 1.25
- ffn_in: bfloat16 [2, 768, 2, 2048], P('section', 'fsdp'), may hold values from -0.21875 to 0.21875
- ffn_out: bfloat16 [2, 2048, 768], P('section', 'fsdp'), may hold values from -0.25 to 0.25
Outputs:
- layer_out: bfloat16 [2, 2, 64, 64, 768], P('section', None, ('fsdp', 'rep'))
- layer_grad: bfloat16 [2, 2, 64, 64, 768], P('section', None, ('fsdp', 'rep'))
- encoder_grad: float32 [2, 64, 256, 768], P(None, ('fsdp', 'rep'))
- grad_norm_gains: float32 [2, 3, 768], P('section', None, 'fsdp')
- grad_self_query: float32 [2, 768, 768], P('section', 'fsdp')
- grad_self_kv: float32 [2, 768, 2, 768], P('section', 'fsdp')
- grad_self_out: float32 [2, 768, 768], P('section', 'fsdp')
- grad_rel_bias: float32 [2, 32, 12], P('section', 'fsdp')
- grad_cross_query: float32 [2, 768, 768], P('section', 'fsdp')
- grad_cross_kv: float32 [2, 768, 2, 768], P('section', 'fsdp')
- grad_cross_out: float32 [2, 768, 768], P('section', 'fsdp')
- grad_ffn_in: float32 [2, 768, 2, 2048], P('section', 'fsdp')
- grad_ffn_out: float32 [2, 2048, 768], P('section', 'fsdp')
Inputs may be any that keep to these rules, and one draw needn't show every extreme that they name: `dec_segments`: within each packed row the ids start at 0 and rise by one at each of 3 places, so every id of 0 to 3 is present. `enc_segments`: within each row of encoder states the ids start at 0 and rise by one at each of 3 places, so every id of 0 to 3 is present.
All inputs are finite; a program needn't handle non-finite values.
Results may differ from a plain program's by a relative error of at most 0.035.
Values may be sent and summed in bfloat16 or wider, within the bound.
No kernel may reach another device: no remote copies, remote signals or barrier semaphores. Data moves between devices by JAX's collectives and lax.ppermute only.
A program may use at most 128 MiB of HBM per device.

v0:
```python
import jax
import jax.numpy as jnp
import numpy as np
from jax import lax
from jax.sharding import PartitionSpec as P

HEADS = 12
HEAD = 64
BUCKETS = 32
MAX_DIST = 128


epsilon = 1e-06
highest = lax.Precision.HIGHEST


def shifted_2(value, axis, steps):
    count = lax.axis_size(axis)
    first, last = (max(0, -steps), min(count, count - steps))
    return lax.ppermute(value, axis, [(source, source + steps) for source in range(first, last)])


def bucket_row(length):
    distance = np.arange(length)
    half_count = BUCKETS // 2
    scaled = (
        np.log(np.maximum(distance, half_count) / half_count)
        / np.log(MAX_DIST / half_count)
        * (BUCKETS - half_count)
    )
    far_bucket = np.minimum(half_count + np.floor(scaled).astype(np.int32), BUCKETS - 1)
    return np.where(distance < half_count, distance, far_bucket).astype(np.int32)


def bucket_onehot(length):
    return (bucket_row(length)[None, :] == np.arange(BUCKETS)[:, None]).astype(np.float32)


def spread_distance(by_distance):
    head_count, length = by_distance.shape
    padded_row = jnp.concatenate(
        [jnp.zeros((head_count, length - 1), jnp.float32), by_distance], axis=1
    )
    tiled = jnp.tile(padded_row, (1, length))
    tiled = jnp.concatenate([tiled, jnp.zeros((head_count, length), jnp.float32)], axis=1)
    return tiled.reshape(head_count, length, 2 * length)[:, :, :length][:, :, ::-1]


def gather_distance(grid):
    head_count, length, _ = grid.shape
    flipped = jnp.concatenate(
        [grid[:, :, ::-1], jnp.zeros((head_count, length, length), jnp.float32)], axis=2
    )
    flat = flipped.reshape(head_count, 2 * length * length)[:, : length * (2 * length - 1)]
    return jnp.sum(flat.reshape(head_count, length, 2 * length - 1), axis=1)[:, length - 1 :]


def normalize(value, gain):
    return value * lax.rsqrt(jnp.mean(value * value, axis=-1, keepdims=True) + epsilon) * gain


def geglu(gate_rows, up_rows):
    return jax.nn.gelu(gate_rows, approximate=True) * up_rows


def split_heads(matrix):
    return matrix.reshape(matrix.shape[0], HEADS, HEAD)


def attend_forward(queries, key_rows, value_rows, position_bias, allowed):
    scores = (
        jnp.einsum(
            "qhe,khe->hqk",
            split_heads(queries),
            split_heads(key_rows),
            preferred_element_type=jnp.float32,
        )
        + position_bias
    )
    scores = jnp.where(allowed[None], scores, -jnp.inf)
    shifted = jnp.exp(scores - jnp.max(scores, axis=-1, keepdims=True))
    probability = shifted / jnp.sum(shifted, axis=-1, keepdims=True)
    attended = jnp.einsum(
        "hqk,khe->qhe",
        probability.astype(jnp.bfloat16),
        split_heads(value_rows),
        preferred_element_type=jnp.float32,
    )
    return (attended.reshape(queries.shape[0], HEADS * HEAD).astype(jnp.bfloat16), probability)


def attend_backward(grad_attended, queries, key_rows, value_rows, probability, allowed):
    width = HEADS * HEAD
    grad_heads = split_heads(grad_attended)
    grad_prob = jnp.einsum(
        "qhe,khe->hqk", grad_heads, split_heads(value_rows), preferred_element_type=jnp.float32
    )
    grad_values = jnp.einsum(
        "hqk,qhe->khe",
        probability.astype(jnp.bfloat16),
        grad_heads,
        preferred_element_type=jnp.float32,
    )
    grad_scores = probability * (
        grad_prob - jnp.sum(probability * grad_prob, axis=-1, keepdims=True)
    )
    grad_scores = jnp.where(allowed[None], grad_scores, 0.0).astype(jnp.bfloat16)
    grad_queries = jnp.einsum(
        "hqk,khe->qhe", grad_scores, split_heads(key_rows), preferred_element_type=jnp.float32
    )
    grad_keys = jnp.einsum(
        "hqk,qhe->khe", grad_scores, split_heads(queries), preferred_element_type=jnp.float32
    )
    return (
        grad_queries.reshape(-1, width).astype(jnp.bfloat16),
        grad_keys.reshape(-1, width).astype(jnp.bfloat16),
        grad_values.reshape(-1, width).astype(jnp.bfloat16),
        grad_scores,
    )


def layer_forward(layer_input, encoder_rows, dec_ids, enc_ids, weights):
    norm_gain, w_query, w_kv, w_out, bias_table, c_query, c_kv, c_out, w_in, w_ffn = weights
    length = layer_input.shape[0]
    positions = jnp.arange(length)
    self_allowed = (dec_ids[:, None] == dec_ids[None, :]) & (
        positions[None, :] <= positions[:, None]
    )
    cross_allowed = dec_ids[:, None] == enc_ids[None, :]
    by_distance = jnp.dot(
        bias_table.astype(jnp.float32).T, bucket_onehot(length), precision=highest
    )
    position_bias = spread_distance(by_distance)
    gain_wide = norm_gain.astype(jnp.float32)
    norm_one = normalize(layer_input, gain_wide[0]).astype(jnp.bfloat16)
    queries = jnp.dot(norm_one, w_query, preferred_element_type=jnp.float32).astype(jnp.bfloat16)
    key_value = jnp.einsum(
        "ld,dcj->clj", norm_one, w_kv, preferred_element_type=jnp.float32
    ).astype(jnp.bfloat16)
    attended, probability = attend_forward(
        queries, key_value[0], key_value[1], position_bias, self_allowed
    )
    after_self = layer_input + jnp.dot(attended, w_out, preferred_element_type=jnp.float32)
    norm_two = normalize(after_self, gain_wide[1]).astype(jnp.bfloat16)
    cross_queries = jnp.dot(norm_two, c_query, preferred_element_type=jnp.float32).astype(
        jnp.bfloat16
    )
    cross_pair = jnp.einsum(
        "kd,dcj->ckj", encoder_rows, c_kv, preferred_element_type=jnp.float32
    ).astype(jnp.bfloat16)
    cross_attended, cross_prob = attend_forward(
        cross_queries, cross_pair[0], cross_pair[1], 0.0, cross_allowed
    )
    after_cross = after_self + jnp.dot(cross_attended, c_out, preferred_element_type=jnp.float32)
    norm_three = normalize(after_cross, gain_wide[2]).astype(jnp.bfloat16)
    gate_up = jnp.einsum("ld,dcf->clf", norm_three, w_in, preferred_element_type=jnp.float32)
    hidden = geglu(gate_up[0], gate_up[1]).astype(jnp.bfloat16)
    result = after_cross + jnp.dot(hidden, w_ffn, preferred_element_type=jnp.float32)
    saved = (
        layer_input,
        encoder_rows,
        self_allowed,
        cross_allowed,
        norm_one,
        queries,
        key_value,
        probability,
        attended,
        after_self,
        norm_two,
        cross_queries,
        cross_pair,
        cross_prob,
        cross_attended,
        after_cross,
        norm_three,
        gate_up,
        hidden,
    )
    return (result, saved)


def layer_backward(grad_out, saved, weights):
    norm_gain, w_query, w_kv, w_out, bias_table, c_query, c_kv, c_out, w_in, w_ffn = weights
    (
        layer_input,
        encoder_rows,
        self_allowed,
        cross_allowed,
        norm_one,
        queries,
        key_value,
        probability,
        attended,
        after_self,
        norm_two,
        cross_queries,
        cross_pair,
        cross_prob,
        cross_attended,
        after_cross,
        norm_three,
        gate_up,
        hidden,
    ) = saved
    gain_wide = norm_gain.astype(jnp.float32)
    grad_ffn = grad_out.astype(jnp.bfloat16)
    grad_hidden = jnp.einsum("ld,fd->lf", grad_ffn, w_ffn, preferred_element_type=jnp.float32)
    _, pull_gate = jax.vjp(geglu, gate_up[0], gate_up[1])
    grad_gate, grad_up = pull_gate(grad_hidden)
    grad_gate_up = jnp.stack([grad_gate, grad_up]).astype(jnp.bfloat16)
    grad_norm = jnp.einsum("clf,dcf->ld", grad_gate_up, w_in, preferred_element_type=jnp.float32)
    _, pull_norm = jax.vjp(normalize, after_cross, gain_wide[2])
    grad_back, grad_gain_three = pull_norm(grad_norm)
    grad_stream = grad_out + grad_back
    grad_cross_branch = grad_stream.astype(jnp.bfloat16)
    grad_cross_att = jnp.einsum(
        "ld,jd->lj", grad_cross_branch, c_out, preferred_element_type=jnp.float32
    ).astype(jnp.bfloat16)
    grad_cross_q, grad_cross_k, grad_cross_v, _ = attend_backward(
        grad_cross_att, cross_queries, cross_pair[0], cross_pair[1], cross_prob, cross_allowed
    )
    grad_cross_pair = jnp.stack([grad_cross_k, grad_cross_v])
    grad_encoder = jnp.einsum(
        "ckj,dcj->kd", grad_cross_pair, c_kv, preferred_element_type=jnp.float32
    )
    grad_norm = jnp.einsum("lj,dj->ld", grad_cross_q, c_query, preferred_element_type=jnp.float32)
    _, pull_norm = jax.vjp(normalize, after_self, gain_wide[1])
    grad_back, grad_gain_two = pull_norm(grad_norm)
    grad_stream = grad_stream + grad_back
    grad_self_branch = grad_stream.astype(jnp.bfloat16)
    grad_self_att = jnp.einsum(
        "ld,jd->lj", grad_self_branch, w_out, preferred_element_type=jnp.float32
    ).astype(jnp.bfloat16)
    grad_queries, grad_keys, grad_values, grad_scores = attend_backward(
        grad_self_att, queries, key_value[0], key_value[1], probability, self_allowed
    )
    grad_pair = jnp.stack([grad_keys, grad_values])
    grad_norm = jnp.einsum(
        "lj,dj->ld", grad_queries, w_query, preferred_element_type=jnp.float32
    ) + jnp.einsum("clj,dcj->ld", grad_pair, w_kv, preferred_element_type=jnp.float32)
    _, pull_norm = jax.vjp(normalize, layer_input, gain_wide[0])
    grad_back, grad_gain_one = pull_norm(grad_norm)
    grad_input = grad_stream + grad_back
    length = layer_input.shape[0]
    diagonal_sums = gather_distance(grad_scores.astype(jnp.float32))
    grad_table = jnp.dot(bucket_onehot(length), diagonal_sums.T, precision=highest)
    grad_gains = jnp.stack([grad_gain_one, grad_gain_two, grad_gain_three])
    rows_for_weights = (
        norm_one,
        grad_queries,
        grad_pair,
        attended,
        grad_self_branch,
        norm_two,
        grad_cross_q,
        encoder_rows,
        grad_cross_pair,
        cross_attended,
        grad_cross_branch,
        norm_three,
        grad_gate_up,
        hidden,
        grad_ffn,
        grad_gains,
        grad_table,
    )
    return (grad_input, grad_encoder, rows_for_weights)


def weight_grads(records):

    def joined(slot_index, along):
        return jnp.concatenate([record[slot_index] for record in records], axis=along)

    norm_one = joined(0, 0)
    grad_query = jnp.einsum("ld,lj->dj", norm_one, joined(1, 0), preferred_element_type=jnp.float32)
    grad_kv = jnp.einsum("ld,clj->dcj", norm_one, joined(2, 1), preferred_element_type=jnp.float32)
    grad_out = jnp.einsum(
        "lj,ld->jd", joined(3, 0), joined(4, 0), preferred_element_type=jnp.float32
    )
    grad_c_query = jnp.einsum(
        "ld,lj->dj", joined(5, 0), joined(6, 0), preferred_element_type=jnp.float32
    )
    grad_c_kv = jnp.einsum(
        "kd,ckj->dcj", joined(7, 0), joined(8, 1), preferred_element_type=jnp.float32
    )
    grad_c_out = jnp.einsum(
        "lj,ld->jd", joined(9, 0), joined(10, 0), preferred_element_type=jnp.float32
    )
    grad_in = jnp.einsum(
        "ld,clf->dcf", joined(11, 0), joined(12, 1), preferred_element_type=jnp.float32
    )
    grad_ffn = jnp.einsum(
        "lf,ld->fd", joined(13, 0), joined(14, 0), preferred_element_type=jnp.float32
    )
    grad_gains = jnp.sum(jnp.stack([record[15] for record in records]), axis=0)
    grad_table = jnp.sum(jnp.stack([record[16] for record in records]), axis=0)
    return (
        grad_gains,
        grad_query,
        grad_kv,
        grad_out,
        grad_table,
        grad_c_query,
        grad_c_kv,
        grad_c_out,
        grad_in,
        grad_ffn,
    )


def shards(
    layer_in,
    cotangent,
    encoder,
    dec_segments,
    enc_segments,
    norm_gains,
    self_query,
    self_kv,
    self_out,
    rel_bias,
    cross_query,
    cross_kv,
    cross_out,
    ffn_in,
    ffn_out,
):
    section_index = lax.axis_index("section")
    batches = layer_in.shape[0]
    length = layer_in.shape[2]
    width = layer_in.shape[3]
    gathered = (
        lax.all_gather(norm_gains, "fsdp", axis=2, tiled=True),
        lax.all_gather(self_query, "fsdp", axis=1, tiled=True),
        lax.all_gather(self_kv, "fsdp", axis=1, tiled=True),
        lax.all_gather(self_out, "fsdp", axis=1, tiled=True),
        lax.all_gather(rel_bias, "fsdp", axis=1, tiled=True),
        lax.all_gather(cross_query, "fsdp", axis=1, tiled=True),
        lax.all_gather(cross_kv, "fsdp", axis=1, tiled=True),
        lax.all_gather(cross_out, "fsdp", axis=1, tiled=True),
        lax.all_gather(ffn_in, "fsdp", axis=1, tiled=True),
        lax.all_gather(ffn_out, "fsdp", axis=1, tiled=True),
    )
    weights = tuple((member[0] for member in gathered))
    slot_ids = jnp.arange(batches)
    received = jnp.zeros((length, width), jnp.bfloat16)
    outputs = jnp.zeros((batches, length, width), jnp.bfloat16)
    saved_list = []
    for moment in range(batches + 1):
        micro_batch = moment - section_index
        picked = jnp.clip(micro_batch, 0, batches - 1)
        current = jnp.where(section_index == 0, layer_in[min(moment, batches - 1), 0], received)
        encoder_rows = lax.dynamic_index_in_dim(encoder[:, 0], picked, 0, keepdims=False)
        dec_ids = lax.dynamic_index_in_dim(dec_segments[:, 0], picked, 0, keepdims=False)
        enc_ids = lax.dynamic_index_in_dim(enc_segments[:, 0], picked, 0, keepdims=False)
        result, saved = layer_forward(
            current.astype(jnp.float32), encoder_rows, dec_ids, enc_ids, weights
        )
        sent_rows = result.astype(jnp.bfloat16)
        outputs = jnp.where((slot_ids == micro_batch)[:, None, None], sent_rows[None], outputs)
        saved_list.append(saved)
        if moment < batches:
            received = shifted_2(sent_rows, "section", 1)
    regathered = (
        lax.all_gather(norm_gains, "fsdp", axis=2, tiled=True),
        lax.all_gather(self_query, "fsdp", axis=1, tiled=True),
        lax.all_gather(self_kv, "fsdp", axis=1, tiled=True),
        lax.all_gather(self_out, "fsdp", axis=1, tiled=True),
        lax.all_gather(rel_bias, "fsdp", axis=1, tiled=True),
        lax.all_gather(cross_query, "fsdp", axis=1, tiled=True),
        lax.all_gather(cross_kv, "fsdp", axis=1, tiled=True),
        lax.all_gather(cross_out, "fsdp", axis=1, tiled=True),
        lax.all_gather(ffn_in, "fsdp", axis=1, tiled=True),
        lax.all_gather(ffn_out, "fsdp", axis=1, tiled=True),
    )
    back_weights = tuple((member[0] for member in regathered))
    returned = jnp.zeros((length, width), jnp.bfloat16)
    input_grads = jnp.zeros((batches, length, width), jnp.bfloat16)
    encoder_sum = jnp.zeros((batches, encoder.shape[2], width), jnp.float32)
    records = []
    owned = None
    for moment in range(batches + 1):
        micro_batch = batches - moment - section_index
        given = cotangent[max(batches - 1 - moment, 0), 0]
        incoming = jnp.where(section_index == 1, given, returned).astype(jnp.float32)
        live = (micro_batch >= 0) & (micro_batch < batches)
        incoming = jnp.where(live, incoming, 0.0)
        grad_input, grad_encoder, rows_for_weights = layer_backward(
            incoming, saved_list[batches - moment], back_weights
        )
        grad_low = grad_input.astype(jnp.bfloat16)
        hit_slot = (slot_ids == micro_batch)[:, None, None]
        input_grads = jnp.where(hit_slot, grad_low[None], input_grads)
        encoder_sum = encoder_sum + jnp.where(hit_slot, grad_encoder[None], 0.0)
        records.append(rows_for_weights)
        if moment < batches:
            returned = shifted_2(grad_low, "section", -1)
    encoder_total = lax.psum(encoder_sum.astype(jnp.bfloat16), "section").astype(jnp.float32)
    full_grads = weight_grads(records)
    owned = (
        lax.psum_scatter(
            full_grads[0][None].astype(jnp.bfloat16), "fsdp", scatter_dimension=2, tiled=True
        ).astype(jnp.float32),
        lax.psum_scatter(
            full_grads[1][None].astype(jnp.bfloat16), "fsdp", scatter_dimension=1, tiled=True
        ).astype(jnp.float32),
        lax.psum_scatter(
            full_grads[2][None].astype(jnp.bfloat16), "fsdp", scatter_dimension=1, tiled=True
        ).astype(jnp.float32),
        lax.psum_scatter(
            full_grads[3][None].astype(jnp.bfloat16), "fsdp", scatter_dimension=1, tiled=True
        ).astype(jnp.float32),
        lax.psum_scatter(
            full_grads[4][None].astype(jnp.bfloat16), "fsdp", scatter_dimension=1, tiled=True
        ).astype(jnp.float32),
        lax.psum_scatter(
            full_grads[5][None].astype(jnp.bfloat16), "fsdp", scatter_dimension=1, tiled=True
        ).astype(jnp.float32),
        lax.psum_scatter(
            full_grads[6][None].astype(jnp.bfloat16), "fsdp", scatter_dimension=1, tiled=True
        ).astype(jnp.float32),
        lax.psum_scatter(
            full_grads[7][None].astype(jnp.bfloat16), "fsdp", scatter_dimension=1, tiled=True
        ).astype(jnp.float32),
        lax.psum_scatter(
            full_grads[8][None].astype(jnp.bfloat16), "fsdp", scatter_dimension=1, tiled=True
        ).astype(jnp.float32),
        lax.psum_scatter(
            full_grads[9][None].astype(jnp.bfloat16), "fsdp", scatter_dimension=1, tiled=True
        ).astype(jnp.float32),
    )
    summed = (
        lax.psum(owned[0].astype(jnp.bfloat16), "rep").astype(jnp.float32),
        lax.psum(owned[1].astype(jnp.bfloat16), "rep").astype(jnp.float32),
        lax.psum(owned[2].astype(jnp.bfloat16), "rep").astype(jnp.float32),
        lax.psum(owned[3].astype(jnp.bfloat16), "rep").astype(jnp.float32),
        lax.psum(owned[4].astype(jnp.bfloat16), "rep").astype(jnp.float32),
        lax.psum(owned[5].astype(jnp.bfloat16), "rep").astype(jnp.float32),
        lax.psum(owned[6].astype(jnp.bfloat16), "rep").astype(jnp.float32),
        lax.psum(owned[7].astype(jnp.bfloat16), "rep").astype(jnp.float32),
        lax.psum(owned[8].astype(jnp.bfloat16), "rep").astype(jnp.float32),
        lax.psum(owned[9].astype(jnp.bfloat16), "rep").astype(jnp.float32),
    )
    return (
        outputs[None, :, None],
        input_grads[None, :, None],
        encoder_total[:, None],
        summed[0],
        summed[1],
        summed[2],
        summed[3],
        summed[4],
        summed[5],
        summed[6],
        summed[7],
        summed[8],
        summed[9],
    )


def solution(mesh):
    return jax.shard_map(
        shards,
        mesh=mesh,
        in_specs=(
            P(None, ("fsdp", "rep"), None, None),
            P(None, ("fsdp", "rep"), None, None),
            P(None, ("fsdp", "rep"), None, None),
            P(None, ("fsdp", "rep"), None),
            P(None, ("fsdp", "rep"), None),
            P("section", None, "fsdp"),
            P("section", "fsdp", None),
            P("section", "fsdp", None, None),
            P("section", "fsdp", None),
            P("section", "fsdp", None),
            P("section", "fsdp", None),
            P("section", "fsdp", None, None),
            P("section", "fsdp", None),
            P("section", "fsdp", None, None),
            P("section", "fsdp", None),
        ),
        out_specs=(
            P("section", None, ("fsdp", "rep"), None, None),
            P("section", None, ("fsdp", "rep"), None, None),
            P(None, ("fsdp", "rep"), None, None),
            P("section", None, "fsdp"),
            P("section", "fsdp", None),
            P("section", "fsdp", None, None),
            P("section", "fsdp", None),
            P("section", "fsdp", None),
            P("section", "fsdp", None),
            P("section", "fsdp", None, None),
            P("section", "fsdp", None),
            P("section", "fsdp", None, None),
            P("section", "fsdp", None),
        ),
        check_vma=False,
    )
```

profile of v0, /device:TPU:1, one launch (start us, length us, event | category | flops | bytes accessed | tf_op | source)
XLA Modules:
  0.0 1333.3 jit_solution(8427287147905890458)
XLA Ops:
  16.2 20.8 %all_gather.42 = bf16[1,32,12]{2,0,1:T(2,128)(2,1)S(1)} all-gather(bf16[1,2,12]{2,0,1:T(2,128)(2,1)S(1)} %copy.277), channel_id=1, replica_groups=mesh['section'=2,'fsdp'=16,'rep'=4] {'fsdp'}, dimensions={1}, use_global_device_ids=true | all-gather | bytes 816 | tf_op jit(solution)/shard_map/all_gather | solution.py:339
  37.2 18.5 %all_gather.39 = bf16[1,3,768]{1,0,2:T(2,128)(2,1)S(1)} all-gather(bf16[1,3,48]{1,0,2:T(2,128)(2,1)S(1)} %copy.273), channel_id=1, replica_groups=mesh['section'=2,'fsdp'=16,'rep'=4] {'fsdp'}, dimensions={2}, use_global_device_ids=true | all-gather | bytes 4896 | tf_op jit(solution)/shard_map/all_gather | solution.py:335
  59.1 7.6 slice_reduce_fusion
  68.6 35.2 %all-gather.9.cloned.1.call-done = bf16[1,768,2,768]{3,1,2,0:T(8,128)(2,1)} async-done(((bf16[1,48,2,768]{3,1,2,0:T(8,128)(2,1)}), bf16[1,768,2,768]{3,1,2,0:T(8,128)(2,1)}) %all-gather.9.cloned.1.call-update) | async-done | bytes 2359312 | tf_op jit(solution)/shard_map/all_gather | solution.py:337
  107.8 40.7 %all-gather.13.cloned.1.call-done = bf16[1,768,768]{2,1,0:T(8,128)(2,1)} async-done(((bf16[1,48,768]{2,1,0:T(8,128)(2,1)}), bf16[1,768,768]{2,1,0:T(8,128)(2,1)}) %all-gather.13.cloned.1.call-update) | async-done | bytes 1179664 | tf_op jit(solution)/shard_map/all_gather | solution.py:338
  150.9 42.1 %all-gather.17.cloned.1.call-done = bf16[1,768,768]{2,1,0:T(8,128)(2,1)} async-done(((bf16[1,48,768]{2,1,0:T(8,128)(2,1)}), bf16[1,768,768]{2,1,0:T(8,128)(2,1)}) %all-gather.17.cloned.1.call-update) | async-done | bytes 1179664 | tf_op jit(solution)/shard_map/all_gather | solution.py:340
  194.8 45.8 %all-gather.15.cloned.1.call-done = bf16[1,768,2,768]{3,1,2,0:T(8,128)(2,1)} async-done(((bf16[1,48,2,768]{3,1,2,0:T(8,128)(2,1)}), bf16[1,768,2,768]{3,1,2,0:T(8,128)(2,1)}) %all-gather.15.cloned.1.call-update) | async-done | bytes 2359312 | tf_op jit(solution)/shard_map/all_gather | solution.py:341
  240.6 2.4 fusion.129
  245.6 39.6 %all-gather.19.cloned.1.call-done = bf16[1,768,768]{2,1,0:T(8,128)(2,1)} async-done(((bf16[1,48,768]{2,1,0:T(8,128)(2,1)}), bf16[1,768,768]{2,1,0:T(8,128)(2,1)}) %all-gather.19.cloned.1.call-update) | async-done | bytes 1179664 | tf_op jit(solution)/shard_map/all_gather | solution.py:342
  287.1 3.7 fusion.126
  292.6 56.4 %all-gather.21.cloned.1.call-done = bf16[1,768,2,2048]{3,1,2,0:T(8,128)(2,1)} async-done(((bf16[1,48,2,2048]{3,1,2,0:T(8,128)(2,1)}), bf16[1,768,2,2048]{3,1,2,0:T(8,128)(2,1)}) %all-gather.21.cloned.1.call-update) | async-done | bytes 6291472 | tf_op jit(solution)/shard_map/all_gather | solution.py:343
  348.9 4.0 fusion.37
  352.9 45.6 %all-gather.23.cloned.1.call-done = bf16[1,2048,768]{2,1,0:T(8,128)(2,1)} async-done(((bf16[1,128,768]{2,1,0:T(8,128)(2,1)}), bf16[1,2048,768]{2,1,0:T(8,128)(2,1)}) %all-gather.23.cloned.1.call-update) | async-done | bytes 3145744 | tf_op jit(solution)/shard_map/all_gather | solution.py:344
  398.5 3.3 fusion.331
  428.9 2.2 fusion.310
  432.9 3.0 fusion.726
  435.8 2.7 convolution_convert_fusion.25
  441.1 4.2 fusion.40
  477.7 3.0 fusion.728
  480.7 2.7 convolution_convert_fusion.23
  485.5 4.2 fusion.43
  498.1 2.3 fusion.737
  500.4 6.6 convolution_convert_fusion.22
  507.0 2.5 multiply_reduce_fusion.11
  519.6 2.5 convolution_convert_fusion.20
  522.1 2.4 convolution_convert_fusion.21
  531.6 5.1 collective-permute-start.2
  538.2 4.1 fusion.525
  542.3 5.6 multiply_reduce_fusion.8
  552.2 2.3 fusion.738
  554.5 6.6 convolution_convert_fusion.18
  561.2 2.5 multiply_reduce_fusion.9
  573.8 2.5 convolution_convert_fusion.16
  576.3 2.4 convolution_convert_fusion.17
  585.8 3.8 collective-permute-start.3
  591.3 4.1 fusion.524
  595.4 5.6 multiply_reduce_fusion.6
  605.3 2.4 fusion.739
  607.7 6.6 convolution_convert_fusion.14
  614.3 3.0 fusion.100
  617.6 2.5 multiply_reduce_fusion.7
  625.0 2.8 fusion.101
  627.9 2.5 fusion.304
  634.0 2.5 convolution_convert_fusion.12
  642.0 2.4 fusion.268
  650.4 5.9 convolution_convert_fusion.10
  659.3 6.7 convolution_convert_fusion.8
  671.3 6.7 convolution_convert_fusion.6
  682.6 4.8 convert_bitcast_fusion.1
  692.1 2.8 fusion.36
  696.3 3.7 convert_bitcast_fusion
  707.9 2.5 fusion.111
  714.6 2.6 fusion.325
  719.1 45.2 %reduce-scatter.14.cloned.1.call-done = bf16[1,48,768]{2,1,0:T(8,128)(2,1)} async-done(((bf16[1,768,768]{2,1,0:T(8,128)(2,1)}), bf16[1,48,768]{2,1,0:T(8,128)(2,1)}) %reduce-scatter.14.cloned.1.call-update) | async-done | bytes 73744 | tf_op jit(solution)/shard_map/reduce_scatter | solution.py:412
  764.3 75.9 %reduce-scatter.20.cloned.1.call-done = bf16[1,48,768]{2,1,0:T(8,128)(2,1)} async-done(((bf16[1,768,768]{2,1,0:T(8,128)(2,1)}), bf16[1,48,768]{2,1,0:T(8,128)(2,1)}) %reduce-scatter.20.cloned.1.call-update) | async-done | bytes 73744 | tf_op jit(solution)/shard_map/reduce_scatter | solution.py:424
  840.2 76.2 %reduce-scatter.10.cloned.1.call-done = bf16[1,48,768]{2,1,0:T(8,128)(2,1)} async-done(((bf16[1,768,768]{2,1,0:T(8,128)(2,1)}), bf16[1,48,768]{2,1,0:T(8,128)(2,1)}) %reduce-scatter.10.cloned.1.call-update) | async-done | bytes 73744 | tf_op jit(solution)/shard_map/reduce_scatter | solution.py:406
  916.3 77.6 %reduce-scatter.18.cloned.1.call-done = bf16[1,48,2,768]{3,1,2,0:T(8,128)(2,1)} async-done(((bf16[1,768,2,768]{3,1,2,0:T(8,128)(2,1)}), bf16[1,48,2,768]{3,1,2,0:T(8,128)(2,1)}) %reduce-scatter.18.cloned.1.call-update) | async-done | bytes 147472 | tf_op jit(solution)/shard_map/reduce_scatter | solution.py:421
  993.9 77.5 %reduce-scatter.12.cloned.1.call-done = bf16[1,48,2,768]{3,1,2,0:T(8,128)(2,1)} async-done(((bf16[1,768,2,768]{3,1,2,0:T(8,128)(2,1)}), bf16[1,48,2,768]{3,1,2,0:T(8,128)(2,1)}) %reduce-scatter.12.cloned.1.call-update) | async-done | bytes 147472 | tf_op jit(solution)/shard_map/reduce_scatter | solution.py:409
  1071.4 78.2 %reduce-scatter.24.cloned.1.call-done = bf16[1,128,768]{2,1,0:T(8,128)(2,1)} async-done(((bf16[1,2048,768]{2,1,0:T(8,128)(2,1)}), bf16[1,128,768]{2,1,0:T(8,128)(2,1)}) %reduce-scatter.24.cloned.1.call-update) | async-done | bytes 196624 | tf_op jit(solution)/shard_map/reduce_scatter | solution.py:430
  1149.6 84.6 %reduce-scatter.22.cloned.1.call-done = bf16[1,48,2,2048]{3,1,2,0:T(8,128)(2,1)} async-done(((bf16[1,768,2,2048]{3,1,2,0:T(8,128)(2,1)}), bf16[1,48,2,2048]{3,1,2,0:T(8,128)(2,1)}) %reduce-scatter.22.cloned.1.call-update) | async-done | bytes 393232 | tf_op jit(solution)/shard_map/reduce_scatter | solution.py:427
  1236.4 58.0 %all-reduce.11 = (bf16[1,3,768]{2,0,1:T(2,128)(2,1)S(1)}, bf16[1,32,12]{2,0,1:T(2,128)(2,1)S(1)}) all-reduce(bf16[1,3,768]{2,0,1:T(2,128)(2,1)S(1)} %fusion.626, bf16[1,32,12]{2,0,1:T(2,128)(2,1)S(1)} %copy.349), channel_id=2, replica_groups=mesh['section'=2,'fsdp'=16,'rep'=4] {'fsdp'}, use_global_device_ids=true, to_apply=%region_46.47.clone | all-reduce | flops 2688 | bytes 10752
  1294.6 8.4 all-reduce.12
  1306.2 2.4 broadcast_in_dim.350
  1308.6 4.6 all-reduce.19.cloned.1.call-done
  (663 shorter events, 217.3 us)
Async XLA Ops:
  7.2 48.9 %copy-start.111 = (f32[32,64]{1,0:T(8,128)S(1)}, f32[32,64]{1,0:T(8,128)}, u32[]{:S(2)}) copy-start(f32[32,64]{1,0:T(8,128)} %constant.98.clone) | copy-start | bytes 24580
  7.2 8.7 copy-start.194
  7.2 8.7 copy-start.174
  7.2 8.8 copy-start.173
  7.2 29.8 %copy-start.177 = (bf16[1,3,48]{2,1,0:T(4,128)(2,1)S(1)}, bf16[1,3,48]{2,1,0:T(4,128)(2,1)}, u32[]{:S(2)}) copy-start(bf16[1,3,48]{2,1,0:T(4,128)(2,1)} %param.26) | copy-start | bytes 868
  7.2 59.5 %all-gather.11.cloned.1.call-start = ((), (), s32[]{:S(2)}) async-start(), calls=%async_computation.9 | async-start | bytes 1253376 | tf_op jit(solution)/shard_map/all_gather | solution.py:336
  8.0 95.8 %all-gather.9.cloned.1.call-start = ((), (), s32[]{:S(2)}) async-start(), calls=%async_computation.8 | async-start | bytes 2506752 | tf_op jit(solution)/shard_map/all_gather | solution.py:337
  9.6 138.9 %all-gather.13.cloned.1.call-start = ((), (), s32[]{:S(2)}) async-start(), calls=%async_computation.10 | async-start | bytes 1253376 | tf_op jit(solution)/shard_map/all_gather | solution.py:338
  10.4 182.7 %all-gather.17.cloned.1.call-start = ((), (), s32[]{:S(2)}) async-start(), calls=%async_computation.12 | async-start | bytes 1253376 | tf_op jit(solution)/shard_map/all_gather | solution.py:340
  10.9 229.7 %all-gather.15.cloned.1.call-start = ((), (), s32[]{:S(2)}) async-start(), calls=%async_computation.11 | async-start | bytes 2506752 | tf_op jit(solution)/shard_map/all_gather | solution.py:341
  12.6 272.6 %all-gather.19.cloned.1.call-start = ((), (), s32[]{:S(2)}) async-start(), calls=%async_computation.13 | async-start | bytes 1253376 | tf_op jit(solution)/shard_map/all_gather | solution.py:342
  13.2 335.8 %all-gather.21.cloned.1.call-start = ((), (), s32[]{:S(2)}) async-start(), calls=%async_computation.14 | async-start | bytes 6684672 | tf_op jit(solution)/shard_map/all_gather | solution.py:343
  15.1 383.4 %all-gather.23.cloned.1.call-start = ((), (), s32[]{:S(2)}) async-start(), calls=%async_computation.15 | async-start | bytes 3342336 | tf_op jit(solution)/shard_map/all_gather | solution.py:344
  15.9 703.2 %reduce-scatter.16.cloned.1.call-start = ((), (), s32[]{:S(2)}) async-start(), calls=%async_computation.20 | async-start | bytes 1253376 | tf_op jit(solution)/shard_map/reduce_scatter | solution.py:418
  16.1 90.3 %copy-start.131 = (pred[64,64]{0,1:T(8,128)(4,1)}, pred[64,64]{0,1:T(8,128)(4,1)S(1)}, u32[]{:S(2)}) copy-start(pred[64,64]{0,1:T(8,128)(4,1)S(1)} %fusion.610) | copy-start | bytes 12292
  16.2 228.6 %copy-start.127 = (pred[64,256]{1,0:T(8,128)(4,1)}, pred[64,256]{1,0:T(8,128)(4,1)S(1)}, u32[]{:S(2)}) copy-start(pred[64,256]{1,0:T(8,128)(4,1)S(1)} %broadcast_compare_fusion.2) | copy-start | bytes 49156
  57.0 49.3 %copy-start.13 = (f32[12,64,64]{1,2,0:T(8,128)}, f32[12,64,64]{1,2,0:T(8,128)S(1)}, u32[]{:S(2)}) copy-start(f32[12,64,64]{1,2,0:T(8,128)S(1)} %rev.18) | copy-start | bytes 589828
  57.7 48.3 %copy-start.178 = (f32[64]{0:T(128)}, f32[64]{0:T(128)S(1)}, u32[]{:S(2)}) copy-start(f32[64]{0:T(128)S(1)} %fusion.543) | copy-start | bytes 772
  58.3 47.6 %copy-start.155 = (f32[64]{0:T(128)}, f32[64]{0:T(128)S(1)}, u32[]{:S(2)}) copy-start(f32[64]{0:T(128)S(1)} %fusion.666) | copy-start | bytes 772
  68.6 38.1 %copy-start.48 = (bf16[64,768]{0,1:T(8,128)(2,1)}, bf16[64,768]{0,1:T(8,128)(2,1)S(1)}, u32[]{:S(2)}) copy-start(bf16[64,768]{0,1:T(8,128)(2,1)S(1)} %copy.379) | copy-start | bytes 294916
  106.4 43.9 %copy-start.47 = (bf16[64,12,64]{2,1,0:T(8,128)(2,1)}, bf16[64,12,64]{2,1,0:T(8,128)(2,1)S(1)}, u32[]{:S(2)}) copy-start(bf16[64,12,64]{2,1,0:T(8,128)(2,1)S(1)} %reshape_squeeze.48) | copy-start | bytes 294916
  106.7 41.8 %copy-start.37 = (f32[12,64,64]{1,2,0:T(8,128)}, f32[12,64,64]{1,2,0:T(8,128)S(1)}, u32[]{:S(2)}) copy-start(f32[12,64,64]{1,2,0:T(8,128)S(1)} %fusion.153) | copy-start | bytes 589828
  107.5 87.1 %copy-start.147 = (f32[12,64]{1,0:T(8,128)}, f32[12,64]{1,0:T(8,128)S(1)}, u32[]{:S(2)}) copy-start(f32[12,64]{1,0:T(8,128)S(1)} %get-tuple-element.147) | copy-start | bytes 9220
  107.5 133.1 %copy-start.33 = (bf16[2,1,256,768]{3,2,1,0:T(8,128)(2,1)S(1)}, bf16[2,1,256,768]{3,2,1,0:T(8,128)(2,1)}, u32[]{:S(2)}) copy-start(bf16[2,1,256,768]{3,2,1,0:T(8,128)(2,1)} %param.23) | copy-start | bytes 2359300
  107.8 135.2 %copy-start.120 = (bf16[12,64,64]{2,1,0:T(8,128)(2,1)}, bf16[12,64,64]{2,1,0:T(8,128)(2,1)S(1)}, u32[]{:S(2)}) copy-start(bf16[12,64,64]{2,1,0:T(8,128)(2,1)S(1)} %convolution_convert_fusion.28) | copy-start | bytes 294916
  150.3 135.0 %copy-start.16 = (f32[64,768]{1,0:T(8,128)}, f32[64,768]{1,0:T(8,128)S(1)}, u32[]{:S(2)}) copy-start(f32[64,768]{1,0:T(8,128)S(1)} %get-tuple-element.150) | copy-start | bytes 589828
  150.9 92.2 %copy-start.91 = (bf16[64,768]{1,0:T(8,128)(2,1)}, bf16[64,768]{1,0:T(8,128)(2,1)S(1)}, u32[]{:S(2)}) copy-start(bf16[64,768]{1,0:T(8,128)(2,1)S(1)} %multiply_convert_fusion.8) | copy-start | bytes 294916
  194.8 50.0 %copy-start.55 = (bf16[64,768]{0,1:T(8,128)(2,1)}, bf16[64,768]{0,1:T(8,128)(2,1)S(1)}, u32[]{:S(2)}) copy-start(bf16[64,768]{0,1:T(8,128)(2,1)S(1)} %copy.381) | copy-start | bytes 294916
  244.8 40.4 %copy-start.150 = (f32[12,64]{1,0:T(8,128)}, f32[12,64]{1,0:T(8,128)S(1)}, u32[]{:S(2)}) copy-start(f32[12,64]{1,0:T(8,128)S(1)} %get-tuple-element.151) | copy-start | bytes 9220
  245.6 41.4 %copy-start.122 = (bf16[12,64,64]{2,1,0:T(8,128)(2,1)}, bf16[12,64,64]{2,1,0:T(8,128)(2,1)S(1)}, u32[]{:S(2)}) copy-start(bf16[12,64,64]{2,1,0:T(8,128)(2,1)S(1)} %convolution_convert_fusion.27) | copy-start | bytes 294916
  287.0 111.5 %copy-start.17 = (f32[64,768]{1,0:T(8,128)}, f32[64,768]{1,0:T(8,128)S(1)}, u32[]{:S(2)}) copy-start(f32[64,768]{1,0:T(8,128)S(1)} %get-tuple-element.154) | copy-start | bytes 589828
  287.1 61.8 %copy-start.63 = (bf16[64,768]{1,0:T(8,128)(2,1)}, bf16[64,768]{1,0:T(8,128)(2,1)S(1)}, u32[]{:S(2)}) copy-start(bf16[64,768]{1,0:T(8,128)(2,1)S(1)} %multiply_convert_fusion.7) | copy-start | bytes 294916
  352.9 45.6 %copy-start.11 = (f32[2,64,2048]{2,1,0:T(8,128)}, f32[2,64,2048]{2,1,0:T(8,128)S(1)}, u32[]{:S(2)}) copy-start(f32[2,64,2048]{2,1,0:T(8,128)S(1)} %fusion.37) | copy-start | bytes 3145732
  401.8 9.3 copy-start.1
  401.8 12.0 copy-start
  401.8 6.3 collective-permute-start
  446.6 6.5 collective-permute-start.1
  531.6 5.6 collective-permute-start.2
  585.8 4.5 collective-permute-start.3
  617.3 147.0 %reduce-scatter.14.cloned.1.call-start = ((), (), s32[]{:S(2)}) async-start(), calls=%async_computation.19 | async-start | bytes 1253376 | tf_op jit(solution)/shard_map/reduce_scatter | solution.py:412
  624.9 215.3 %reduce-scatter.20.cloned.1.call-start = ((), (), s32[]{:S(2)}) async-start(), calls=%async_computation.22 | async-start | bytes 1253376 | tf_op jit(solution)/shard_map/reduce_scatter | solution.py:424
  627.8 288.5 %reduce-scatter.10.cloned.1.call-start = ((), (), s32[]{:S(2)}) async-start(), calls=%async_computation.17 | async-start | bytes 1253376 | tf_op jit(solution)/shard_map/reduce_scatter | solution.py:406
  650.2 343.7 %reduce-scatter.18.cloned.1.call-start = ((), (), s32[]{:S(2)}) async-start(), calls=%async_computation.21 | async-start | bytes 2506752 | tf_op jit(solution)/shard_map/reduce_scatter | solution.py:421
  659.2 8.6 copy-start.38
  687.5 383.9 %reduce-scatter.12.cloned.1.call-start = ((), (), s32[]{:S(2)}) async-start(), calls=%async_computation.18 | async-start | bytes 2506752 | tf_op jit(solution)/shard_map/reduce_scatter | solution.py:409
  690.8 458.8 %reduce-scatter.24.cloned.1.call-start = ((), (), s32[]{:S(2)}) async-start(), calls=%async_computation.24 | async-start | bytes 3342336 | tf_op jit(solution)/shard_map/reduce_scatter | solution.py:430
  694.9 539.2 %reduce-scatter.22.cloned.1.call-start = ((), (), s32[]{:S(2)}) async-start(), calls=%async_computation.23 | async-start | bytes 6684672 | tf_op jit(solution)/shard_map/reduce_scatter | solution.py:427
  700.1 606.1 %all-reduce.17.cloned.1.call-start = ((), (), s32[]{:S(2)}) async-start(), calls=%async_computation.16 | async-start | bytes 1572864 | tf_op jit(solution)/shard_map/psum | solution.py:400
  713.6 599.6 %all-reduce.19.cloned.1.call-start = ((), (), s32[]{:S(2)}) async-start(), calls=%async_computation.25 | async-start | bytes 2359296 | tf_op jit(solution)/shard_map/psum | solution.py:437
  717.6 516.6 %copy-start.75 = (f32[12,64,64]{1,2,0:T(8,128)S(1)}, f32[12,64,64]{1,2,0:T(8,128)}, u32[]{:S(2)}) copy-start(f32[12,64,64]{1,2,0:T(8,128)} %get-tuple-element.148) | copy-start | bytes 589828
  717.7 516.6 %copy-start.80 = (f32[12,64,64]{1,2,0:T(8,128)S(1)}, f32[12,64,64]{1,2,0:T(8,128)}, u32[]{:S(2)}) copy-start(f32[12,64,64]{1,2,0:T(8,128)} %fusion.582) | copy-start | bytes 589828
  717.7 516.6 %copy-start.148 = (f32[12,64]{1,0:T(8,128)S(1)}, f32[12,64]{1,0:T(8,128)}, u32[]{:S(2)}) copy-start(f32[12,64]{1,0:T(8,128)} %copy-done.147) | copy-start | bytes 9220
  718.8 515.6 %copy-start.139 = (f32[768]{0:T(1024)S(1)}, f32[768]{0:T(1024)}, u32[]{:S(2)}) copy-start(f32[768]{0:T(1024)} %get-tuple-element.77) | copy-start | bytes 9220
  718.8 515.6 %copy-start.142 = (f32[768]{0:T(1024)S(1)}, f32[768]{0:T(1024)}, u32[]{:S(2)}) copy-start(f32[768]{0:T(1024)} %get-tuple-element.75) | copy-start | bytes 9220
  1234.5 69.6 %copy-start.179 = (f32[64]{0:T(128)S(1)}, f32[64]{0:T(128)}, u32[]{:S(2)}) copy-start(f32[64]{0:T(128)} %copy-done.178) | copy-start | bytes 772
  1234.5 69.6 %copy-start.187 = (f32[64]{0:T(128)S(1)}, f32[64]{0:T(128)}, u32[]{:S(2)}) copy-start(f32[64]{0:T(128)} %get-tuple-element.74) | copy-start | bytes 772
  1234.5 69.6 %copy-start.24 = (bf16[2,1,64,768]{3,2,1,0:T(8,128)(2,1)S(1)}, bf16[2,1,64,768]{3,2,1,0:T(8,128)(2,1)}, u32[]{:S(2)}) copy-start(bf16[2,1,64,768]{3,2,1,0:T(8,128)(2,1)} %param.21) | copy-start | bytes 589828
  1234.5 69.6 %copy-start.52 = (f32[64,768]{1,0:T(8,128)S(1)}, f32[64,768]{1,0:T(8,128)}, u32[]{:S(2)}) copy-start(f32[64,768]{1,0:T(8,128)} %get-tuple-element.99) | copy-start | bytes 589828
  1234.5 69.6 %copy-start.156 = (f32[64]{0:T(128)S(1)}, f32[64]{0:T(128)}, u32[]{:S(2)}) copy-start(f32[64]{0:T(128)} %copy-done.155) | copy-start | bytes 772
  1234.7 69.5 %copy-start.88 = (bf16[64,768]{1,0:T(8,128)(2,1)S(1)}, bf16[64,768]{1,0:T(8,128)(2,1)}, u32[]{:S(2)}) copy-start(bf16[64,768]{1,0:T(8,128)(2,1)} %fusion.325) | copy-start | bytes 294916
  1234.7 69.5 %copy-start.170 = (pred[2]{0:T(512)(128)(4,1)S(1)}, pred[2]{0:T(512)(128)(4,1)}, u32[]{:S(2)}) copy-start(pred[2]{0:T(512)(128)(4,1)} %get-tuple-element.184) | copy-start | bytes 10
  1234.7 69.5 %copy-start.172 = (pred[2]{0:T(512)(128)(4,1)S(1)}, pred[2]{0:T(512)(128)(4,1)}, u32[]{:S(2)}) copy-start(pred[2]{0:T(512)(128)(4,1)} %get-tuple-element.185) | copy-start | bytes 10
  1234.8 69.5 %copy-start.176 = (pred[2]{0:T(512)(128)(4,1)S(1)}, pred[2]{0:T(512)(128)(4,1)}, u32[]{:S(2)}) copy-start(pred[2]{0:T(512)(128)(4,1)} %iota_compare_fusion.2) | copy-start | bytes 10
  1313.2 11.4 copy-start.86
  (159 other events, 454.1 us)
Sparse Core Ops, SparseCore 0:
  10.3 45.9 all-gather.10
  58.9 44.7 all-gather.8
  105.9 42.5 all-gather.12
  150.5 42.4 all-gather.16
  195.6 44.9 all-gather.14
  242.6 42.5 all-gather.18
  287.4 61.5 all-gather.20
  351.1 47.3 all-gather.22
  617.4 71.1 reduce-scatter.15
  691.7 72.5 reduce-scatter.13
  767.5 72.6 reduce-scatter.19
  843.8 72.4 reduce-scatter.9
  919.6 74.2 reduce-scatter.17
  997.1 74.2 reduce-scatter.11
  1074.6 75.0 reduce-scatter.23
  1152.9 81.2 reduce-scatter.21
  1237.0 25.5 all-reduce.16
  1265.6 47.6 all-reduce.18
where the time goes:
time: 1360 us; the launch traced here: 1330 us
  waiting for transfers between devices  829 us (61%)
  matrix products  229 us (17%)
  blocking collectives  106 us (8%)
  local copies, waits for them, and re-layouts  99 us (7%)
  other arithmetic  38.4 us (3%)
  between operations  18.7 us (1%)
    reduce_scatter x1, waiting for transfers between devices, shards(): lax.psum_scatter(full_grads[8][None].astype(jnp.bfloat16), 'fsdp', scatte...  84.6 us
    reduce_scatter x1, waiting for transfers between devices, shards(): lax.psum_scatter(full_grads[9][None].astype(jnp.bfloat16), 'fsdp', scatte...  78.2 us
    reduce_scatter x1, waiting for transfers between devices, shards(): lax.psum_scatter(full_grads[6][None].astype(jnp.bfloat16), 'fsdp', scatte...  77.6 us
    reduce_scatter x1, waiting for transfers between devices, shards(): lax.psum_scatter(full_grads[2][None].astype(jnp.bfloat16), 'fsdp', scatte...  77.5 us
    reduce_scatter x1, waiting for transfers between devices, shards(): lax.psum_scatter(full_grads[1][None].astype(jnp.bfloat16), 'fsdp', scatte...  76.2 us
    reduce_scatter x1, waiting for transfers between devices, shards(): lax.psum_scatter(full_grads[7][None].astype(jnp.bfloat16), 'fsdp', scatte...  75.9 us
    unnamed x1, blocking collectives  58 us
    all_gather x1, waiting for transfers between devices, shards(): lax.all_gather(ffn_in, 'fsdp', axis=1, tiled=True)  56.4 us
  transfers between devices with their start and end apart: 22, of which 17 were waited for; matrix products, arithmetic and copies ran while one was open for 11% of the time, Pallas kernels for 0%

commit v1 on v0

--- a/solution.py
+++ b/solution.py
@@ -8,16 +8,12 @@
 HEAD = 64
 BUCKETS = 32
 MAX_DIST = 128
+PARTS = 16
+EXTRA = 128
 
 
 epsilon = 1e-06
 highest = lax.Precision.HIGHEST
-
-
-def shifted_2(value, axis, steps):
-    count = lax.axis_size(axis)
-    first, last = (max(0, -steps), min(count, count - steps))
-    return lax.ppermute(value, axis, [(source, source + steps) for source in range(first, last)])
 
 
 def bucket_row(length):
@@ -310,6 +306,72 @@
     )
 
 
+def pack(gains, query, kv, out, table, c_query, c_kv, c_out, w_in, w_ffn):
+    rows = query.shape[0]
+    extra = jnp.zeros((rows, EXTRA), query.dtype)
+    extra = extra.at[:, :3].set(gains.T)
+    extra = extra.at[: BUCKETS // PARTS, 16 : 16 + HEADS].set(table)
+    return jnp.concatenate(
+        [
+            query,
+            kv.reshape(rows, -1),
+            out,
+            c_query,
+            c_kv.reshape(rows, -1),
+            c_out,
+            w_in.reshape(rows, -1),
+            w_ffn.reshape(rows, -1),
+            extra,
+        ],
+        axis=1,
+    )
+
+
+def unpack(block, parts):
+    rows = block.shape[0]
+    start = 0
+    pieces = []
+    for width in (768, 1536, 768, 768, 1536, 768, 4096, 2048, EXTRA):
+        pieces.append(block[:, start : start + width])
+        start += width
+    query, kv, out, c_query, c_kv, c_out, w_in, w_ffn, extra = pieces
+    gains = extra[:, :3].T
+    table = extra.reshape(parts, rows // parts, EXTRA)[:, : BUCKETS // PARTS, 16 : 16 + HEADS]
+    return (
+        gains,
+        query,
+        kv.reshape(rows, 2, 768),
+        out,
+        table.reshape(-1, HEADS),
+        c_query,
+        c_kv.reshape(rows, 2, 768),
+        c_out,
+        w_in.reshape(rows, 2, 2048),
+        w_ffn.reshape(-1, 768),
+    )
+
+
+def pack_full(gains, query, kv, out, table, c_query, c_kv, c_out, w_in, w_ffn):
+    rows = query.shape[0]
+    extra = jnp.zeros((PARTS, rows // PARTS, EXTRA), jnp.bfloat16)
+    extra = extra.at[:, :, :3].set(gains.T.reshape(PARTS, rows // PARTS, 3).astype(jnp.bfloat16))
+    extra = extra.at[:, : BUCKETS // PARTS, 16 : 16 + HEADS].set(
+        table.reshape(PARTS, BUCKETS // PARTS, HEADS).astype(jnp.bfloat16)
+    )
+    members = [
+        query,
+        kv.reshape(rows, -1),
+        out,
+        c_query,
+        c_kv.reshape(rows, -1),
+        c_out,
+        w_in.reshape(rows, -1),
+        w_ffn.reshape(rows, -1),
+        extra.reshape(rows, EXTRA),
+    ]
+    return jnp.concatenate([member.astype(jnp.bfloat16) for member in members], axis=1)
+
+
 def shards(
     layer_in,
     cotangent,
@@ -329,135 +391,48 @@
 ):
     section_index = lax.axis_index("section")
     batches = layer_in.shape[0]
-    length = layer_in.shape[2]
-    width = layer_in.shape[3]
-    gathered = (
-        lax.all_gather(norm_gains, "fsdp", axis=2, tiled=True),
-        lax.all_gather(self_query, "fsdp", axis=1, tiled=True),
-        lax.all_gather(self_kv, "fsdp", axis=1, tiled=True),
-        lax.all_gather(self_out, "fsdp", axis=1, tiled=True),
-        lax.all_gather(rel_bias, "fsdp", axis=1, tiled=True),
-        lax.all_gather(cross_query, "fsdp", axis=1, tiled=True),
-        lax.all_gather(cross_kv, "fsdp", axis=1, tiled=True),
-        lax.all_gather(cross_out, "fsdp", axis=1, tiled=True),
-        lax.all_gather(ffn_in, "fsdp", axis=1, tiled=True),
-        lax.all_gather(ffn_out, "fsdp", axis=1, tiled=True),
-    )
-    weights = tuple((member[0] for member in gathered))
-    slot_ids = jnp.arange(batches)
-    received = jnp.zeros((length, width), jnp.bfloat16)
-    outputs = jnp.zeros((batches, length, width), jnp.bfloat16)
-    saved_list = []
-    for moment in range(batches + 1):
-        micro_batch = moment - section_index
-        picked = jnp.clip(micro_batch, 0, batches - 1)
-        current = jnp.where(section_index == 0, layer_in[min(moment, batches - 1), 0], received)
-        encoder_rows = lax.dynamic_index_in_dim(encoder[:, 0], picked, 0, keepdims=False)
-        dec_ids = lax.dynamic_index_in_dim(dec_segments[:, 0], picked, 0, keepdims=False)
-        enc_ids = lax.dynamic_index_in_dim(enc_segments[:, 0], picked, 0, keepdims=False)
-        result, saved = layer_forward(
-            current.astype(jnp.float32), encoder_rows, dec_ids, enc_ids, weights
-        )
-        sent_rows = result.astype(jnp.bfloat16)
-        outputs = jnp.where((slot_ids == micro_batch)[:, None, None], sent_rows[None], outputs)
-        saved_list.append(saved)
-        if moment < batches:
-            received = shifted_2(sent_rows, "section", 1)
-    regathered = (
-        lax.all_gather(norm_gains, "fsdp", axis=2, tiled=True),
-        lax.all_gather(self_query, "fsdp", axis=1, tiled=True),
-        lax.all_gather(self_kv, "fsdp", axis=1, tiled=True),
-        lax.all_gather(self_out, "fsdp", axis=1, tiled=True),
-        lax.all_gather(rel_bias, "fsdp", axis=1, tiled=True),
-        lax.all_gather(cross_query, "fsdp", axis=1, tiled=True),
-        lax.all_gather(cross_kv, "fsdp", axis=1, tiled=True),
-        lax.all_gather(cross_out, "fsdp", axis=1, tiled=True),
-        lax.all_gather(ffn_in, "fsdp", axis=1, tiled=True),
-        lax.all_gather(ffn_out, "fsdp", axis=1, tiled=True),
-    )
-    back_weights = tuple((member[0] for member in regathered))
-    returned = jnp.zeros((length, width), jnp.bfloat16)
-    input_grads = jnp.zeros((batches, length, width), jnp.bfloat16)
-    encoder_sum = jnp.zeros((batches, encoder.shape[2], width), jnp.float32)
-    records = []
-    owned = None
-    for moment in range(batches + 1):
-        micro_batch = batches - moment - section_index
-        given = cotangent[max(batches - 1 - moment, 0), 0]
-        incoming = jnp.where(section_index == 1, given, returned).astype(jnp.float32)
-        live = (micro_batch >= 0) & (micro_batch < batches)
-        incoming = jnp.where(live, incoming, 0.0)
-        grad_input, grad_encoder, rows_for_weights = layer_backward(
-            incoming, saved_list[batches - moment], back_weights
-        )
-        grad_low = grad_input.astype(jnp.bfloat16)
-        hit_slot = (slot_ids == micro_batch)[:, None, None]
-        input_grads = jnp.where(hit_slot, grad_low[None], input_grads)
-        encoder_sum = encoder_sum + jnp.where(hit_slot, grad_encoder[None], 0.0)
-        records.append(rows_for_weights)
-        if moment < batches:
-            returned = shifted_2(grad_low, "section", -1)
-    encoder_total = lax.psum(encoder_sum.astype(jnp.bfloat16), "section").astype(jnp.float32)
-    full_grads = weight_grads(records)
-    owned = (
-        lax.psum_scatter(
-            full_grads[0][None].astype(jnp.bfloat16), "fsdp", scatter_dimension=2, tiled=True
-        ).astype(jnp.float32),
-        lax.psum_scatter(
-            full_grads[1][None].astype(jnp.bfloat16), "fsdp", scatter_dimension=1, tiled=True
-        ).astype(jnp.float32),
-        lax.psum_scatter(
-            full_grads[2][None].astype(jnp.bfloat16), "fsdp", scatter_dimension=1, tiled=True
-        ).astype(jnp.float32),
-        lax.psum_scatter(
-            full_grads[3][None].astype(jnp.bfloat16), "fsdp", scatter_dimension=1, tiled=True
-        ).astype(jnp.float32),
-        lax.psum_scatter(
-            full_grads[4][None].astype(jnp.bfloat16), "fsdp", scatter_dimension=1, tiled=True
-        ).astype(jnp.float32),
-        lax.psum_scatter(
-            full_grads[5][None].astype(jnp.bfloat16), "fsdp", scatter_dimension=1, tiled=True
-        ).astype(jnp.float32),
-        lax.psum_scatter(
-            full_grads[6][None].astype(jnp.bfloat16), "fsdp", scatter_dimension=1, tiled=True
-        ).astype(jnp.float32),
-        lax.psum_scatter(
-            full_grads[7][None].astype(jnp.bfloat16), "fsdp", scatter_dimension=1, tiled=True
-        ).astype(jnp.float32),
-        lax.psum_scatter(
-            full_grads[8][None].astype(jnp.bfloat16), "fsdp", scatter_dimension=1, tiled=True
-        ).astype(jnp.float32),
-        lax.psum_scatter(
-            full_grads[9][None].astype(jnp.bfloat16), "fsdp", scatter_dimension=1, tiled=True
-        ).astype(jnp.float32),
-    )
-    summed = (
-        lax.psum(owned[0].astype(jnp.bfloat16), "rep").astype(jnp.float32),
-        lax.psum(owned[1].astype(jnp.bfloat16), "rep").astype(jnp.float32),
-        lax.psum(owned[2].astype(jnp.bfloat16), "rep").astype(jnp.float32),
-        lax.psum(owned[3].astype(jnp.bfloat16), "rep").astype(jnp.float32),
-        lax.psum(owned[4].astype(jnp.bfloat16), "rep").astype(jnp.float32),
-        lax.psum(owned[5].astype(jnp.bfloat16), "rep").astype(jnp.float32),
-        lax.psum(owned[6].astype(jnp.bfloat16), "rep").astype(jnp.float32),
-        lax.psum(owned[7].astype(jnp.bfloat16), "rep").astype(jnp.float32),
-        lax.psum(owned[8].astype(jnp.bfloat16), "rep").astype(jnp.float32),
-        lax.psum(owned[9].astype(jnp.bfloat16), "rep").astype(jnp.float32),
-    )
+    own = pack(
+        norm_gains[0],
+        self_query[0],
+        self_kv[0],
+        self_out[0],
+        rel_bias[0],
+        cross_query[0],
+        cross_kv[0],
+        cross_out[0],
+        ffn_in[0],
+        ffn_out[0],
+    )
+    weights = unpack(lax.all_gather(own, "fsdp", axis=0, tiled=True), PARTS)
+    rows_in = layer_in[:, 0]
+    states = encoder[:, 0]
+    dec_ids = dec_segments[:, 0]
+    enc_ids = enc_segments[:, 0]
+    forward = jax.vmap(layer_forward, in_axes=(0, 0, 0, 0, None))
+    backward = jax.vmap(layer_backward, in_axes=(0, 0, None))
+    first, _ = forward(rows_in.astype(jnp.float32), states, dec_ids, enc_ids, weights)
+    received = lax.ppermute(first.astype(jnp.bfloat16), "section", [(0, 1)])
+    current = jnp.where(section_index == 0, rows_in, received)
+    result, saved = forward(current.astype(jnp.float32), states, dec_ids, enc_ids, weights)
+    outputs = result.astype(jnp.bfloat16)
+    given = cotangent[:, 0]
+    grad_first, _, _ = backward(given.astype(jnp.float32), saved, weights)
+    returned = lax.ppermute(grad_first.astype(jnp.bfloat16), "section", [(1, 0)])
+    incoming = jnp.where(section_index == 1, given, returned)
+    grad_input, grad_encoder, records = backward(incoming.astype(jnp.float32), saved, weights)
+    input_grads = grad_input.astype(jnp.bfloat16)
+    encoder_total = lax.psum(grad_encoder.astype(jnp.bfloat16), "section").astype(jnp.float32)
+    full_grads = weight_grads(
+        [jax.tree.map(lambda member: member[slot], records) for slot in range(batches)]
+    )
+    owned = lax.psum_scatter(pack_full(*full_grads), "fsdp", scatter_dimension=0, tiled=True)
+    summed = lax.psum(owned, "rep").astype(jnp.float32)
+    grads = unpack(summed, 1)
     return (
         outputs[None, :, None],
         input_grads[None, :, None],
         encoder_total[:, None],
-        summed[0],
-        summed[1],
-        summed[2],
-        summed[3],
-        summed[4],
-        summed[5],
-        summed[6],
-        summed[7],
-        summed[8],
-        summed[9],
-    )
+    ) + tuple(member[None] for member in grads)
 
 
 def solution(mesh):

time: 1360 us -> 840 us (0.62); the launches traced: 1330 us -> 829 us
  waiting for transfers between devices: 829 us -> 458 us
  blocking collectives: 106 us -> 0 us
  local copies, waits for them, and re-layouts: 99 us -> 152 us
  matrix products: 229 us -> 179 us
  other arithmetic: 38.4 us -> 19.9 us
    reduce_scatter x8 -> x0, waiting for transfers between devices: 515 us -> none  [the longest x1 84.6 us: shards(): lax.psum_scatter(full_grads[8][None].astype(jnp.bfloat16), 'fsdp', scatte...]
    unnamed x18 -> x5, waiting for transfers between devices: 3.32 us -> 237 us
    all_gather x8 -> x1, waiting for transfers between devices: 305 us -> 125 us  [shards(): weights = unpack(lax.all_gather(own, 'fsdp', axis=0, tiled=True), PARTS)]
    psum x2, waiting for transfers between devices: 4.61 us -> 94.1 us  [the longest x1 77.1 us: shards(): summed = lax.psum(owned, 'rep').astype(jnp.float32)]
    unnamed x1 -> x0, blocking collectives: 58 us -> none
    all_gather x2 -> x0, blocking collectives: 39.3 us -> none  [the longest x1 20.8 us: shards(): lax.all_gather(rel_bias, 'fsdp', axis=1, tiled=True)]
    convert_element_type x1 -> x5, local copies, waits for them, and re-layouts: 0.11 us -> 20.4 us  [the longest x3 20.1 us: pack_full(): member.astype(jnp.bfloat16)]
    slice x3 -> x18, local copies, waits for them, and re-layouts: 4.02 us -> 23.7 us  [the longest x11 21.1 us: unpack(): pieces.append(block[:, start:start + width])]
  transfers between devices with their start and end apart: 22 -> 6, of which waited for: 17 -> 5; matrix products, arithmetic and copies ran while one was open for 11% -> 2% of each run, Pallas kernels for 0% -> 0%
where the time goes in v1:
time: 840 us; the launch traced here: 829 us
  waiting for transfers between devices  458 us (55%)
  matrix products  179 us (21%)
  local copies, waits for them, and re-layouts  152 us (18%)
  other arithmetic  19.9 us (2%)
  between operations  16.8 us (2%)
    unnamed x5, waiting for transfers between devices  237 us
    all_gather x1, waiting for transfers between devices, shards(): weights = unpack(lax.all_gather(own, 'fsdp', axis=0, tiled=True), PARTS)  125 us
    psum x1, waiting for transfers between devices, shards(): summed = lax.psum(owned, 'rep').astype(jnp.float32)  77.1 us
    unnamed x356, local copies, waits for them, and re-layouts  45.7 us
    dot_general x4, matrix products, attend_backward(): jnp.einsum('hqk,khe->qhe', grad_scores, split_heads(key_rows), preferred_...  28.4 us
    slice x11, local copies, waits for them, and re-layouts, unpack(): pieces.append(block[:, start:start + width])  21.1 us
    convert_element_type x3, local copies, waits for them, and re-layouts, pack_full(): member.astype(jnp.bfloat16)  20.1 us
    dot_general x4, matrix products, attend_backward(): jnp.einsum('qhe,khe->hqk', grad_heads, split_heads(value_rows), preferred...  19.2 us
  transfers between devices with their start and end apart: 6, of which 5 were waited for; matrix products, arithmetic and copies ran while one was open for 2% of the time, Pallas kernels for 0%

profile of v1, /device:TPU:1, one launch (start us, length us, event | category | flops | bytes accessed | tf_op | source)
XLA Modules:
  0.0 829.4 jit_solution(17336855491350386983)
XLA Ops:
  14.3 1.9 broadcast_select_fusion.1
  20.1 125.4 %all-gather.2.cloned.1.call-done = bf16[768,12416]{1,0:T(8,128)(2,1)} async-done(((bf16[48,12416]{1,0:T(8,128)(2,1)}), bf16[768,12416]{1,0:T(8,128)(2,1)}) %all-gather.2.cloned.1.call-update) | async-done | bytes 19070992 | tf_op jit(solution)/shard_map/all_gather | solution.py:406
  145.5 4.9 fusion.305
  150.3 2.8 copy.334
  163.9 2.2 reshape.493
  166.1 3.3 fusion.47
  170.4 2.0 convolution_convert_fusion.20
  179.0 1.9 slice-done.11
  180.9 4.4 reshape.518
  185.2 6.3 slice.426
  191.6 11.5 %reshape.495 = bf16[768,2,2048]{2,1,0:T(2,128)(2,1)} reshape(bf16[768,4096]{1,0:T(8,128)(2,1)} %slice.426) | data formatting | bytes 12582912 | tf_op jit(solution)/shard_map/reshape | solution.py:349
  203.1 4.8 convolution_convert_fusion.11
  209.6 5.2 fusion.16
  234.2 2.0 convolution_convert_fusion.9
  236.2 1.9 multiply_reduce_fusion.10
  238.4 6.2 fusion.19
  244.6 2.4 fusion.161
  247.1 3.7 multiply_reduce_fusion.9
  252.8 2.1 reshape.500
  254.9 14.9 %fusion.187 = f32[2,12,64,256]{3,2,1,0:T(8,128)} fusion(bf16[2,256,12,64]{1,3,2,0:T(8,128)(2,1)S(1)} %bitcast.510, bf16[2,64,12,64]{3,2,1,0:T(8,128)(2,1)} %reshape.500), kind=kOutput, calls=%fused_computation.260 | convolution fusion | flops 50331648 | bytes 2555904 | tf_op jit(solution)/shard_map/vmap(qhe,khe->hqk)/dot_general | solution.py:91
  269.8 11.2 %fusion.79 = bf16[2,12,64,64]{3,2,1,0:T(8,128)(2,1)S(1)} fusion(bf16[2,256,12,64]{1,3,2,0:T(8,128)(2,1)S(1)} %bitcast.505, f32[2,12,64,256]{3,2,1,0:T(8,128)} %fusion.187, pred[2,64,256]{2,1,0:T(8,128)(4,1)S(1)} %copy-done.95, f32[2,12,64,256]{3,2,1,0:T(8,128)} %get-tuple-element.205, f32[2,12,64]{2,1,0:T(8,128)S(1)} %copy-done.119), kind=kOutput, calls=%fused_computation.83 | convolution fusion | flops 53184256 | bytes 4167680 | tf_op jit(solution)/shard_map/vmap(hqk,khe->qhe)/dot_general | solution.py:104
  281.0 1.9 multiply_reduce_fusion.8
  284.5 1.8 convolution_convert_fusion.23
  286.6 2.6 convolution_convert_fusion.16
  290.3 2.7 convolution_convert_fusion.17
  293.0 3.2 convolution_convert_fusion.18
  299.7 1.8 copy.367
  301.5 2.4 convolution_bitcast_fusion.2
  303.9 2.1 fusion.179
  306.8 2.2 collective-permute-start.1
  312.2 3.2 fusion.162
  315.4 7.4 multiply_reduce_fusion.4
  325.5 2.0 copy.474
  327.5 2.9 fusion.324
  330.4 11.0 %fusion.76 = bf16[2,12,64,64]{3,2,1,0:T(8,128)(2,1)} fusion(bf16[2,256,12,64]{1,3,2,0:T(8,128)(2,1)S(1)} %bitcast.506, f32[2,12,64,256]{3,2,1,0:T(8,128)} %fusion.324, pred[2,64,256]{2,1,0:T(8,128)(4,1)} %copy-done.93, f32[2,12,64,256]{3,2,1,0:T(8,128)S(1)} %copy-done.29, f32[2,12,64]{2,1,0:T(8,128)} %copy-done.118), kind=kOutput, calls=%fused_computation.82 | convolution fusion | flops 53184256 | bytes 4167680 | tf_op jit(solution)/shard_map/vmap(hqk,khe->qhe)/dot_general | solution.py:104
  341.4 2.6 multiply_reduce_fusion.5
  347.8 2.5 convolution_convert_fusion.13
  351.5 3.3 convolution_convert_fusion.14
  354.8 3.1 convolution_convert_fusion.15
  359.3 12.2 %fusion.60 = bf16[2,12,64,256]{3,2,1,0:T(8,128)(2,1)} fusion(bf16[2,64,12,64]{1,3,2,0:T(8,128)(2,1)S(1)} %bitcast.538, f32[2,12,64,256]{3,2,1,0:T(8,128)} %fusion.324, pred[2,64,256]{2,1,0:T(8,128)(4,1)} %copy-done.93, f32[2,12,64,256]{3,2,1,0:T(8,128)} %get-tuple-element.205, f32[2,12,64]{2,1,0:T(8,128)} %copy-done.118), kind=kOutput, calls=%fused_computation.65 | convolution fusion | flops 53479168 | bytes 4167680 | tf_op jit(solution)/shard_map/vmap(hqk,qhe->khe)/dot_general | solution.py:107
  380.2 2.6 copy.387
  386.8 4.4 convolution_convert_fusion
  391.2 8.7 %copy.394 = bf16[768,2,2048]{0,2,1:T(8,128)(2,1)} copy(bf16[768,2,2048]{2,0,1:T(8,128)(2,1)} %convolution_convert_fusion) | data formatting | bytes 12582912 | tf_op jit(solution)/shard_map/convert_element_type | solution.py:372
  399.9 2.7 convolution_convert_fusion.1
  402.6 6.6 convert_element_type.497
  409.2 4.7 copy.399
  414.0 2.6 fusion.166
  418.1 1.9 reshape.505
  420.4 1.9 broadcast_select_fusion
  422.3 6.2 scatter.19
  428.6 2.6 fusion.44
  442.4 3.1 constant_dynamic-update-slice_fusion.7
  445.6 2.0 constant_dynamic-update-slice_fusion.6
  450.2 3.7 fusion.63
  453.9 237.1 %all-reduce.16.cloned.1.call-done = bf16[768,12416]{0,1:T(8,128)(2,1)} async-done(((bf16[768,12416]{0,1:T(8,128)(2,1)}), bf16[768,12416]{0,1:T(8,128)(2,1)}) %all-reduce.16.cloned.1.call-update) | async-done | bytes 19070992
  691.0 4.6 constant_dynamic-slice_fusion
  697.2 3.4 fusion.96
  701.5 17.0 %all-reduce.12.cloned.1.call-done = bf16[2,1,256,768]{3,2,0,1:T(8,128)(2,1)} async-done(((bf16[2,1,256,768]{3,2,0,1:T(8,128)(2,1)}), bf16[2,1,256,768]{3,2,0,1:T(8,128)(2,1)}) %all-reduce.12.cloned.1.call-update) | async-done | bytes 786448 | tf_op jit(solution)/shard_map/psum | solution.py:424
  718.5 2.4 bitcast_convert_fusion.1
  720.9 77.1 %all-reduce.14.cloned.1.call-done = bf16[48,12416]{0,1:T(8,128)(2,1)} async-done(((bf16[48,12416]{0,1:T(8,128)(2,1)}), bf16[48,12416]{0,1:T(8,128)(2,1)}) %all-reduce.14.cloned.1.call-update) | async-done | bytes 1191952 | tf_op jit(solution)/shard_map/psum | solution.py:429
  798.0 2.1 convert_element_type.505
  804.9 2.1 copy.407
  811.3 2.1 copy.411
  816.6 2.6 copy.413
  (502 shorter events, 116.9 us)
Async XLA Ops:
  7.2 5.0 copy-start.146
  7.2 4.9 copy-start.142
  7.2 6.2 copy-start.97
  7.2 6.2 copy-start.98
  7.2 6.3 copy-start.99
  7.2 138.2 %all-gather.2.cloned.1.call-start = ((), (), s32[]{:S(2)}) async-start(), calls=%async_computation | async-start | bytes 20262912 | tf_op jit(solution)/shard_map/all_gather | solution.py:406
  13.4 5.6 copy-start.141
  13.4 5.6 copy-start.143
  13.5 6.3 copy-start.25
  13.5 6.4 copy-start.135
  18.9 672.1 %all-reduce.16.cloned.1.call-start = ((), (), s32[]{:S(2)}) async-start(), calls=%async_computation.3 | async-start | bytes 38141952
  20.1 157.4 %copy-start.93 = (pred[2,64,256]{2,1,0:T(8,128)(4,1)}, pred[2,64,256]{2,1,0:T(8,128)(4,1)S(1)}, u32[]{:S(2)}) copy-start(pred[2,64,256]{2,1,0:T(8,128)(4,1)S(1)} %broadcast_compare_fusion) | copy-start | bytes 98308
  155.0 19.2 %copy-start.108 = (f32[768]{0:T(1024)}, f32[768]{0:T(1024)S(1)}, u32[]{:S(2)}) copy-start(f32[768]{0:T(1024)S(1)} %get-tuple-element.133) | copy-start | bytes 9220
  155.0 54.6 %copy-start.104 = (f32[768]{0:T(1024)}, f32[768]{0:T(1024)S(1)}, u32[]{:S(2)}) copy-start(f32[768]{0:T(1024)S(1)} %get-tuple-element.132) | copy-start | bytes 9220
  161.2 4.8 copy-start.13
  170.4 7.1 copy-start.7
  191.6 11.5 %copy-start.10 = (bf16[2,1,256,768]{2,3,0,1:T(8,128)(2,1)S(1)}, bf16[2,1,256,768]{2,3,0,1:T(8,128)(2,1)}, u32[]{:S(2)}) copy-start(bf16[2,1,256,768]{2,3,0,1:T(8,128)(2,1)} %get-tuple-element.161) | copy-start | bytes 2359300
  203.1 4.8 copy-start.43
  209.6 5.2 copy-start.17
  215.7 3.5 collective-permute-start
  220.7 68.4 %copy-start.15 = (bf16[2,64,12,64]{3,2,1,0:T(8,128)(2,1)}, bf16[2,64,12,64]{3,2,1,0:T(8,128)(2,1)S(1)}, u32[]{:S(2)}) copy-start(bf16[2,64,12,64]{3,2,1,0:T(8,128)(2,1)S(1)} %squeeze.175) | copy-start | bytes 589828
  234.2 17.4 %slice-start = ((s8[19070976]{0:T(1024)(128)(4,1)}), s8[4194304]{0:T(1024)(128)(4,1)S(1)}, s32[]{:S(2)}) async-start(s8[19070976]{0:T(1024)(128)(4,1)} %bitcast.487), calls=%async_computation.4 | async-start | bytes 8388608
  236.2 8.4 %copy-start.23 = (bf16[2,1,64,768]{3,2,1,0:T(8,128)(2,1)S(1)}, bf16[2,1,64,768]{3,2,1,0:T(8,128)(2,1)}, u32[]{:S(2)}) copy-start(bf16[2,1,64,768]{3,2,1,0:T(8,128)(2,1)} %param.27) | copy-start | bytes 589828
  236.2 10.8 %slice-start.14 = ((s8[6291456]{0:T(1024)(128)(4,1)}), s8[4194304]{0:T(1024)(128)(4,1)S(1)}, s32[]{:S(2)}) async-start(s8[6291456]{0:T(1024)(128)(4,1)} %bitcast.514), calls=%async_computation.18 | async-start | bytes 8388608
  236.2 15.3 %slice-start.1 = ((s8[19070976]{0:T(1024)(128)(4,1)}), s8[4194304]{0:T(1024)(128)(4,1)S(1)}, s32[]{:S(2)}) async-start(s8[19070976]{0:T(1024)(128)(4,1)} %bitcast.487), calls=%async_computation.5 | async-start | bytes 8388608
  238.2 84.6 %copy-start.112 = (f32[2,64]{1,0:T(2,128)}, f32[2,64]{1,0:T(2,128)S(1)}, u32[]{:S(2)}) copy-start(f32[2,64]{1,0:T(2,128)S(1)} %fusion.276) | copy-start | bytes 1540
  238.2 6.4 copy-start.18
  238.3 6.3 copy-start.62
  238.3 8.7 %slice-start.15 = ((s8[6291456]{0:T(1024)(128)(4,1)}), s8[2097152]{0:T(1024)(128)(4,1)S(1)}, s32[]{:S(2)}) async-start(s8[6291456]{0:T(1024)(128)(4,1)} %bitcast.514), calls=%async_computation.19 | async-start | bytes 4194304
  238.3 13.2 %slice-start.2 = ((s8[19070976]{0:T(1024)(128)(4,1)}), s8[4194304]{0:T(1024)(128)(4,1)S(1)}, s32[]{:S(2)}) async-start(s8[19070976]{0:T(1024)(128)(4,1)} %bitcast.487), calls=%async_computation.6 | async-start | bytes 8388608
  244.6 6.9 slice-start.3
  252.8 17.0 %copy-start.95 = (pred[2,64,256]{2,1,0:T(8,128)(4,1)S(1)}, pred[2,64,256]{2,1,0:T(8,128)(4,1)}, u32[]{:S(2)}) copy-start(pred[2,64,256]{2,1,0:T(8,128)(4,1)} %copy-done.93) | copy-start | bytes 98308
  252.8 17.0 %copy-start.119 = (f32[2,12,64]{2,1,0:T(8,128)S(1)}, f32[2,12,64]{2,1,0:T(8,128)}, u32[]{:S(2)}) copy-start(f32[2,12,64]{2,1,0:T(8,128)} %copy-done.118) | copy-start | bytes 18436
  269.8 11.2 %copy-start.110 = (f32[768]{0:T(1024)S(1)}, f32[768]{0:T(1024)}, u32[]{:S(2)}) copy-start(f32[768]{0:T(1024)} %copy-done.108) | copy-start | bytes 9220
  293.0 11.0 %copy-start.102 = (f32[768]{0:T(1024)S(1)}, f32[768]{0:T(1024)}, u32[]{:S(2)}) copy-start(f32[768]{0:T(1024)} %copy-done.100) | copy-start | bytes 9220
  293.0 31.3 %slice-start.5 = ((s8[19070976]{0:T(1024)(128)(4,1)}), s8[2293760]{0:T(1024)(128)(4,1)S(1)}, s32[]{:S(2)}) async-start(s8[19070976]{0:T(1024)(128)(4,1)} %bitcast.489), calls=%async_computation.9 | async-start | bytes 4587520
  301.5 22.8 %slice-start.6 = ((s8[19070976]{0:T(1024)(128)(4,1)}), s8[4194304]{0:T(1024)(128)(4,1)S(1)}, s32[]{:S(2)}) async-start(s8[19070976]{0:T(1024)(128)(4,1)} %bitcast.489), calls=%async_computation.10 | async-start | bytes 8388608
  303.9 5.1 copy-start.36
  306.8 5.4 copy-start.24
  306.8 5.3 collective-permute-start.1
  310.6 13.7 %slice-start.7 = ((s8[19070976]{0:T(1024)(128)(4,1)}), s8[4194304]{0:T(1024)(128)(4,1)S(1)}, s32[]{:S(2)}) async-start(s8[19070976]{0:T(1024)(128)(4,1)} %bitcast.489), calls=%async_computation.11 | async-start | bytes 8388608
  312.2 12.1 %slice-start.8 = ((s8[19070976]{0:T(1024)(128)(4,1)}), s8[4194304]{0:T(1024)(128)(4,1)S(1)}, s32[]{:S(2)}) async-start(s8[19070976]{0:T(1024)(128)(4,1)} %bitcast.489), calls=%async_computation.12 | async-start | bytes 8388608
  315.4 7.4 copy-start.69
  315.4 7.4 copy-start.71
  315.4 7.4 copy-start.139
  315.4 8.8 %slice-start.9 = ((s8[19070976]{0:T(1024)(128)(4,1)}), s8[4194304]{0:T(1024)(128)(4,1)S(1)}, s32[]{:S(2)}) async-start(s8[19070976]{0:T(1024)(128)(4,1)} %bitcast.489), calls=%async_computation.13 | async-start | bytes 8388608
  325.5 4.9 copy-start.9
  325.5 4.9 copy-start.29
  359.3 14.9 %copy-start.2 = (bf16[768,1536]{0,1:T(8,128)(2,1)S(1)}, bf16[768,1536]{0,1:T(8,128)(2,1)}, u32[]{:S(2)}) copy-start(bf16[768,1536]{0,1:T(8,128)(2,1)} %copy-done) | copy-start | bytes 7077892
  391.2 8.7 %copy-start.45 = (bf16[64,2048]{1,0:T(8,128)(2,1)S(1)}, bf16[64,2048]{1,0:T(8,128)(2,1)}, u32[]{:S(2)}) copy-start(bf16[64,2048]{1,0:T(8,128)(2,1)} %get-tuple-element.166) | copy-start | bytes 786436
  391.2 8.7 %copy-start.46 = (bf16[64,2048]{1,0:T(8,128)(2,1)S(1)}, bf16[64,2048]{1,0:T(8,128)(2,1)}, u32[]{:S(2)}) copy-start(bf16[64,2048]{1,0:T(8,128)(2,1)} %get-tuple-element.167) | copy-start | bytes 786436
  391.2 8.7 %copy-start.91 = (bf16[64,768]{1,0:T(8,128)(2,1)S(1)}, bf16[64,768]{1,0:T(8,128)(2,1)}, u32[]{:S(2)}) copy-start(bf16[64,768]{1,0:T(8,128)(2,1)} %get-tuple-element.182) | copy-start | bytes 294916
  391.2 8.7 %copy-start.92 = (bf16[64,768]{1,0:T(8,128)(2,1)S(1)}, bf16[64,768]{1,0:T(8,128)(2,1)}, u32[]{:S(2)}) copy-start(bf16[64,768]{1,0:T(8,128)(2,1)} %get-tuple-element.183) | copy-start | bytes 294916
  409.2 4.8 copy-start.79
  409.2 4.8 copy-start.103
  409.2 4.8 copy-start.123
  418.0 10.6 %copy-start.75 = (bf16[64,768]{1,0:T(8,128)(2,1)S(1)}, bf16[64,768]{1,0:T(8,128)(2,1)}, u32[]{:S(2)}) copy-start(bf16[64,768]{1,0:T(8,128)(2,1)} %get-tuple-element.192) | copy-start | bytes 294916
  418.0 10.6 %copy-start.76 = (bf16[64,768]{1,0:T(8,128)(2,1)S(1)}, bf16[64,768]{1,0:T(8,128)(2,1)}, u32[]{:S(2)}) copy-start(bf16[64,768]{1,0:T(8,128)(2,1)} %get-tuple-element.193) | copy-start | bytes 294916
  420.0 11.2 %copy-start.60 = (bf16[2,64,768]{2,1,0:T(8,128)(2,1)S(1)}, bf16[2,64,768]{2,1,0:T(8,128)(2,1)}, u32[]{:S(2)}) copy-start(bf16[2,64,768]{2,1,0:T(8,128)(2,1)} %get-tuple-element.174) | copy-start | bytes 589828
  420.0 11.2 %copy-start.61 = (bf16[2,64,768]{2,1,0:T(8,128)(2,1)S(1)}, bf16[2,64,768]{2,1,0:T(8,128)(2,1)}, u32[]{:S(2)}) copy-start(bf16[2,64,768]{2,1,0:T(8,128)(2,1)} %get-tuple-element.175) | copy-start | bytes 589828
  434.5 8.0 slice-start.12
  436.0 6.4 slice-start.13
  448.3 270.2 %all-reduce.12.cloned.1.call-start = ((), (), s32[]{:S(2)}) async-start(), calls=%async_computation.1 | async-start | bytes 1572864 | tf_op jit(solution)/shard_map/psum | solution.py:424
  453.9 344.1 %all-reduce.14.cloned.1.call-start = ((), (), s32[]{:S(2)}) async-start(), calls=%async_computation.2 | async-start | bytes 6356992 | tf_op jit(solution)/shard_map/psum | solution.py:429
  (107 other events, 240.2 us)
Sparse Core Ops, SparseCore 0:
  19.1 126.3 all-gather.1
  448.4 242.5 all-reduce.15
  693.6 24.8 all-reduce.11
  720.7 77.1 all-reduce.13

commit v2 on v1

v2 whole, which is shorter than its diff:
```python
import jax
import jax.numpy as jnp
import numpy as np
from jax import lax
from jax.experimental import pallas as pl
from jax.experimental.pallas import tpu as pltpu
from jax.sharding import PartitionSpec as P

HEADS = 12
HEAD = 64
BUCKETS = 32
MAX_DIST = 128
PARTS = 16
GELU_SCALE = float(np.sqrt(2.0 / np.pi))


epsilon = 1e-06
highest = lax.Precision.HIGHEST


def bucket_row(length):
    distance = np.arange(length)
    half_count = BUCKETS // 2
    scaled = (
        np.log(np.maximum(distance, half_count) / half_count)
        / np.log(MAX_DIST / half_count)
        * (BUCKETS - half_count)
    )
    far_bucket = np.minimum(half_count + np.floor(scaled).astype(np.int32), BUCKETS - 1)
    return np.where(distance < half_count, distance, far_bucket).astype(np.int32)


def bucket_onehot(length):
    return (bucket_row(length)[None, :] == np.arange(BUCKETS)[:, None]).astype(np.float32)


def spread_distance(by_distance):
    head_count, length = by_distance.shape
    padded_row = jnp.concatenate(
        [jnp.zeros((head_count, length - 1), jnp.float32), by_distance], axis=1
    )
    tiled = jnp.tile(padded_row, (1, length))
    tiled = jnp.concatenate([tiled, jnp.zeros((head_count, length), jnp.float32)], axis=1)
    return tiled.reshape(head_count, length, 2 * length)[:, :, :length][:, :, ::-1]


def gather_distance(grid):
    head_count, length, _ = grid.shape
    flipped = jnp.concatenate(
        [grid[:, :, ::-1], jnp.zeros((head_count, length, length), jnp.float32)], axis=2
    )
    flat = flipped.reshape(head_count, 2 * length * length)[:, : length * (2 * length - 1)]
    return jnp.sum(flat.reshape(head_count, length, 2 * length - 1), axis=1)[:, length - 1 :]


ROWS_OWN = 48
TOKENS = 64
WIDE = 768
FF = 2048
GROUP = 256
GROUPS = 3
BATCHES = 2
STATES = 256
CHUNK = 512
ATT = 6144
VMEM_BYTES = 60 * 1024 * 1024
FULL = (PARTS, ROWS_OWN, WIDE)
GATED = (PARTS, ROWS_OWN, FF)
DOWN = (PARTS, FF // PARTS, WIDE)
DOWN_PIECES = [(piece, block) for piece in range(GROUPS) for block in range(8)]


def product(left, right, along_left=1, along_right=0):
    return lax.dot_general(
        left,
        right,
        (((along_left,), (along_right,)), ((), ())),
        preferred_element_type=jnp.float32,
    )


def low(value):
    return value.astype(jnp.bfloat16)


def same_head():
    row = lax.broadcasted_iota(jnp.int32, (GROUP, GROUP), 0) // HEAD
    lane = lax.broadcasted_iota(jnp.int32, (GROUP, GROUP), 1) // HEAD
    return jnp.where(row == lane, 1.0, 0.0)


def spread_heads(block, own_low):
    return jnp.concatenate([block] * 4, axis=0) * own_low


def fold_heads(block, own):
    kept = block * own
    return kept[:64] + kept[64:128] + kept[128:192] + kept[192:]


def scale_of(value):
    return lax.rsqrt(jnp.mean(value * value, axis=-1, keepdims=True) + epsilon)


def norm_back(grad, value, gain):
    scale = scale_of(value)
    carried = grad * gain
    mean = jnp.mean(value * carried, axis=-1, keepdims=True)
    grad_value = carried * scale - value * (scale * scale * scale) * mean
    grad_gain = jnp.sum(grad * value * scale, axis=0, keepdims=True)
    return grad_value, grad_gain


def square(ref):
    return ref[...].reshape(WIDE, WIDE)


def down_at(ref, base, piece, block):
    return ref.at[:, pl.ds(16 * piece, 16), pl.ds(base + GROUP * block, GROUP)]


def rows_at(ref, piece, block):
    return ref.at[:, pl.ds(16 * block, 16), pl.ds(GROUP * piece, GROUP)]


def softmax_rows(scores):
    raised = jnp.exp(scores - jnp.max(scores, axis=-1, keepdims=True))
    return raised / jnp.sum(raised, axis=-1, keepdims=True)


def gelu_parts(gate):
    cube = gate * gate * gate
    bent = jnp.tanh(GELU_SCALE * (gate + 0.044715 * cube))
    half = 0.5 * (1.0 + bent)
    slope = half + 0.5 * gate * (1.0 - bent * bent) * GELU_SCALE * (
        1.0 + 3.0 * 0.044715 * gate * gate
    )
    return gate * half, slope


def weight_copies(weight, slots, sems):
    copies = {}
    for place, (name, column) in enumerate(
        (("q", 0), ("k", 1), ("v", 2), ("o", 3), ("cq", 4), ("ck", 5), ("cv", 6), ("co", 7))
    ):
        if name in slots:
            source = weight.at[:, :, pl.ds(WIDE * column, WIDE)]
            copies[name] = [pltpu.make_async_copy(source, slots[name], sems.at[place])]
    for place, (name, column) in enumerate((("gate", ATT), ("up", ATT + FF))):
        if name in slots:
            source = weight.at[:, :, pl.ds(column, FF)]
            copies[name] = [pltpu.make_async_copy(source, slots[name], sems.at[8 + place])]
    if "down" in slots:
        copies["down"] = [
            pltpu.make_async_copy(
                down_at(weight, ATT + 2 * FF, piece, block),
                rows_at(slots["down"], piece, block),
                sems.at[10 + place],
            )
            for place, (piece, block) in enumerate(DOWN_PIECES)
        ]
    return copies


def begin(copies, names):
    for name in names:
        for copy in copies[name]:
            copy.start()


def finish(copies, name):
    for copy in copies[name]:
        copy.wait()


def forward_kernel(
    x_ref,
    enc_ref,
    self_add_ref,
    cross_add_ref,
    gains_ref,
    weight,
    out_ref,
    n1_ref,
    q_ref,
    k_ref,
    v_ref,
    p_ref,
    o_ref,
    a2_ref,
    n2_ref,
    cq_ref,
    ck_ref,
    cv_ref,
    cp_ref,
    co_ref,
    a3_ref,
    n3_ref,
    gate_ref,
    up_ref,
    hid_ref,
    wq,
    wk,
    wv,
    wo,
    wcq,
    wck,
    wcv,
    wco,
    wg,
    wu,
    wd,
    sems,
):
    slots = dict(q=wq, k=wk, v=wv, o=wo, cq=wcq, ck=wck, cv=wcv, co=wco, gate=wg, up=wu, down=wd)
    copies = weight_copies(weight, slots, sems)
    begin(copies, ("ck", "cv", "q", "k", "v", "o", "cq", "co", "gate", "up", "down"))
    own = same_head()
    own_low = low(own)
    stream = x_ref[...].astype(jnp.float32)
    normed = low(stream * scale_of(stream) * gains_ref[0:1])
    n1_ref[...] = normed
    finish(copies, "ck")
    for row in range(BATCHES):
        part = pl.ds(STATES * row, STATES)
        ck_ref[part] = low(product(enc_ref[part], square(wck)))
    finish(copies, "cv")
    for row in range(BATCHES):
        part = pl.ds(STATES * row, STATES)
        cv_ref[part] = low(product(enc_ref[part], square(wcv)))
    finish(copies, "q")
    q_ref[...] = low(product(normed, square(wq)))
    finish(copies, "k")
    k_ref[...] = low(product(normed, square(wk)))
    finish(copies, "v")
    v_ref[...] = low(product(normed, square(wv)))
    for row in range(BATCHES):
        part = pl.ds(TOKENS * row, TOKENS)
        for group in range(GROUPS):
            lanes = pl.ds(GROUP * group, GROUP)
            spread = spread_heads(q_ref[part, lanes], own_low)
            scores = product(spread, k_ref[part, lanes], 1, 1) + self_add_ref[row, lanes]
            chance = softmax_rows(scores)
            p_ref[row, lanes] = chance
            mixed = product(low(chance), v_ref[part, lanes])
            o_ref[part, lanes] = low(fold_heads(mixed, own))
    finish(copies, "o")
    stream = stream + product(o_ref[...], square(wo))
    a2_ref[...] = stream
    normed = low(stream * scale_of(stream) * gains_ref[1:2])
    n2_ref[...] = normed
    finish(copies, "cq")
    cq_ref[...] = low(product(normed, square(wcq)))
    for row in range(BATCHES):
        part = pl.ds(TOKENS * row, TOKENS)
        keys = pl.ds(STATES * row, STATES)
        add = jnp.concatenate([cross_add_ref[row]] * 4, axis=0)
        for group in range(GROUPS):
            lanes = pl.ds(GROUP * group, GROUP)
            spread = spread_heads(cq_ref[part, lanes], own_low)
            scores = product(spread, ck_ref[keys, lanes], 1, 1) + add
            chance = softmax_rows(scores)
            cp_ref[row, lanes] = chance
            mixed = product(low(chance), cv_ref[keys, lanes])
            co_ref[part, lanes] = low(fold_heads(mixed, own))
    finish(copies, "co")
    stream = a2_ref[...] + product(co_ref[...], square(wco))
    a3_ref[...] = stream
    n3_ref[...] = low(stream * scale_of(stream) * gains_ref[2:3])
    finish(copies, "gate")
    finish(copies, "up")
    finish(copies, "down")

    def step(index, total):
        lanes = pl.ds(pl.multiple_of(index * CHUNK, CHUNK), CHUNK)
        rows = n3_ref[...]
        gate = product(rows, wg[:, :, lanes].reshape(WIDE, CHUNK))
        up = product(rows, wu[:, :, lanes].reshape(WIDE, CHUNK))
        gate_ref[:, lanes] = gate
        up_ref[:, lanes] = up
        bent = 0.5 * (1.0 + jnp.tanh(GELU_SCALE * (gate + 0.044715 * (gate * gate * gate))))
        hidden = low(gate * bent * up)
        hid_ref[:, lanes] = hidden
        return total + product(hidden, wd[pl.ds(4 * index, 4)].reshape(CHUNK, WIDE))

    total = lax.fori_loop(0, FF // CHUNK, step, jnp.zeros((BATCHES * TOKENS, WIDE), jnp.float32))
    out_ref[...] = low(a3_ref[...] + total)


def backward_kernel(
    c_ref,
    x_ref,
    gains_ref,
    q_ref,
    k_ref,
    v_ref,
    p_ref,
    a2_ref,
    cq_ref,
    ck_ref,
    cv_ref,
    cp_ref,
    a3_ref,
    gate_ref,
    up_ref,
    weight,
    da_ref,
    dgate_ref,
    dup_ref,
    dc_ref,
    dcq_ref,
    dck_ref,
    dcv_ref,
    dself_ref,
    dq_ref,
    dk_ref,
    dv_ref,
    dgain_ref,
    dscore_ref,
    wq,
    wk,
    wv,
    wo,
    wcq,
    wco,
    wg,
    wu,
    wd,
    sems,
):
    slots = dict(q=wq, k=wk, v=wv, o=wo, cq=wcq, co=wco, gate=wg, up=wu, down=wd)
    copies = weight_copies(weight, slots, sems)
    begin(copies, ("down", "gate", "up", "co", "cq", "o", "q", "k", "v"))
    own = same_head()
    own_low = low(own)
    finish(copies, "down")
    finish(copies, "gate")
    finish(copies, "up")

    def step(index, total):
        lanes = pl.ds(pl.multiple_of(index * CHUNK, CHUNK), CHUNK)
        grad = product(c_ref[...], wd[pl.ds(4 * index, 4)].reshape(CHUNK, WIDE), 1, 1)
        bent, slope = gelu_parts(gate_ref[:, lanes])
        dgate = low(grad * up_ref[:, lanes] * slope)
        dup = low(grad * bent)
        dgate_ref[:, lanes] = dgate
        dup_ref[:, lanes] = dup
        total = total + product(dgate, wg[:, :, lanes].reshape(WIDE, CHUNK), 1, 1)
        return total + product(dup, wu[:, :, lanes].reshape(WIDE, CHUNK), 1, 1)

    grad = lax.fori_loop(0, FF // CHUNK, step, jnp.zeros((BATCHES * TOKENS, WIDE), jnp.float32))
    back, dgain = norm_back(grad, a3_ref[...], gains_ref[2:3])
    dgain_ref[2:3] = dgain
    stream = c_ref[...].astype(jnp.float32) + back
    dc_ref[...] = low(stream)
    finish(copies, "co")
    datt = low(product(dc_ref[...], square(wco), 1, 1))
    for row in range(BATCHES):
        part = pl.ds(TOKENS * row, TOKENS)
        keys = pl.ds(STATES * row, STATES)
        for group in range(GROUPS):
            lanes = pl.ds(GROUP * group, GROUP)
            left = GROUP * group
            dout = spread_heads(
                datt[TOKENS * row : TOKENS * (row + 1), left : left + GROUP], own_low
            )
            spread = spread_heads(cq_ref[part, lanes], own_low)
            chance = cp_ref[row, lanes]
            dchance = product(dout, cv_ref[keys, lanes], 1, 1)
            dcv_ref[keys, lanes] = low(product(low(chance), dout, 0, 0))
            inner = jnp.sum(chance * dchance, axis=-1, keepdims=True)
            dscore = low(chance * (dchance - inner))
            dcq_ref[part, lanes] = low(fold_heads(product(dscore, ck_ref[keys, lanes]), own))
            dck_ref[keys, lanes] = low(product(dscore, spread, 0, 0))
    finish(copies, "cq")
    grad = product(dcq_ref[...], square(wcq), 1, 1)
    back, dgain = norm_back(grad, a2_ref[...], gains_ref[1:2])
    dgain_ref[1:2] = dgain
    stream = stream + back
    dself_ref[...] = low(stream)
    finish(copies, "o")
    datt = low(product(dself_ref[...], square(wo), 1, 1))
    for row in range(BATCHES):
        part = pl.ds(TOKENS * row, TOKENS)
        for group in range(GROUPS):
            lanes = pl.ds(GROUP * group, GROUP)
            left = GROUP * group
            dout = spread_heads(
                datt[TOKENS * row : TOKENS * (row + 1), left : left + GROUP], own_low
            )
            spread = spread_heads(q_ref[part, lanes], own_low)
            chance = p_ref[row, lanes]
            dchance = product(dout, v_ref[part, lanes], 1, 1)
            dv_ref[part, lanes] = low(product(low(chance), dout, 0, 0))
            inner = jnp.sum(chance * dchance, axis=-1, keepdims=True)
            dscore = low(chance * (dchance - inner))
            if row == 0:
                dscore_ref[lanes] = dscore.astype(jnp.float32)
            else:
                dscore_ref[lanes] += dscore.astype(jnp.float32)
            dq_ref[part, lanes] = low(fold_heads(product(dscore, k_ref[part, lanes]), own))
            dk_ref[part, lanes] = low(product(dscore, spread, 0, 0))
    finish(copies, "q")
    grad = product(dq_ref[...], square(wq), 1, 1)
    finish(copies, "k")
    grad = grad + product(dk_ref[...], square(wk), 1, 1)
    finish(copies, "v")
    grad = grad + product(dv_ref[...], square(wv), 1, 1)
    back, dgain = norm_back(grad, x_ref[...].astype(jnp.float32), gains_ref[0:1])
    dgain_ref[0:1] = dgain
    da_ref[...] = low(stream + back)


def weight_kernel(
    c_ref,
    enc_ref,
    n1_ref,
    o_ref,
    n2_ref,
    co_ref,
    n3_ref,
    hid_ref,
    dgate_ref,
    dup_ref,
    dc_ref,
    dcq_ref,
    dck_ref,
    dcv_ref,
    dself_ref,
    dq_ref,
    dk_ref,
    dv_ref,
    weight,
    grads,
    denc_ref,
    wck,
    wcv,
    gq,
    gk,
    gv,
    go,
    gcq,
    gck,
    gcv,
    gco,
    gg,
    gu,
    gd,
    sems,
    out_sems,
):
    copies = weight_copies(weight, dict(ck=wck, cv=wcv), sems)
    begin(copies, ("ck", "cv"))
    slots = dict(q=gq, k=gk, v=gv, o=go, cq=gcq, ck=gck, cv=gcv, co=gco, gate=gg, up=gu, down=gd)
    outward = {
        name: [pltpu.make_async_copy(slots[name], grads.at[:, :, pl.ds(WIDE * place, WIDE)], out_sems.at[place])]
        for place, name in enumerate(("q", "k", "v", "o", "cq", "ck", "cv", "co"))
    }
    for place, name in enumerate(("gate", "up")):
        target = grads.at[:, :, pl.ds(ATT + FF * place, FF)]
        outward[name] = [pltpu.make_async_copy(slots[name], target, out_sems.at[8 + place])]
    outward["down"] = [
        pltpu.make_async_copy(
            rows_at(gd, piece, block),
            down_at(grads, ATT + 2 * FF, piece, block),
            out_sems.at[10 + place],
        )
        for place, (piece, block) in enumerate(DOWN_PIECES)
    ]

    def down_step(index, carry):
        lanes = pl.ds(pl.multiple_of(index * CHUNK, CHUNK), CHUNK)
        grad = low(product(hid_ref[:, lanes], c_ref[...], 0, 0))
        gd[pl.ds(4 * index, 4)] = grad.reshape(4, FF // PARTS, WIDE)
        return carry

    lax.fori_loop(0, FF // CHUNK, down_step, 0)
    begin(outward, ("down",))

    def up_step(index, carry):
        lanes = pl.ds(pl.multiple_of(index * CHUNK, CHUNK), CHUNK)
        rows = n3_ref[...]
        shape = (PARTS, ROWS_OWN, CHUNK)
        gg[:, :, lanes] = low(product(rows, dgate_ref[:, lanes], 0, 0)).reshape(shape)
        gu[:, :, lanes] = low(product(rows, dup_ref[:, lanes], 0, 0)).reshape(shape)
        return carry

    lax.fori_loop(0, FF // CHUNK, up_step, 0)
    begin(outward, ("gate", "up"))
    for name, left, right in (
        ("co", co_ref, dc_ref),
        ("cq", n2_ref, dcq_ref),
        ("ck", enc_ref, dck_ref),
        ("cv", enc_ref, dcv_ref),
        ("o", o_ref, dself_ref),
        ("q", n1_ref, dq_ref),
        ("k", n1_ref, dk_ref),
        ("v", n1_ref, dv_ref),
    ):
        slots[name][...] = low(product(left[...], right[...], 0, 0)).reshape(FULL)
        begin(outward, (name,))
    finish(copies, "ck")
    finish(copies, "cv")
    for row in range(BATCHES):
        keys = pl.ds(STATES * row, STATES)
        denc_ref[keys] = low(
            product(dck_ref[keys], square(wck), 1, 1) + product(dcv_ref[keys], square(wcv), 1, 1)
        )
    for name in ("down", "gate", "up", "co", "cq", "ck", "cv", "o", "q", "k", "v"):
        finish(outward, name)


def in_vmem(count):
    return [pl.BlockSpec(memory_space=pltpu.VMEM)] * count


def held(*shapes):
    return [pltpu.VMEM(shape, jnp.bfloat16) for shape in shapes]


def shape_of(dims, kind=jnp.bfloat16):
    return jax.ShapeDtypeStruct(dims, kind)


ALL_TOKENS = (BATCHES * TOKENS, WIDE)
ALL_STATES = (BATCHES * STATES, WIDE)
HIDDEN = (BATCHES * TOKENS, FF)
params = pltpu.CompilerParams(vmem_limit_bytes=VMEM_BYTES)


def run_forward(x, enc, self_add, cross_add, gains, weight):
    wide = jnp.float32
    outs = [
        shape_of(ALL_TOKENS),
        shape_of(ALL_TOKENS),
        shape_of(ALL_TOKENS),
        shape_of(ALL_TOKENS),
        shape_of(ALL_TOKENS),
        shape_of((BATCHES, WIDE, TOKENS), wide),
        shape_of(ALL_TOKENS),
        shape_of(ALL_TOKENS, wide),
        shape_of(ALL_TOKENS),
        shape_of(ALL_TOKENS),
        shape_of(ALL_STATES),
        shape_of(ALL_STATES),
        shape_of((BATCHES, WIDE, STATES), wide),
        shape_of(ALL_TOKENS),
        shape_of(ALL_TOKENS, wide),
        shape_of(ALL_TOKENS),
        shape_of(HIDDEN, wide),
        shape_of(HIDDEN, wide),
        shape_of(HIDDEN),
    ]
    return pl.pallas_call(
        forward_kernel,
        out_shape=outs,
        in_specs=in_vmem(5) + [pl.BlockSpec(memory_space=pl.ANY)],
        out_specs=in_vmem(len(outs)),
        scratch_shapes=held(*[FULL] * 8, GATED, GATED, DOWN) + [pltpu.SemaphoreType.DMA((34,))],
        compiler_params=params,
        name="layer_forward",
    )(x, enc, self_add, cross_add, gains, weight)


def run_backward(cotangent, x, gains, saved, weight):
    (n1, q, k, v, p, o, a2, n2, cq, ck, cv, cp, co, a3, n3, gate, up, hid) = saved
    outs = [
        shape_of(ALL_TOKENS),
        shape_of(HIDDEN),
        shape_of(HIDDEN),
        shape_of(ALL_TOKENS),
        shape_of(ALL_TOKENS),
        shape_of(ALL_STATES),
        shape_of(ALL_STATES),
        shape_of(ALL_TOKENS),
        shape_of(ALL_TOKENS),
        shape_of(ALL_TOKENS),
        shape_of(ALL_TOKENS),
        shape_of((3, WIDE), jnp.float32),
        shape_of((WIDE, TOKENS), jnp.float32),
    ]
    return pl.pallas_call(
        backward_kernel,
        out_shape=outs,
        in_specs=in_vmem(15) + [pl.BlockSpec(memory_space=pl.ANY)],
        out_specs=in_vmem(len(outs)),
        scratch_shapes=held(*[FULL] * 6, GATED, GATED, DOWN) + [pltpu.SemaphoreType.DMA((34,))],
        compiler_params=params,
        name="layer_backward",
    )(cotangent, x, gains, q, k, v, p, a2, cq, ck, cv, cp, a3, gate, up, weight)


def run_weights(cotangent, enc, saved, records, weight):
    (n1, q, k, v, p, o, a2, n2, cq, ck, cv, cp, co, a3, n3, gate, up, hid) = saved
    (dgate, dup, dc, dcq, dck, dcv, dself, dq, dk, dv) = records
    return pl.pallas_call(
        weight_kernel,
        out_shape=[shape_of((PARTS, ROWS_OWN, 2 * ATT)), shape_of(ALL_STATES)],
        in_specs=in_vmem(18) + [pl.BlockSpec(memory_space=pl.ANY)],
        out_specs=[pl.BlockSpec(memory_space=pl.ANY)] + in_vmem(1),
        scratch_shapes=held(FULL, FULL, *[FULL] * 8, GATED, GATED, DOWN)
        + [pltpu.SemaphoreType.DMA((34,)), pltpu.SemaphoreType.DMA((34,))],
        compiler_params=params,
        name="weight_gradients",
    )(
        cotangent, enc, n1, o, n2, co, n3, hid, dgate, dup, dc, dcq, dck, dcv, dself, dq, dk, dv, weight
    )


def pack(query, kv, out, c_query, c_kv, c_out, w_in, w_ffn):
    rows = query.shape[0]
    pieces = w_ffn.reshape(8, 16, GROUPS, GROUP).transpose(2, 1, 0, 3)
    return jnp.concatenate(
        [
            query,
            kv.reshape(rows, -1),
            out,
            c_query,
            c_kv.reshape(rows, -1),
            c_out,
            w_in.reshape(rows, -1),
            pieces.reshape(rows, FF),
        ],
        axis=1,
    )


def unpack(block):
    rows = block.shape[0]
    start = 0
    pieces = []
    for width in (768, 1536, 768, 768, 1536, 768, 4096, 2048):
        pieces.append(block[:, start : start + width])
        start += width
    query, kv, out, c_query, c_kv, c_out, w_in, w_ffn = pieces
    return (
        query,
        kv.reshape(rows, 2, WIDE),
        out,
        c_query,
        c_kv.reshape(rows, 2, WIDE),
        c_out,
        w_in.reshape(rows, 2, FF),
        w_ffn.reshape(GROUPS, 16, 8, GROUP).transpose(2, 1, 0, 3).reshape(FF // PARTS, WIDE),
    )


def score_terms(table, dec_ids, enc_ids):
    positions = jnp.arange(TOKENS)
    by_distance = jnp.dot(table.astype(jnp.float32).T, bucket_onehot(TOKENS), precision=highest)
    bias = spread_distance(by_distance)
    allowed = (dec_ids[:, :, None] == dec_ids[:, None, :]) & (
        positions[None, :] <= positions[:, None]
    )
    self_add = jnp.where(allowed[:, None], bias[None], -jnp.inf)
    cross_add = jnp.where(dec_ids[:, :, None] == enc_ids[:, None, :], 0.0, -jnp.inf)
    return self_add.reshape(BATCHES, WIDE, TOKENS), cross_add


def shards(
    layer_in,
    cotangent,
    encoder,
    dec_segments,
    enc_segments,
    norm_gains,
    self_query,
    self_kv,
    self_out,
    rel_bias,
    cross_query,
    cross_kv,
    cross_out,
    ffn_in,
    ffn_out,
):
    section_index = lax.axis_index("section")
    part_index = lax.axis_index("fsdp")
    own = pack(
        self_query[0],
        self_kv[0],
        self_out[0],
        cross_query[0],
        cross_kv[0],
        cross_out[0],
        ffn_in[0],
        ffn_out[0],
    )
    weight = lax.all_gather(own, "fsdp", axis=0, tiled=True).reshape(PARTS, ROWS_OWN, 2 * ATT)
    small = jnp.zeros((8, 128), jnp.bfloat16)
    small = small.at[:3, :ROWS_OWN].set(norm_gains[0])
    small = small.at[3:5, :HEADS].set(rel_bias[0])
    small = lax.all_gather(small, "fsdp", axis=0, tiled=False)
    gains = small[:, :3, :ROWS_OWN].transpose(1, 0, 2).reshape(3, WIDE).astype(jnp.float32)
    table = small[:, 3:5, :HEADS].reshape(BUCKETS, HEADS)
    self_add, cross_add = score_terms(table, dec_segments[:, 0], enc_segments[:, 0])
    rows_in = layer_in[:, 0].reshape(ALL_TOKENS)
    given = cotangent[:, 0].reshape(ALL_TOKENS)
    enc = encoder[:, 0].reshape(ALL_STATES)
    first = run_forward(rows_in, enc, self_add, cross_add, gains, weight)[0]
    received = lax.ppermute(first, "section", [(0, 1)])
    current = jnp.where(section_index == 0, rows_in, received)
    result, *saved = run_forward(current, enc, self_add, cross_add, gains, weight)
    grad_first = run_backward(given, current, gains, saved, weight)[0]
    returned = lax.ppermute(grad_first, "section", [(1, 0)])
    incoming = jnp.where(section_index == 1, given, returned)
    grad_input, *records, grad_gains, grad_scores = run_backward(
        incoming, current, gains, saved, weight
    )
    grads, grad_enc = run_weights(incoming, enc, saved, records, weight)
    owned = lax.psum_scatter(
        grads.reshape(WIDE, 2 * ATT), "fsdp", scatter_dimension=0, tiled=True
    )
    other_enc = lax.ppermute(grad_enc, "section", [(0, 1), (1, 0)])
    encoder_total = grad_enc.astype(jnp.float32) + other_enc.astype(jnp.float32)
    diagonal_sums = gather_distance(grad_scores.reshape(HEADS, TOKENS, TOKENS))
    grad_table = jnp.dot(bucket_onehot(TOKENS), diagonal_sums.T, precision=highest)
    little = jnp.zeros((8, WIDE), jnp.float32)
    little = little.at[:3].set(grad_gains)
    little = little.at[3, : BUCKETS * HEADS].set(grad_table.reshape(-1))
    little = lax.psum(little, ("fsdp", "rep"))
    own_gains = lax.dynamic_slice(little, (0, part_index * ROWS_OWN), (3, ROWS_OWN))
    own_table = lax.dynamic_slice(little, (3, part_index * 2 * HEADS), (1, 2 * HEADS))
    quarters = owned.reshape(ROWS_OWN, 4, 2 * ATT // 4)
    quarters = lax.all_to_all(quarters, "rep", split_axis=1, concat_axis=1, tiled=True)
    quarter = low(jnp.sum(quarters.astype(jnp.float32), axis=1))
    summed = lax.all_gather(quarter, "rep", axis=1, tiled=True).astype(jnp.float32)
    query, kv, out, c_query, c_kv, c_out, w_in, w_ffn = unpack(summed)
    ordered = (
        own_gains,
        query,
        kv,
        out,
        own_table.reshape(2, HEADS),
        c_query,
        c_kv,
        c_out,
        w_in,
        w_ffn,
    )
    return (
        result.reshape(1, BATCHES, 1, TOKENS, WIDE),
        grad_input.reshape(1, BATCHES, 1, TOKENS, WIDE),
        encoder_total.reshape(BATCHES, 1, STATES, WIDE),
    ) + tuple(member[None] for member in ordered)


def solution(mesh):
    return jax.shard_map(
        shards,
        mesh=mesh,
        in_specs=(
            P(None, ("fsdp", "rep"), None, None),
            P(None, ("fsdp", "rep"), None, None),
            P(None, ("fsdp", "rep"), None, None),
            P(None, ("fsdp", "rep"), None),
            P(None, ("fsdp", "rep"), None),
            P("section", None, "fsdp"),
            P("section", "fsdp", None),
            P("section", "fsdp", None, None),
            P("section", "fsdp", None),
            P("section", "fsdp", None),
            P("section", "fsdp", None),
            P("section", "fsdp", None, None),
            P("section", "fsdp", None),
            P("section", "fsdp", None, None),
            P("section", "fsdp", None),
        ),
        out_specs=(
            P("section", None, ("fsdp", "rep"), None, None),
            P("section", None, ("fsdp", "rep"), None, None),
            P(None, ("fsdp", "rep"), None, None),
            P("section", None, "fsdp"),
            P("section", "fsdp", None),
            P("section", "fsdp", None, None),
            P("section", "fsdp", None),
            P("section", "fsdp", None),
            P("section", "fsdp", None),
            P("section", "fsdp", None, None),
            P("section", "fsdp", None),
            P("section", "fsdp", None, None),
            P("section", "fsdp", None),
        ),
        check_vma=False,
    )
```

time: 840 us -> 742 us (0.88)
  the two profiles are of different devices: /device:TPU:1 before, /device:TPU:0 now
where the time goes in v2:
time: 742 us; the launch traced here: 741 us
  blocking collectives  391 us (53%)
  waiting for transfers between devices  220 us (30%)
  Pallas kernels  86.2 us (12%)
  local copies, waits for them, and re-layouts  18.8 us (3%)
  between operations  14.3 us (2%)
    psum x1, blocking collectives, shards(): little = lax.psum(little, ('fsdp', 'rep'))  345 us
    reduce_scatter x1, waiting for transfers between devices, shards(): lax.psum_scatter(grads.reshape(WIDE, 2 * ATT), 'fsdp', scatter_dimension=...  121 us
    all_gather x1, waiting for transfers between devices, shards(): lax.all_gather(own, 'fsdp', axis=0, tiled=True)  95.9 us
    pallas_call x2, Pallas kernels, run_backward(): pl.pallas_call(backward_kernel, out_shape=outs, in_specs=in_vmem(15) + [p...  42.4 us
    pallas_call x2, Pallas kernels, run_forward(): pl.pallas_call(forward_kernel, out_shape=outs, in_specs=in_vmem(5) + [pl....  30.1 us
    all_gather x1, blocking collectives, shards(): small = lax.all_gather(small, 'fsdp', axis=0, tiled=False)  24.7 us
    all_to_all x1, blocking collectives, shards(): lax.all_to_all(quarters, 'rep', split_axis=1, concat_axis=1, tiled=True)  20.5 us
  transfers between devices with their start and end apart: 6, of which 4 were waited for; matrix products, arithmetic and copies ran while one was open for 1% of the time, Pallas kernels for 0%

profile of v2, /device:TPU:0, one launch (start us, length us, event | category | flops | bytes accessed | tf_op | source)
XLA Modules:
  0.0 741.1 jit_solution(4179262509064751541)
XLA Ops:
  7.2 0.0 all-gather.3.cloned.1.call-start
  7.2 0.9 bitcast_dynamic-update-slice_fusion.3
  8.2 0.9 copy.69
  9.1 0.9 copy.70
  10.0 1.2 copy.71
  11.2 0.1 reshape_squeeze.26
  11.3 0.1 copy.58
  11.6 0.5 copy-done.9
  12.2 1.0 copy-done.1
  13.2 0.0 reduce-scatter.2.cloned.1.call-start
  13.3 0.3 scatter.15
  13.6 24.7 %all_gather.13 = bf16[16,8,128]{2,1,0:T(8,128)(2,1)S(1)} all-gather(bf16[1,8,128]{2,1,0:T(8,128)(2,1)S(1)} %scatter.15), channel_id=1, replica_groups=mesh['section'=2,'fsdp'=16,'rep'=4] {'fsdp'}, dimensions={0}, use_global_device_ids=true | all-gather | bytes 34816 | tf_op jit(solution)/shard_map/all_gather | solution.py:693
  38.4 0.7 reshape.223.gains_ref
  39.1 0.2 fusion.3
  39.3 0.1 concatenate.20
  39.4 0.3 tile.10
  39.7 0.1 copy.68
  39.9 0.2 rev.6
  40.0 0.4 copy-done.13
  40.4 0.1 compare_and_fusion
  40.5 0.9 bitcast_select_fusion.self_add_ref
  41.4 0.7 compare_select_fusion.cross_add_ref
  42.2 95.9 %all-gather.3.cloned.1.call-done = bf16[768,12288]{1,0:T(8,128)(2,1)} async-done(((bf16[48,12288]{1,0:T(8,128)(2,1)}), bf16[768,12288]{1,0:T(8,128)(2,1)}) %all-gather.3.cloned.1.call-update) | async-done | bytes 18874384 | tf_op jit(solution)/shard_map/all_gather | solution.py:689
  138.1 15.1 %layer_forward.2 = (bf16[128,768]{1,0:T(8,128)(2,1)}, bf16[128,768]{1,0:T(8,128)(2,1)}, bf16[128,768]{1,0:T(8,128)(2,1)}, bf16[128,768]{1,0:T(8,128)(2,1)}, bf16...) custom-call(bf16[128,768]{1,0:T(8,128)(2,1)} %bitcast.101, ...), custom_call_target="tpu_custom_call" | custom-call | tf_op jit(solution)/shard_map/layer_forward/pallas_call | solution.py:554
  153.2 1.9 collective-permute-start
  155.1 1.1 collective-permute-done
  156.2 0.7 broadcast_select_fusion.1.x_ref
  156.9 15.0 %layer_forward.3 = (bf16[128,768]{1,0:T(8,128)(2,1)}, bf16[128,768]{1,0:T(8,128)(2,1)}, bf16[128,768]{1,0:T(8,128)(2,1)}, bf16[128,768]{1,0:T(8,128)(2,1)}, bf16...) custom-call(bf16[128,768]{1,0:T(8,128)(2,1)} %broadcast_select_fusio, ...), custom_call_target="tpu_custom_call" | custom-call | tf_op jit(solution)/shard_map/layer_forward/pallas_call | solution.py:554
  172.0 21.2 %layer_backward.2 = (bf16[128,768]{1,0:T(8,128)(2,1)}, bf16[128,2048]{1,0:T(8,128)(2,1)}, bf16[128,2048]{1,0:T(8,128)(2,1)}, bf16[128,768]{1,0:T(8,128)(2,1)}, b...) custom-call(bf16[128,768]{1,0:T(8,128)(2,1)} %bitcast.102, ...), custom_call_target="tpu_custom_call" | custom-call | tf_op jit(solution)/shard_map/layer_backward/pallas_call | solution.py:582
  193.2 1.5 collective-permute-start.1
  194.7 2.0 collective-permute-done.1
  196.7 0.7 broadcast_select_fusion.c_ref
  197.4 21.1 %layer_backward.3 = (bf16[128,768]{1,0:T(8,128)(2,1)}, bf16[128,2048]{1,0:T(8,128)(2,1)}, bf16[128,2048]{1,0:T(8,128)(2,1)}, bf16[128,768]{1,0:T(8,128)(2,1)}, b...) custom-call(bf16[128,768]{1,0:T(8,128)(2,1)} %broadcast_select_fusio, ...), custom_call_target="tpu_custom_call" | custom-call | tf_op jit(solution)/shard_map/layer_backward/pallas_call | solution.py:582
  218.6 13.8 %weight_gradients.1 = (bf16[16,48,12288]{2,1,0:T(8,128)(2,1)}, bf16[512,768]{1,0:T(8,128)(2,1)}) custom-call(bf16[128,768]{1,0:T(8,128)(2,1)} %broadcast_select_fusion.c_ref, bf16[512,768]{1,0:T(8,128)(2,1)} %bitcast.87, bf16[128,768]{1,0:T(8,128)(2,1)} %get-tuple-element.113.n1_ref, bf16[128,768]{1,0:T(8,128)(2,1)} %get-tuple-element.114.o_ref, ...), custom_call_target="tpu_custom_call" | custom-call | tf_op jit(solution)/shard_map/weight_gradients/pallas_call | solution.py:596
  232.4 0.0 all-gather.5.cloned.1.call-start
  232.4 120.9 %reduce-scatter.2.cloned.1.call-done = bf16[48,12288]{1,0:T(8,128)(2,1)} async-done(((bf16[768,12288]{1,0:T(8,128)(2,1)}), bf16[48,12288]{1,0:T(8,128)(2,1)}) %reduce-scatter.2.cloned.1.call-update) | async-done | bytes 1179664 | tf_op jit(solution)/shard_map/reduce_scatter | solution.py:711
  353.4 1.3 copy.78
  354.7 20.5 %all_to_all.5 = bf16[48,4,3072]{2,0,1:T(8,128)(2,1)S(1)} all-to-all(bf16[48,4,3072]{2,0,1:T(8,128)(2,1)S(1)} %bitcast.88), channel_id=1, replica_groups=mesh['section'=2,'fsdp'=16,'rep'=4] {'rep'}, dimensions={1} | all-to-all | bytes 2359296 | tf_op jit(solution)/shard_map/all_to_all | solution.py:725
  375.3 0.9 reduce_sum.22
  376.2 0.2 copy-done.4
  376.4 0.2 collective-permute-start.2
  376.6 0.2 rev.7
  376.9 0.3 copy.73
  377.2 0.7 reshape.218
  377.9 0.1 reduce_sum.21
  378.0 0.2 fusion
  378.2 0.1 reshape.219
  378.3 0.3 scatter.19
  378.6 345.4 %psum.7 = f32[8,768]{1,0:T(8,128)S(1)} all-reduce(f32[8,768]{1,0:T(8,128)S(1)} %scatter.19), channel_id=1, replica_groups=mesh['section'=2,'fsdp'=16,'rep'=4] {'fsdp','rep'}, use_global_device_ids=true, to_apply=%region_1.0 | all-reduce | flops 6144 | bytes 49152 | tf_op jit(solution)/shard_map/psum | solution.py:721
  724.0 0.1 dynamic-slice_reduce_fusion
  724.1 0.6 broadcast_in_dim_reshape.16
  724.8 0.1 constant_dynamic-slice_fusion
  724.8 0.6 broadcast_in_dim.64
  725.4 1.3 convert_add_fusion
  726.7 1.4 convert_element_type.24
  728.1 0.8 slice_bitcast_fusion
  729.0 0.7 copy-done
  729.7 0.1 copy.74
  729.8 0.3 copy.79
  730.1 1.0 broadcast_in_dim_reshape.19
  731.1 0.1 slice.139
  731.1 1.5 broadcast_in_dim_reshape.18
  732.7 0.9 broadcast_in_dim_reshape.15
  733.6 0.9 broadcast_in_dim_reshape.17
  (54 shorter events, 0.6 us)
Async XLA Ops:
  7.2 4.0 copy-start.6
  7.2 130.9 %all-gather.3.cloned.1.call-start = ((), (), s32[]{:S(2)}) async-start(), calls=%async_computation.2 | async-start | bytes 20054016 | tf_op jit(solution)/shard_map/all_gather | solution.py:689
  10.0 1.5 copy-start.7
  10.0 1.5 copy-start.8
  11.2 0.9 copy-start.9
  12.1 1.2 copy-start.14
  12.1 1.2 copy-start.15
  12.1 27.0 %copy-start.10 = (f32[32,64]{1,0:T(8,128)S(1)}, f32[32,64]{1,0:T(8,128)}, u32[]{:S(2)}) copy-start(f32[32,64]{1,0:T(8,128)} %constant.139.clone) | copy-start | bytes 24580
  12.2 1.0 copy-start.1
  13.2 340.1 %reduce-scatter.2.cloned.1.call-start = ((), (), s32[]{:S(2)}) async-start(), calls=%async_computation.3 | async-start | bytes 20054016 | tf_op jit(solution)/shard_map/reduce_scatter | solution.py:711
  39.7 0.7 copy-start.13
  39.7 0.7 copy-start.12
  138.1 18.1 %copy-start.2 = (bf16[2,1,64,768]{3,2,1,0:T(8,128)(2,1)S(1)}, bf16[2,1,64,768]{3,2,1,0:T(8,128)(2,1)}, u32[]{:S(2)}) copy-start(bf16[2,1,64,768]{3,2,1,0:T(8,128)(2,1)} %param.25) | copy-start | bytes 589828
  153.2 3.0 collective-permute-start
  171.9 24.8 %copy-start.3 = (bf16[2,1,64,768]{3,2,1,0:T(8,128)(2,1)S(1)}, bf16[2,1,64,768]{3,2,1,0:T(8,128)(2,1)}, u32[]{:S(2)}) copy-start(bf16[2,1,64,768]{3,2,1,0:T(8,128)(2,1)} %param.26) | copy-start | bytes 589828
  193.2 3.5 collective-permute-start.1
  232.4 494.3 %all-gather.5.cloned.1.call-start = ((), (), s32[]{:S(2)}) async-start(), calls=%async_computation.4 | async-start | bytes 1474560 | tf_op jit(solution)/shard_map/all_gather | solution.py:727
  375.3 1.1 copy-start.4
  375.3 1.3 copy-start.5
  376.4 349.0 %collective-permute-start.2 = (bf16[512,768]{1,0:T(8,128)(2,1)S(1)}, bf16[512,768]{1,0:T(8,128)(2,1)S(1)}, u32[]{:S(2)}, u32[]{:S(2)}) collective-permute-start(bf16[512,768]{1,0:T(8,128)(2,1)S(1)} %copy-done.4), channel_id=1, source_target_pairs={{0,64},{64,0},{1,65},{65,1},{2,66},{66,2},{3,67},{67,3},{4,68},{68... | collective-permute-start | bytes 2359304 | tf_op jit(solution)/shard_map/ppermute | solution.py:714
  376.9 1.4 copy-start.11
  728.1 1.5 copy-start
Sparse Core Ops, SparseCore 0:
  13.4 124.6 all-gather.2
  232.5 120.8 reduce-scatter.1
  376.4 22.5 all-gather.4

commit v3 on v2

--- a/solution.py
+++ b/solution.py
@@ -115,8 +115,8 @@
     return ref[...].reshape(WIDE, WIDE)
 
 
-def down_at(ref, base, piece, block):
-    return ref.at[:, pl.ds(16 * piece, 16), pl.ds(base + GROUP * block, GROUP)]
+def down_at(ref, piece, block):
+    return ref.at[:, 1, pl.ds(16 * piece, 16), pl.ds(2 * FF + GROUP * block, GROUP)]
 
 
 def rows_at(ref, piece, block):
@@ -144,16 +144,16 @@
         (("q", 0), ("k", 1), ("v", 2), ("o", 3), ("cq", 4), ("ck", 5), ("cv", 6), ("co", 7))
     ):
         if name in slots:
-            source = weight.at[:, :, pl.ds(WIDE * column, WIDE)]
+            source = weight.at[:, 0, :, pl.ds(WIDE * column, WIDE)]
             copies[name] = [pltpu.make_async_copy(source, slots[name], sems.at[place])]
-    for place, (name, column) in enumerate((("gate", ATT), ("up", ATT + FF))):
+    for place, (name, column) in enumerate((("gate", 0), ("up", FF))):
         if name in slots:
-            source = weight.at[:, :, pl.ds(column, FF)]
+            source = weight.at[:, 1, :, pl.ds(column, FF)]
             copies[name] = [pltpu.make_async_copy(source, slots[name], sems.at[8 + place])]
     if "down" in slots:
         copies["down"] = [
             pltpu.make_async_copy(
-                down_at(weight, ATT + 2 * FF, piece, block),
+                down_at(weight, piece, block),
                 rows_at(slots["down"], piece, block),
                 sems.at[10 + place],
             )
@@ -173,7 +173,8 @@
         copy.wait()
 
 
-def forward_kernel(
+def forward_body(
+    keys_given,
     x_ref,
     enc_ref,
     self_add_ref,
@@ -212,22 +213,24 @@
     wd,
     sems,
 ):
-    slots = dict(q=wq, k=wk, v=wv, o=wo, cq=wcq, ck=wck, cv=wcv, co=wco, gate=wg, up=wu, down=wd)
+    slots = dict(q=wq, k=wk, v=wv, o=wo, cq=wcq, co=wco, gate=wg, up=wu, down=wd)
+    if not keys_given:
+        slots.update(ck=wck, cv=wcv)
     copies = weight_copies(weight, slots, sems)
-    begin(copies, ("ck", "cv", "q", "k", "v", "o", "cq", "co", "gate", "up", "down"))
+    if not keys_given:
+        begin(copies, ("ck", "cv"))
+    begin(copies, ("q", "k", "v", "o", "cq", "co", "gate", "up", "down"))
     own = same_head()
     own_low = low(own)
     stream = x_ref[...].astype(jnp.float32)
     normed = low(stream * scale_of(stream) * gains_ref[0:1])
     n1_ref[...] = normed
-    finish(copies, "ck")
-    for row in range(BATCHES):
-        part = pl.ds(STATES * row, STATES)
-        ck_ref[part] = low(product(enc_ref[part], square(wck)))
-    finish(copies, "cv")
-    for row in range(BATCHES):
-        part = pl.ds(STATES * row, STATES)
-        cv_ref[part] = low(product(enc_ref[part], square(wcv)))
+    if not keys_given:
+        for name, held_weight, target in (("ck", wck, ck_ref), ("cv", wcv, cv_ref)):
+            finish(copies, name)
+            for row in range(BATCHES):
+                part = pl.ds(STATES * row, STATES)
+                target[part] = low(product(enc_ref[part], square(held_weight)))
     finish(copies, "q")
     q_ref[...] = low(product(normed, square(wq)))
     finish(copies, "k")
@@ -285,6 +288,30 @@
 
     total = lax.fori_loop(0, FF // CHUNK, step, jnp.zeros((BATCHES * TOKENS, WIDE), jnp.float32))
     out_ref[...] = low(a3_ref[...] + total)
+
+
+def first_kernel(
+    x_ref, enc_ref, self_add_ref, cross_add_ref, gains_ref, weight, out_ref, ck_ref, cv_ref, *rest
+):
+    (n1, q, k, v, p, o, a2, n2, cq, cp, co, a3, n3, gate, up, hid, *scratch) = rest
+    forward_body(
+        False,
+        x_ref, enc_ref, self_add_ref, cross_add_ref, gains_ref, weight, out_ref,
+        n1, q, k, v, p, o, a2, n2, cq, ck_ref, cv_ref, cp, co, a3, n3, gate, up, hid, *scratch,
+    )
+
+
+def second_kernel(
+    x_ref, ck_ref, cv_ref, self_add_ref, cross_add_ref, gains_ref, weight, out_ref, *rest
+):
+    (n1, q, k, v, p, o, a2, n2, cq, cp, co, a3, n3, gate, up, hid, *scratch) = rest
+    (wq, wk, wv, wo, wcq, wco, wg, wu, wd, sems) = scratch
+    forward_body(
+        True,
+        x_ref, None, self_add_ref, cross_add_ref, gains_ref, weight, out_ref,
+        n1, q, k, v, p, o, a2, n2, cq, ck_ref, cv_ref, cp, co, a3, n3, gate, up, hid,
+        wq, wk, wv, wo, wcq, None, None, wco, wg, wu, wd, sems,
+    )
 
 
 def backward_kernel(
@@ -453,16 +480,20 @@
     begin(copies, ("ck", "cv"))
     slots = dict(q=gq, k=gk, v=gv, o=go, cq=gcq, ck=gck, cv=gcv, co=gco, gate=gg, up=gu, down=gd)
     outward = {
-        name: [pltpu.make_async_copy(slots[name], grads.at[:, :, pl.ds(WIDE * place, WIDE)], out_sems.at[place])]
+        name: [
+            pltpu.make_async_copy(
+                slots[name], grads.at[:, 0, :, pl.ds(WIDE * place, WIDE)], out_sems.at[place]
+            )
+        ]
         for place, name in enumerate(("q", "k", "v", "o", "cq", "ck", "cv", "co"))
     }
     for place, name in enumerate(("gate", "up")):
-        target = grads.at[:, :, pl.ds(ATT + FF * place, FF)]
+        target = grads.at[:, 1, :, pl.ds(FF * place, FF)]
         outward[name] = [pltpu.make_async_copy(slots[name], target, out_sems.at[8 + place])]
     outward["down"] = [
         pltpu.make_async_copy(
             rows_at(gd, piece, block),
-            down_at(grads, ATT + 2 * FF, piece, block),
+            down_at(grads, piece, block),
             out_sems.at[10 + place],
         )
         for place, (piece, block) in enumerate(DOWN_PIECES)
@@ -528,42 +559,56 @@
 params = pltpu.CompilerParams(vmem_limit_bytes=VMEM_BYTES)
 
 
-def run_forward(x, enc, self_add, cross_add, gains, weight):
-    wide = jnp.float32
-    outs = [
-        shape_of(ALL_TOKENS),
-        shape_of(ALL_TOKENS),
-        shape_of(ALL_TOKENS),
-        shape_of(ALL_TOKENS),
-        shape_of(ALL_TOKENS),
-        shape_of((BATCHES, WIDE, TOKENS), wide),
-        shape_of(ALL_TOKENS),
-        shape_of(ALL_TOKENS, wide),
-        shape_of(ALL_TOKENS),
-        shape_of(ALL_TOKENS),
-        shape_of(ALL_STATES),
-        shape_of(ALL_STATES),
-        shape_of((BATCHES, WIDE, STATES), wide),
-        shape_of(ALL_TOKENS),
-        shape_of(ALL_TOKENS, wide),
-        shape_of(ALL_TOKENS),
-        shape_of(HIDDEN, wide),
-        shape_of(HIDDEN, wide),
-        shape_of(HIDDEN),
-    ]
+SAVED = (
+    (ALL_TOKENS, jnp.bfloat16),
+    (ALL_TOKENS, jnp.bfloat16),
+    (ALL_TOKENS, jnp.bfloat16),
+    (ALL_TOKENS, jnp.bfloat16),
+    ((BATCHES, WIDE, TOKENS), jnp.float32),
+    (ALL_TOKENS, jnp.bfloat16),
+    (ALL_TOKENS, jnp.float32),
+    (ALL_TOKENS, jnp.bfloat16),
+    (ALL_TOKENS, jnp.bfloat16),
+    ((BATCHES, WIDE, STATES), jnp.float32),
+    (ALL_TOKENS, jnp.bfloat16),
+    (ALL_TOKENS, jnp.float32),
+    (ALL_TOKENS, jnp.bfloat16),
+    (HIDDEN, jnp.float32),
+    (HIDDEN, jnp.float32),
+    (HIDDEN, jnp.bfloat16),
+)
+
+
+def run_first(x, enc, self_add, cross_add, gains, weight):
+    outs = [shape_of(ALL_TOKENS), shape_of(ALL_STATES), shape_of(ALL_STATES)]
     return pl.pallas_call(
-        forward_kernel,
+        first_kernel,
         out_shape=outs,
         in_specs=in_vmem(5) + [pl.BlockSpec(memory_space=pl.ANY)],
         out_specs=in_vmem(len(outs)),
-        scratch_shapes=held(*[FULL] * 8, GATED, GATED, DOWN) + [pltpu.SemaphoreType.DMA((34,))],
+        scratch_shapes=[pltpu.VMEM(dims, kind) for dims, kind in SAVED]
+        + held(*[FULL] * 8, GATED, GATED, DOWN)
+        + [pltpu.SemaphoreType.DMA((34,))],
         compiler_params=params,
-        name="layer_forward",
+        name="first_forward",
     )(x, enc, self_add, cross_add, gains, weight)
 
 
+def run_second(x, ck, cv, self_add, cross_add, gains, weight):
+    outs = [shape_of(ALL_TOKENS)] + [shape_of(dims, kind) for dims, kind in SAVED]
+    return pl.pallas_call(
+        second_kernel,
+        out_shape=outs,
+        in_specs=in_vmem(6) + [pl.BlockSpec(memory_space=pl.ANY)],
+        out_specs=in_vmem(len(outs)),
+        scratch_shapes=held(*[FULL] * 6, GATED, GATED, DOWN) + [pltpu.SemaphoreType.DMA((34,))],
+        compiler_params=params,
+        name="second_forward",
+    )(x, ck, cv, self_add, cross_add, gains, weight)
+
+
 def run_backward(cotangent, x, gains, saved, weight):
-    (n1, q, k, v, p, o, a2, n2, cq, ck, cv, cp, co, a3, n3, gate, up, hid) = saved
+    (ck, cv, n1, q, k, v, p, o, a2, n2, cq, cp, co, a3, n3, gate, up, hid) = saved
     outs = [
         shape_of(ALL_TOKENS),
         shape_of(HIDDEN),
@@ -591,11 +636,11 @@
 
 
 def run_weights(cotangent, enc, saved, records, weight):
-    (n1, q, k, v, p, o, a2, n2, cq, ck, cv, cp, co, a3, n3, gate, up, hid) = saved
+    (ck, cv, n1, q, k, v, p, o, a2, n2, cq, cp, co, a3, n3, gate, up, hid) = saved
     (dgate, dup, dc, dcq, dck, dcv, dself, dq, dk, dv) = records
     return pl.pallas_call(
         weight_kernel,
-        out_shape=[shape_of((PARTS, ROWS_OWN, 2 * ATT)), shape_of(ALL_STATES)],
+        out_shape=[shape_of((PARTS, 2, ROWS_OWN, ATT)), shape_of(ALL_STATES)],
         in_specs=in_vmem(18) + [pl.BlockSpec(memory_space=pl.ANY)],
         out_specs=[pl.BlockSpec(memory_space=pl.ANY)] + in_vmem(1),
         scratch_shapes=held(FULL, FULL, *[FULL] * 8, GATED, GATED, DOWN)
@@ -607,32 +652,28 @@
     )
 
 
-def pack(query, kv, out, c_query, c_kv, c_out, w_in, w_ffn):
+def pack_attention(query, kv, out, c_query, c_kv, c_out):
     rows = query.shape[0]
+    return jnp.concatenate(
+        [query, kv.reshape(rows, -1), out, c_query, c_kv.reshape(rows, -1), c_out], axis=1
+    )
+
+
+def pack_hidden(w_in, w_ffn):
+    rows = w_in.shape[0]
     pieces = w_ffn.reshape(8, 16, GROUPS, GROUP).transpose(2, 1, 0, 3)
-    return jnp.concatenate(
-        [
-            query,
-            kv.reshape(rows, -1),
-            out,
-            c_query,
-            c_kv.reshape(rows, -1),
-            c_out,
-            w_in.reshape(rows, -1),
-            pieces.reshape(rows, FF),
-        ],
-        axis=1,
-    )
-
-
-def unpack(block):
-    rows = block.shape[0]
+    return jnp.concatenate([w_in.reshape(rows, -1), pieces.reshape(rows, FF)], axis=1)
+
+
+def unpack(attention, hidden):
+    rows = attention.shape[0]
     start = 0
     pieces = []
-    for width in (768, 1536, 768, 768, 1536, 768, 4096, 2048):
-        pieces.append(block[:, start : start + width])
+    for width in (768, 1536, 768, 768, 1536, 768):
+        pieces.append(attention[:, start : start + width])
         start += width
-    query, kv, out, c_query, c_kv, c_out, w_in, w_ffn = pieces
+    query, kv, out, c_query, c_kv, c_out = pieces
+    w_ffn = hidden[:, 2 * FF :].reshape(GROUPS, 16, 8, GROUP).transpose(2, 1, 0, 3)
     return (
         query,
         kv.reshape(rows, 2, WIDE),
@@ -640,8 +681,8 @@
         c_query,
         c_kv.reshape(rows, 2, WIDE),
         c_out,
-        w_in.reshape(rows, 2, FF),
-        w_ffn.reshape(GROUPS, 16, 8, GROUP).transpose(2, 1, 0, 3).reshape(FF // PARTS, WIDE),
+        hidden[:, : 2 * FF].reshape(rows, 2, FF),
+        w_ffn.reshape(FF // PARTS, WIDE),
     )
 
 
@@ -674,58 +715,113 @@
     ffn_in,
     ffn_out,
 ):
-    section_index = lax.axis_index("section")
+    core = lax.axis_index("section")
     part_index = lax.axis_index("fsdp")
-    own = pack(
-        self_query[0],
-        self_kv[0],
-        self_out[0],
-        cross_query[0],
-        cross_kv[0],
-        cross_out[0],
-        ffn_in[0],
-        ffn_out[0],
-    )
-    weight = lax.all_gather(own, "fsdp", axis=0, tiled=True).reshape(PARTS, ROWS_OWN, 2 * ATT)
+    plane = lax.axis_index("rep")
+    planes = lax.axis_size("rep")
+    layer = lax.rem(plane, 2)
+    first_core = core == 0
+    at_home = core == layer
+
+    def place(core_index, plane_index):
+        return core_index * planes + plane_index
+
+    def flip_core(value):
+        return lax.ppermute(value, "section", [(0, 1), (1, 0)])
+
+    def from_home(value):
+        pairs = [(place(p % 2, p), place(1 - p % 2, p)) for p in range(planes)]
+        return jnp.where(at_home, value, lax.ppermute(value, ("section", "rep"), pairs))
+
+    def beside(value):
+        return lax.ppermute(value, "rep", [(p, p ^ 1) for p in range(planes)])
+
+    def rows_for_layer(value):
+        pairs = [(place(p % 2, p), place(p % 2, p ^ 1)) for p in range(planes)]
+        return jnp.where(at_home, value, lax.ppermute(value, ("section", "rep"), pairs))
+
+    def rows_back(value):
+        pairs = [(place(1 - p % 2, p), place(p % 2, p ^ 1)) for p in range(planes)]
+        return jnp.where(at_home, value, lax.ppermute(value, ("section", "rep"), pairs))
+
+    def between_layers(value, steps):
+        pairs = [(p, p + steps) for p in range(planes) if p % 2 == (steps < 0)]
+        return lax.ppermute(value, "rep", pairs)
+
+    attention = pack_attention(
+        self_query[0], self_kv[0], self_out[0], cross_query[0], cross_kv[0], cross_out[0]
+    )
+    hidden = pack_hidden(ffn_in[0], ffn_out[0])
+    kept = jnp.where(first_core, attention, hidden)
+    given_away = jnp.where(first_core, hidden, attention)
+    half = jnp.where(at_home, kept, flip_core(given_away))
+    weight = lax.all_gather(half, ("fsdp", "section"), axis=0, tiled=True)
+    weight = weight.reshape(PARTS, 2, ROWS_OWN, ATT)
     small = jnp.zeros((8, 128), jnp.bfloat16)
     small = small.at[:3, :ROWS_OWN].set(norm_gains[0])
     small = small.at[3:5, :HEADS].set(rel_bias[0])
-    small = lax.all_gather(small, "fsdp", axis=0, tiled=False)
+    small = lax.all_gather(from_home(small), "fsdp", axis=0, tiled=False)
     gains = small[:, :3, :ROWS_OWN].transpose(1, 0, 2).reshape(3, WIDE).astype(jnp.float32)
     table = small[:, 3:5, :HEADS].reshape(BUCKETS, HEADS)
-    self_add, cross_add = score_terms(table, dec_segments[:, 0], enc_segments[:, 0])
-    rows_in = layer_in[:, 0].reshape(ALL_TOKENS)
-    given = cotangent[:, 0].reshape(ALL_TOKENS)
-    enc = encoder[:, 0].reshape(ALL_STATES)
-    first = run_forward(rows_in, enc, self_add, cross_add, gains, weight)[0]
-    received = lax.ppermute(first, "section", [(0, 1)])
-    current = jnp.where(section_index == 0, rows_in, received)
-    result, *saved = run_forward(current, enc, self_add, cross_add, gains, weight)
+    ids = jnp.concatenate([dec_segments[:, 0], enc_segments[:, 0]], axis=1)
+    ids = rows_for_layer(ids)
+    self_add, cross_add = score_terms(table, ids[:, :TOKENS], ids[:, TOKENS:])
+    ends = jnp.stack([layer_in[:, 0].reshape(ALL_TOKENS), cotangent[:, 0].reshape(ALL_TOKENS)])
+    ends = rows_for_layer(ends)
+    rows_in, given = ends[0], ends[1]
+    enc = rows_for_layer(encoder[:, 0].reshape(ALL_STATES))
+    weight, rows_in, given, enc, self_add, cross_add, gains = lax.optimization_barrier(
+        (weight, rows_in, given, enc, self_add, cross_add, gains)
+    )
+    first, ck, cv = run_first(rows_in, enc, self_add, cross_add, gains, weight)
+    current = jnp.where(layer == 0, rows_in, between_layers(first, 1))
+    result, *saved = run_second(current, ck, cv, self_add, cross_add, gains, weight)
+    saved = [ck, cv] + saved
     grad_first = run_backward(given, current, gains, saved, weight)[0]
-    returned = lax.ppermute(grad_first, "section", [(1, 0)])
-    incoming = jnp.where(section_index == 1, given, returned)
+    incoming = jnp.where(layer == 1, given, between_layers(grad_first, -1))
     grad_input, *records, grad_gains, grad_scores = run_backward(
         incoming, current, gains, saved, weight
     )
     grads, grad_enc = run_weights(incoming, enc, saved, records, weight)
-    owned = lax.psum_scatter(
-        grads.reshape(WIDE, 2 * ATT), "fsdp", scatter_dimension=0, tiled=True
-    )
-    other_enc = lax.ppermute(grad_enc, "section", [(0, 1), (1, 0)])
-    encoder_total = grad_enc.astype(jnp.float32) + other_enc.astype(jnp.float32)
+    partial = lax.psum_scatter(
+        grads.reshape(2 * WIDE, ATT), ("fsdp", "section"), scatter_dimension=0, tiled=True
+    )
+    outs = rows_back(jnp.stack([result, grad_input]))
+    encoder_total = grad_enc.astype(jnp.float32) + beside(grad_enc).astype(jnp.float32)
+    encoder_total = from_home(encoder_total)
     diagonal_sums = gather_distance(grad_scores.reshape(HEADS, TOKENS, TOKENS))
     grad_table = jnp.dot(bucket_onehot(TOKENS), diagonal_sums.T, precision=highest)
     little = jnp.zeros((8, WIDE), jnp.float32)
     little = little.at[:3].set(grad_gains)
     little = little.at[3, : BUCKETS * HEADS].set(grad_table.reshape(-1))
-    little = lax.psum(little, ("fsdp", "rep"))
+    for axis, bits in (("section", (1,)), ("fsdp", (1, 2, 4, 8)), ("rep", (2,))):
+        for bit in bits:
+            pairs = [(index, index ^ bit) for index in range(lax.axis_size(axis))]
+            little = little + lax.ppermute(little, axis, pairs)
+    little = jnp.where(at_home, little, beside(little))
     own_gains = lax.dynamic_slice(little, (0, part_index * ROWS_OWN), (3, ROWS_OWN))
     own_table = lax.dynamic_slice(little, (3, part_index * 2 * HEADS), (1, 2 * HEADS))
-    quarters = owned.reshape(ROWS_OWN, 4, 2 * ATT // 4)
-    quarters = lax.all_to_all(quarters, "rep", split_axis=1, concat_axis=1, tiled=True)
-    quarter = low(jnp.sum(quarters.astype(jnp.float32), axis=1))
-    summed = lax.all_gather(quarter, "rep", axis=1, tiled=True).astype(jnp.float32)
-    query, kv, out, c_query, c_kv, c_out, w_in, w_ffn = unpack(summed)
+    partial, own_gains, own_table, encoder_total, outs = lax.optimization_barrier(
+        (partial, own_gains, own_table, encoder_total, outs)
+    )
+    up = [(p, (p + 1) % planes) for p in range(planes)]
+    down = [(p, (p - 1) % planes) for p in range(planes)]
+    above = lax.ppermute(partial, "rep", down).astype(jnp.float32)
+    below = lax.ppermute(partial, "rep", up).astype(jnp.float32)
+    other_layer = low(above + below)
+    cut = ATT // 2
+    own_layer = jnp.concatenate(
+        [
+            lax.ppermute(other_layer[:, :cut], "rep", down),
+            lax.ppermute(other_layer[:, cut:], "rep", up),
+        ],
+        axis=1,
+    )
+    mine = jnp.where(at_home, own_layer, other_layer)
+    theirs = flip_core(jnp.where(at_home, other_layer, own_layer))
+    attention = jnp.where(first_core, mine, theirs).astype(jnp.float32)
+    hidden = jnp.where(first_core, theirs, mine).astype(jnp.float32)
+    query, kv, out, c_query, c_kv, c_out, w_in, w_ffn = unpack(attention, hidden)
     ordered = (
         own_gains,
         query,
@@ -739,8 +835,8 @@
         w_ffn,
     )
     return (
-        result.reshape(1, BATCHES, 1, TOKENS, WIDE),
-        grad_input.reshape(1, BATCHES, 1, TOKENS, WIDE),
+        outs[0].reshape(1, BATCHES, 1, TOKENS, WIDE),
+        outs[1].reshape(1, BATCHES, 1, TOKENS, WIDE),
         encoder_total.reshape(BATCHES, 1, STATES, WIDE),
     ) + tuple(member[None] for member in ordered)
 

time: 742 us -> 373 us (0.50)
  the two profiles are of different devices: /device:TPU:0 before, /device:TPU:1 now
where the time goes in v3:
time: 373 us; the launch traced here: 366 us
  waiting for transfers between devices  170 us (46%)
  Pallas kernels  83.9 us (22%)
  starting transfers between devices  43.8 us (12%)
  blocking collectives  20.7 us (6%)
  local copies, waits for them, and re-layouts  18.6 us (5%)
  between operations  15.2 us (4%)
  other arithmetic  12.6 us (3%)
    reduce_scatter x1, waiting for transfers between devices, shards(): lax.psum_scatter(grads.reshape(2 * WIDE, ATT), ('fsdp', 'section'), scatt...  58.6 us
    all_gather x1, waiting for transfers between devices, shards(): weight = lax.all_gather(half, ('fsdp', 'section'), axis=0, tiled=True)  46.9 us
    pallas_call x2, Pallas kernels, run_backward(): pl.pallas_call(backward_kernel, out_shape=outs, in_specs=in_vmem(15) + [p...  42.6 us
    all_gather x1, blocking collectives, shards(): small = lax.all_gather(from_home(small), 'fsdp', axis=0, tiled=False)  20.7 us
    ppermute x2, waiting for transfers between devices, beside(): return lax.ppermute(value, 'rep', [(p, p ^ 1) for p in range(planes)])  17 us
    pallas_call x1, Pallas kernels, run_weights(): pl.pallas_call(weight_kernel, out_shape=[shape_of((PARTS, 2, ROWS_OWN, AT...  15.4 us
    ppermute x6, starting transfers between devices, shards(): little = little + lax.ppermute(little, axis, pairs)  13.5 us
    pallas_call x1, Pallas kernels, run_second(): pl.pallas_call(second_kernel, out_shape=outs, in_specs=in_vmem(6) + [pl.B...  13.3 us
  transfers between devices with their start and end apart: 24, of which 18 were waited for; matrix products, arithmetic and copies ran while one was open for 4% of the time, Pallas kernels for 0%

profile of v3, /device:TPU:1, one launch (start us, length us, event | category | flops | bytes accessed | tf_op | source)
XLA Modules:
  0.0 365.7 jit_solution(10033693003964185048)
XLA Ops:
  7.2 0.9 bitcast_dynamic-update-slice_fusion.3
  8.2 0.9 copy.56
  9.1 0.9 copy.57
  10.0 1.2 copy.58
  12.1 0.9 broadcast_select_fusion.2
  13.0 1.5 collective-permute-start
  14.5 1.8 collective-permute-done
  16.4 1.0 select_select_fusion
  17.5 1.3 collective-permute-start.3
  19.1 1.3 collective-permute-start.4
  20.5 1.3 collective-permute-start.1
  21.8 1.3 collective-permute-start.2
  23.7 20.7 %all-gather = bf16[128,128]{1,0:T(8,128)(2,1)S(1)} all-gather(bf16[8,128]{1,0:T(8,128)(2,1)S(1)} %broadcast_select_fusion.11), channel_id=2, replica_groups=mesh['section'=2,'fsdp'=16,'rep'=4] {'fsdp'}, dimensions={0}, use_global_device_ids=true | all-gather | bytes 34816 | tf_op jit(solution)/shard_map/all_gather | solution.py:763
  46.4 0.9 bitcast_select_fusion.self_add_ref
  47.3 0.7 compare_select_fusion.cross_add_ref
  48.1 1.0 broadcast_select_fusion.6
  49.1 0.8 slice_bitcast_fusion
  49.9 1.0 broadcast_select_fusion.1.enc_ref
  50.9 46.9 %all-gather.3.cloned.1.call-done = bf16[1536,6144]{1,0:T(8,128)(2,1)} async-done(((bf16[48,6144]{1,0:T(8,128)(2,1)}), bf16[1536,6144]{1,0:T(8,128)(2,1)}) %all-gather.3.cloned.1.call-update) | async-done | bytes 18874384 | tf_op jit(solution)/shard_map/all_gather | solution.py:758
  97.8 12.6 %first_forward.1 = (bf16[128,768]{1,0:T(8,128)(2,1)}, bf16[512,768]{1,0:T(8,128)(2,1)}, bf16[512,768]{1,0:T(8,128)(2,1)}) custom-call(bf16[128,768]{1,0:T(8,128)(2,1)} %get-tuple-element.110.x_ref, bf16[512,768]{1,0:T(8,128)(2,1)} %broadcast_select_fusion.1.enc_ref, f32[2,768,64]{2,1,0:T(8,128)} %bitcast_select_fusion.self_add_ref, ...), custom_call_target="tpu_custom_call" | custom-call | tf_op jit(solution)/shard_map/first_forward/pallas_call | solution.py:584
  110.5 3.3 collective-permute-start.5
  113.8 4.2 %collective-permute-done.5 = bf16[128,768]{1,0:T(8,128)(2,1)S(1)} collective-permute-done((bf16[128,768]{1,0:T(8,128)(2,1)}, bf16[128,768]{1,0:T(8,128)(2,1)S(1)}, u32[]{:S(2)}, u32[]{:S(2)}) %collective-permute-start.5) | collective-permute-done | bytes 196640 | tf_op jit(solution)/shard_map/ppermute | solution.py:749
  117.9 0.7 broadcast_select_fusion.7.x_ref
  118.6 13.3 %second_forward.1 = (bf16[128,768]{1,0:T(8,128)(2,1)}, bf16[128,768]{1,0:T(8,128)(2,1)}, bf16[128,768]{1,0:T(8,128)(2,1)}, bf16[128,768]{1,0:T(8,128)(2,1)}, bf1...) custom-call(bf16[128,768]{1,0:T(8,128)(2,1)} %broadcast_select_fusio, ...), custom_call_target="tpu_custom_call" | custom-call | tf_op jit(solution)/shard_map/second_forward/pallas_call | solution.py:599
  131.9 21.2 %layer_backward.2 = (bf16[128,768]{1,0:T(8,128)(2,1)}, bf16[128,2048]{1,0:T(8,128)(2,1)}, bf16[128,2048]{1,0:T(8,128)(2,1)}, bf16[128,768]{1,0:T(8,128)(2,1)}, b...) custom-call(bf16[128,768]{1,0:T(8,128)(2,1)} %get-tuple-element.109., ...), custom_call_target="tpu_custom_call" | custom-call | tf_op jit(solution)/shard_map/layer_backward/pallas_call | solution.py:627
  153.2 1.3 collective-permute-start.6
  154.5 6.2 %collective-permute-done.6 = bf16[128,768]{1,0:T(8,128)(2,1)S(1)} collective-permute-done((bf16[128,768]{1,0:T(8,128)(2,1)}, bf16[128,768]{1,0:T(8,128)(2,1)S(1)}, u32[]{:S(2)}, u32[]{:S(2)}) %collective-permute-start.6) | collective-permute-done | bytes 196640 | tf_op jit(solution)/shard_map/ppermute | solution.py:749
  160.6 0.7 broadcast_select_fusion.8.c_ref
  161.3 21.4 %layer_backward.3 = (bf16[128,768]{1,0:T(8,128)(2,1)}, bf16[128,2048]{1,0:T(8,128)(2,1)}, bf16[128,2048]{1,0:T(8,128)(2,1)}, bf16[128,768]{1,0:T(8,128)(2,1)}, b...) custom-call(bf16[128,768]{1,0:T(8,128)(2,1)} %broadcast_select_fusio, ...), custom_call_target="tpu_custom_call" | custom-call | tf_op jit(solution)/shard_map/layer_backward/pallas_call | solution.py:627
  182.7 15.4 %weight_gradients.1 = (bf16[16,2,48,6144]{3,2,1,0:T(8,128)(2,1)}, bf16[512,768]{1,0:T(8,128)(2,1)}) custom-call(bf16[128,768]{1,0:T(8,128)(2,1)} %broadcast_select_fusion.8.c_ref, bf16[512,768]{1,0:T(8,128)(2,1)} %broadcast_select_fusion.1.enc_ref, bf16[128,768]{1,0:T(8,128)(2,1)} %get-tuple-element.130.n1_ref, bf16[128,768]{1,0:T(8,128)(2,1)} %get-tuple-element.131.o_ref, ...), custom_call_target="tpu_custom_call" | custom-call | tf_op jit(solution)/shard_map/weight_gradients/pallas_call | solution.py:641
  198.1 1.1 copy-done
  199.5 17.0 %collective-permute-done.14 = bf16[512,768]{1,0:T(8,128)(2,1)S(1)} collective-permute-done((bf16[512,768]{1,0:T(8,128)(2,1)S(1)}, bf16[512,768]{1,0:T(8,128)(2,1)S(1)}, u32[]{:S(2)}, u32[]{:S(2)}) %collective-permute-start.14) | collective-permute-done | bytes 786464 | tf_op jit(solution)/shard_map/ppermute | solution.py:737
  216.5 1.3 convert_add_fusion
  217.8 1.3 collective-permute-start.15
  219.7 0.7 reshape.209
  221.2 4.1 %collective-permute-start.7 = (f32[8,768]{1,0:T(8,128)S(1)}, f32[8,768]{1,0:T(8,128)S(1)}, u32[]{:S(2)}, u32[]{:S(2)}) collective-permute-start(f32[8,768]{1,0:T(8,128)S(1)} %scatter.19), channel_id=1, source_target_pairs={{0,64},{64,0},{1,65},{65,1},{2,66},{66,2},{3,67},{67,3},{4,68},{68... | collective-permute-start | bytes 73736 | tf_op jit(solution)/shard_map/ppermute | solution.py:800
  225.3 0.8 collective-permute-done.7
  226.8 2.1 collective-permute-done.8
  228.9 2.3 collective-permute-start.9
  231.1 1.9 collective-permute-done.9
  233.0 1.3 collective-permute-start.10
  234.3 1.4 collective-permute-done.10
  235.7 2.7 collective-permute-start.11
  238.4 1.5 collective-permute-done.11
  239.9 2.5 collective-permute-start.12
  242.4 2.0 collective-permute-done.12
  244.4 0.9 collective-permute-start.13
  245.3 8.5 %collective-permute-start.16 = (bf16[2,128,768]{2,1,0:T(8,128)(2,1)S(1)}, bf16[2,128,768]{2,1,0:T(8,128)(2,1)S(1)}, u32[]{:S(2)}, u32[]{:S(2)}) collective-permute-start(bf16[2,128,768]{2,1,0:T(8,128)(2,1)S(1)} %pad_maximum_fusion.1), channel_id=1, source_target_pairs={{64,1},{1,64},{66,3},{3,66},{68,5},{5,68},{70,7},{7,70},{72,9},{9,... | collective-permute-start | bytes 1179656 | tf_op jit(solution)/shard_map/ppermute | solution.py:745
  254.0 5.7 %collective-permute-done.16 = bf16[2,128,768]{2,1,0:T(8,128)(2,1)S(1)} collective-permute-done((bf16[2,128,768]{2,1,0:T(8,128)(2,1)S(1)}, bf16[2,128,768]{2,1,0:T(8,128)(2,1)S(1)}, u32[]{:S(2)}, u32[]{:S(2)}) %collective-permute-start.16) | collective-permute-done | bytes 393248 | tf_op jit(solution)/shard_map/ppermute | solution.py:745
  259.7 2.8 broadcast_select_fusion
  262.5 58.6 %reduce-scatter.2.cloned.1.call-done = bf16[48,6144]{1,0:T(8,128)(2,1)} async-done(((bf16[1536,6144]{1,0:T(8,128)(2,1)}), bf16[48,6144]{1,0:T(8,128)(2,1)}) %reduce-scatter.2.cloned.1.call-update) | async-done | bytes 589840 | tf_op jit(solution)/shard_map/reduce_scatter | solution.py:786
  321.0 2.5 collective-permute-start.17
  323.6 11.2 %collective-permute-done.17 = bf16[48,6144]{1,0:T(8,128)(2,1)S(1)} collective-permute-done((bf16[48,6144]{1,0:T(8,128)(2,1)}, bf16[48,6144]{1,0:T(8,128)(2,1)S(1)}, u32[]{:S(2)}, u32[]{:S(2)}) %collective-permute-start.17) | collective-permute-done | bytes 589856 | tf_op jit(solution)/shard_map/ppermute | solution.py:809
  334.8 3.0 collective-permute-done.18
  338.4 1.2 collective-permute-start.20
  339.5 4.1 %collective-permute-done.19 = bf16[48,3072]{1,0:T(8,128)(2,1)S(1)} collective-permute-done((bf16[48,3072]{1,0:T(8,128)(2,1)S(1)}, bf16[48,3072]{1,0:T(8,128)(2,1)S(1)}, u32[]{:S(2)}, u32[]{:S(2)}) %collective-permute-start.19) | collective-permute-done | bytes 294944 | tf_op jit(solution)/shard_map/ppermute | solution.py:815
  343.7 1.5 collective-permute-done.20
  345.2 4.1 %collective-permute-start.21 = (bf16[48,6144]{1,0:T(8,128)(2,1)S(1)}, bf16[48,6144]{1,0:T(8,128)(2,1)S(1)}, u32[]{:S(2)}, u32[]{:S(2)}) collective-permute-start(bf16[48,6144]{1,0:T(8,128)(2,1)S(1)} %broadcast_select_fusion.3), channel_id=1, source_target_pairs={{0,64},{64,0},{1,65},{65,1},{2,66},{66,2},{3,67},{67,3},{4,68},{68... | collective-permute-start | bytes 1769480 | tf_op jit(solution)/shard_map/ppermute | solution.py:730
  351.8 0.8 fusion.4
  352.8 0.8 slice_bitcast_fusion.2
  354.1 1.0 broadcast_in_dim_reshape.19
  355.1 1.5 broadcast_in_dim_reshape.18
  356.6 0.9 broadcast_in_dim_reshape.15
  357.5 0.9 broadcast_in_dim_reshape.17
  (122 shorter events, 9.9 us)
Async XLA Ops:
  7.2 4.1 %copy-start.9 = (bf16[1,128,768]{2,1,0:T(8,128)(2,1)S(1)}, bf16[1,128,768]{2,1,0:T(8,128)(2,1)}, u32[]{:S(2)}) copy-start(bf16[1,128,768]{2,1,0:T(8,128)(2,1)} %param.39) | copy-start | bytes 589828
  7.2 90.6 %all-gather.3.cloned.1.call-start = ((), (), s32[]{:S(2)}) async-start(), calls=%async_computation.1 | async-start | bytes 19464192 | tf_op jit(solution)/shard_map/all_gather | solution.py:758
  10.0 1.6 copy-start.10
  10.0 1.6 copy-start.11
  11.2 0.9 copy-start.12
  13.0 4.4 %copy-start.17 = (s32[2,1,256]{2,1,0:T(1,128)S(1)}, s32[2,1,256]{2,1,0:T(1,128)}, u32[]{:S(2)}) copy-start(s32[2,1,256]{2,1,0:T(1,128)} %param.29) | copy-start | bytes 6148
  13.0 4.4 %copy-start.15 = (s32[2,1,64]{2,1,0:T(1,128)S(1)}, s32[2,1,64]{2,1,0:T(1,128)}, u32[]{:S(2)}) copy-start(s32[2,1,64]{2,1,0:T(1,128)} %param.28) | copy-start | bytes 1540
  13.0 5.8 %copy-start.18 = (bf16[1,3,48]{2,1,0:T(4,128)(2,1)S(1)}, bf16[1,3,48]{2,1,0:T(4,128)(2,1)}, u32[]{:S(2)}) copy-start(bf16[1,3,48]{2,1,0:T(4,128)(2,1)} %param.30) | copy-start | bytes 868
  13.0 5.8 %copy-start.19 = (bf16[1,2,12]{2,1,0:T(2,128)(2,1)S(1)}, bf16[1,2,12]{2,1,0:T(2,128)(2,1)}, u32[]{:S(2)}) copy-start(bf16[1,2,12]{2,1,0:T(2,128)(2,1)} %param.34) | copy-start | bytes 148
  13.0 7.4 %copy-start.4 = (bf16[2,1,64,768]{3,2,1,0:T(8,128)(2,1)S(1)}, bf16[2,1,64,768]{3,2,1,0:T(8,128)(2,1)}, u32[]{:S(2)}) copy-start(bf16[2,1,64,768]{3,2,1,0:T(8,128)(2,1)} %param.26) | copy-start | bytes 589828
  13.0 7.4 %copy-start.5 = (bf16[2,1,64,768]{3,2,1,0:T(8,128)(2,1)S(1)}, bf16[2,1,64,768]{3,2,1,0:T(8,128)(2,1)}, u32[]{:S(2)}) copy-start(bf16[2,1,64,768]{3,2,1,0:T(8,128)(2,1)} %param.25) | copy-start | bytes 589828
  13.0 3.3 collective-permute-start
  14.5 7.3 %copy-start.3 = (bf16[2,1,256,768]{3,2,1,0:T(8,128)(2,1)S(1)}, bf16[2,1,256,768]{3,2,1,0:T(8,128)(2,1)}, u32[]{:S(2)}) copy-start(bf16[2,1,256,768]{3,2,1,0:T(8,128)(2,1)} %param.27) | copy-start | bytes 2359300
  14.5 30.0 %copy-start.13 = (f32[32,64]{1,0:T(8,128)S(1)}, f32[32,64]{1,0:T(8,128)}, u32[]{:S(2)}) copy-start(f32[32,64]{1,0:T(8,128)} %constant.142.clone) | copy-start | bytes 24580
  17.4 303.7 %reduce-scatter.2.cloned.1.call-start = ((), (), s32[]{:S(2)}) async-start(), calls=%async_computation.2 | async-start | bytes 19464192 | tf_op jit(solution)/shard_map/reduce_scatter | solution.py:786
  17.5 28.6 %collective-permute-start.3 = (s32[2,320]{1,0:T(2,128)S(1)}, s32[2,320]{1,0:T(2,128)S(1)}, u32[]{:S(2)}, u32[]{:S(2)}) collective-permute-start(s32[2,320]{1,0:T(2,128)S(1)} %pad_add_fusion), channel_id=1, source_target_pairs={{0,1},{65,64},{2,3},{67,66},{4,5},{69,68},{6,7},{71,70},{8,9},{73,... | collective-permute-start | bytes 7688 | tf_op jit(solution)/shard_map/ppermute | solution.py:741
  19.1 4.6 %collective-permute-start.4 = (bf16[8,128]{1,0:T(8,128)(2,1)S(1)}, bf16[8,128]{1,0:T(8,128)(2,1)S(1)}, u32[]{:S(2)}, u32[]{:S(2)}) collective-permute-start(bf16[8,128]{1,0:T(8,128)(2,1)S(1)} %scatter.15), channel_id=1, source_target_pairs={{0,64},{65,1},{2,66},{67,3},{4,68},{69,5},{6,70},{71,7},{8,72},{73... | collective-permute-start | bytes 6152 | tf_op jit(solution)/shard_map/ppermute | solution.py:734
  20.5 27.6 %collective-permute-start.1 = (bf16[2,128,768]{2,1,0:T(8,128)(2,1)S(1)}, bf16[2,128,768]{2,1,0:T(8,128)(2,1)}, u32[]{:S(2)}, u32[]{:S(2)}) collective-permute-start(bf16[2,128,768]{2,1,0:T(8,128)(2,1)S(1)} %pad_maximum_fusion), channel_id=1, source_target_pairs={{0,1},{65,64},{2,3},{67,66},{4,5},{69,68},{6,7},{71,70},{8,9},{73,... | collective-permute-start | bytes 1179656 | tf_op jit(solution)/shard_map/ppermute | solution.py:741
  21.8 28.1 %collective-permute-start.2 = (bf16[512,768]{1,0:T(8,128)(2,1)S(1)}, bf16[512,768]{1,0:T(8,128)(2,1)S(1)}, u32[]{:S(2)}, u32[]{:S(2)}) collective-permute-start(bf16[512,768]{1,0:T(8,128)(2,1)S(1)} %bitcast.98), channel_id=1, source_target_pairs={{0,1},{65,64},{2,3},{67,66},{4,5},{69,68},{6,7},{71,70},{8,9},{73,... | collective-permute-start | bytes 2359304 | tf_op jit(solution)/shard_map/ppermute | solution.py:741
  45.1 1.0 copy-start.16
  97.8 20.1 %copy-start.2 = (bf16[128,768]{1,0:T(8,128)(2,1)S(1)}, bf16[128,768]{1,0:T(8,128)(2,1)}, u32[]{:S(2)}) copy-start(bf16[128,768]{1,0:T(8,128)(2,1)} %get-tuple-element.110.x_ref) | copy-start | bytes 589828
  110.5 7.5 %collective-permute-start.5 = (bf16[128,768]{1,0:T(8,128)(2,1)}, bf16[128,768]{1,0:T(8,128)(2,1)S(1)}, u32[]{:S(2)}, u32[]{:S(2)}) collective-permute-start(bf16[128,768]{1,0:T(8,128)(2,1)} %get-tuple-element.116), channel_id=1, source_target_pairs={{0,1},{2,3},{4,5},{6,7},{8,9},{10,11},{12,13},{14,15},{16,17},{18,... | collective-permute-start | bytes 589832 | tf_op jit(solution)/shard_map/ppermute | solution.py:749
  131.9 28.7 %copy-start.1 = (bf16[128,768]{1,0:T(8,128)(2,1)S(1)}, bf16[128,768]{1,0:T(8,128)(2,1)}, u32[]{:S(2)}) copy-start(bf16[128,768]{1,0:T(8,128)(2,1)} %get-tuple-element.109.c_ref) | copy-start | bytes 589828
  153.2 7.5 %collective-permute-start.6 = (bf16[128,768]{1,0:T(8,128)(2,1)}, bf16[128,768]{1,0:T(8,128)(2,1)S(1)}, u32[]{:S(2)}, u32[]{:S(2)}) collective-permute-start(bf16[128,768]{1,0:T(8,128)(2,1)} %get-tuple-element.129), channel_id=1, source_target_pairs={{1,0},{3,2},{5,4},{7,6},{9,8},{11,10},{13,12},{15,14},{17,16},{19,... | collective-permute-start | bytes 589832 | tf_op jit(solution)/shard_map/ppermute | solution.py:749
  198.1 1.1 copy-start
  199.2 19.9 %copy-start.8 = (f32[768,64]{1,0:T(8,128)S(1)}, f32[768,64]{1,0:T(8,128)}, u32[]{:S(2)}) copy-start(f32[768,64]{1,0:T(8,128)} %get-tuple-element.148) | copy-start | bytes 589828
  199.2 17.3 %collective-permute-start.14 = (bf16[512,768]{1,0:T(8,128)(2,1)S(1)}, bf16[512,768]{1,0:T(8,128)(2,1)S(1)}, u32[]{:S(2)}, u32[]{:S(2)}) collective-permute-start(bf16[512,768]{1,0:T(8,128)(2,1)S(1)} %copy-done), channel_id=1, source_target_pairs={{0,1},{1,0},{2,3},{3,2},{4,5},{5,4},{6,7},{7,6},{8,9},{9,8},{10,11... | collective-permute-start | bytes 2359304 | tf_op jit(solution)/shard_map/ppermute | solution.py:737
  217.8 41.9 %collective-permute-start.15 = (f32[512,768]{1,0:T(8,128)}, f32[512,768]{1,0:T(8,128)}, u32[]{:S(2)}, u32[]{:S(2)}) collective-permute-start(f32[512,768]{1,0:T(8,128)} %convert_add_fusion), channel_id=1, source_target_pairs={{0,64},{65,1},{2,66},{67,3},{4,68},{69,5},{6,70},{71,7},{8,72},{73... | collective-permute-start | bytes 4718600 | tf_op jit(solution)/shard_map/ppermute | solution.py:734
  219.3 1.5 copy-start.14
  219.4 25.8 %copy-start.6 = (bf16[128,768]{1,0:T(8,128)(2,1)S(1)}, bf16[128,768]{1,0:T(8,128)(2,1)}, u32[]{:S(2)}) copy-start(bf16[128,768]{1,0:T(8,128)(2,1)} %get-tuple-element.150) | copy-start | bytes 589828
  219.4 25.8 %copy-start.7 = (bf16[128,768]{1,0:T(8,128)(2,1)S(1)}, bf16[128,768]{1,0:T(8,128)(2,1)}, u32[]{:S(2)}) copy-start(bf16[128,768]{1,0:T(8,128)(2,1)} %get-tuple-element.151) | copy-start | bytes 589828
  221.2 5.0 %collective-permute-start.7 = (f32[8,768]{1,0:T(8,128)S(1)}, f32[8,768]{1,0:T(8,128)S(1)}, u32[]{:S(2)}, u32[]{:S(2)}) collective-permute-start(f32[8,768]{1,0:T(8,128)S(1)} %scatter.19), channel_id=1, source_target_pairs={{0,64},{64,0},{1,65},{65,1},{2,66},{66,2},{3,67},{67,3},{4,68},{68... | collective-permute-start | bytes 73736 | tf_op jit(solution)/shard_map/ppermute | solution.py:800
  226.2 2.7 collective-permute-start.8
  228.9 4.2 %collective-permute-start.9 = (f32[8,768]{1,0:T(8,128)S(1)}, f32[8,768]{1,0:T(8,128)S(1)}, u32[]{:S(2)}, u32[]{:S(2)}) collective-permute-start(f32[8,768]{1,0:T(8,128)S(1)} %add.51), channel_id=1, source_target_pairs={{0,8},{4,12},{8,0},{12,4},{16,24},{20,28},{24,16},{28,20},{32,40},... | collective-permute-start | bytes 73736 | tf_op jit(solution)/shard_map/ppermute | solution.py:800
  233.0 2.7 collective-permute-start.10
  235.7 4.2 %collective-permute-start.11 = (f32[8,768]{1,0:T(8,128)S(1)}, f32[8,768]{1,0:T(8,128)S(1)}, u32[]{:S(2)}, u32[]{:S(2)}) collective-permute-start(f32[8,768]{1,0:T(8,128)S(1)} %add.53), channel_id=1, source_target_pairs={{0,32},{4,36},{8,40},{12,44},{16,48},{20,52},{24,56},{28,60},{32,0... | collective-permute-start | bytes 73736 | tf_op jit(solution)/shard_map/ppermute | solution.py:800
  239.9 4.5 %collective-permute-start.12 = (f32[8,768]{1,0:T(8,128)S(1)}, f32[8,768]{1,0:T(8,128)S(1)}, u32[]{:S(2)}, u32[]{:S(2)}) collective-permute-start(f32[8,768]{1,0:T(8,128)S(1)} %add.54), channel_id=1, source_target_pairs={{0,2},{1,3},{2,0},{3,1},{4,6},{5,7},{6,4},{7,5},{8,10},{9,11},{10,... | collective-permute-start | bytes 73736 | tf_op jit(solution)/shard_map/ppermute | solution.py:800
  244.4 9.4 %collective-permute-start.13 = (f32[8,768]{1,0:T(8,128)S(1)}, f32[8,768]{1,0:T(8,128)S(1)}, u32[]{:S(2)}, u32[]{:S(2)}) collective-permute-start(f32[8,768]{1,0:T(8,128)S(1)} %add.55), channel_id=1, source_target_pairs={{0,1},{1,0},{2,3},{3,2},{4,5},{5,4},{6,7},{7,6},{8,9},{9,8},{10,11... | collective-permute-start | bytes 73736 | tf_op jit(solution)/shard_map/ppermute | solution.py:737
  245.3 14.3 %collective-permute-start.16 = (bf16[2,128,768]{2,1,0:T(8,128)(2,1)S(1)}, bf16[2,128,768]{2,1,0:T(8,128)(2,1)S(1)}, u32[]{:S(2)}, u32[]{:S(2)}) collective-permute-start(bf16[2,128,768]{2,1,0:T(8,128)(2,1)S(1)} %pad_maximum_fusion.1), channel_id=1, source_target_pairs={{64,1},{1,64},{66,3},{3,66},{68,5},{5,68},{70,7},{7,70},{72,9},{9,... | collective-permute-start | bytes 1179656 | tf_op jit(solution)/shard_map/ppermute | solution.py:745
  321.0 13.7 %collective-permute-start.17 = (bf16[48,6144]{1,0:T(8,128)(2,1)}, bf16[48,6144]{1,0:T(8,128)(2,1)S(1)}, u32[]{:S(2)}, u32[]{:S(2)}) collective-permute-start(bf16[48,6144]{1,0:T(8,128)(2,1)} %reduce-scatter.2.cloned.1.call-done), channel_id=1, source_target_pairs={{0,3},{1,0},{2,1},{3,2},{4,7},{5,4},{6,5},{7,6},{8,11},{9,8},{10,9... | collective-permute-start | bytes 1769480 | tf_op jit(solution)/shard_map/ppermute | solution.py:809
  323.6 14.3 %collective-permute-start.18 = (bf16[48,6144]{1,0:T(8,128)(2,1)}, bf16[48,6144]{1,0:T(8,128)(2,1)S(1)}, u32[]{:S(2)}, u32[]{:S(2)}) collective-permute-start(bf16[48,6144]{1,0:T(8,128)(2,1)} %reduce-scatter.2.cloned.1.call-done), channel_id=1, source_target_pairs={{0,1},{1,2},{2,3},{3,0},{4,5},{5,6},{6,7},{7,4},{8,9},{9,10},{10,1... | collective-permute-start | bytes 1769480 | tf_op jit(solution)/shard_map/ppermute | solution.py:810
  338.0 5.6 %collective-permute-start.19 = (bf16[48,3072]{1,0:T(8,128)(2,1)S(1)}, bf16[48,3072]{1,0:T(8,128)(2,1)S(1)}, u32[]{:S(2)}, u32[]{:S(2)}) collective-permute-start(bf16[48,3072]{1,0:T(8,128)(2,1)S(1)} %get-tuple-element.205), channel_id=1, source_target_pairs={{0,3},{1,0},{2,1},{3,2},{4,7},{5,4},{6,5},{7,6},{8,11},{9,8},{10,9... | collective-permute-start | bytes 884744 | tf_op jit(solution)/shard_map/ppermute | solution.py:815
  338.4 6.8 %collective-permute-start.20 = (bf16[48,3072]{1,0:T(8,128)(2,1)S(1)}, bf16[48,3072]{1,0:T(8,128)(2,1)S(1)}, u32[]{:S(2)}, u32[]{:S(2)}) collective-permute-start(bf16[48,3072]{1,0:T(8,128)(2,1)S(1)} %get-tuple-element.204), channel_id=1, source_target_pairs={{0,1},{1,2},{2,3},{3,0},{4,5},{5,6},{6,7},{7,4},{8,9},{9,10},{10,1... | collective-permute-start | bytes 884744 | tf_op jit(solution)/shard_map/ppermute | solution.py:816
  345.2 7.3 %collective-permute-start.21 = (bf16[48,6144]{1,0:T(8,128)(2,1)S(1)}, bf16[48,6144]{1,0:T(8,128)(2,1)S(1)}, u32[]{:S(2)}, u32[]{:S(2)}) collective-permute-start(bf16[48,6144]{1,0:T(8,128)(2,1)S(1)} %broadcast_select_fusion.3), channel_id=1, source_target_pairs={{0,64},{64,0},{1,65},{65,1},{2,66},{66,2},{3,67},{67,3},{4,68},{68... | collective-permute-start | bytes 1769480 | tf_op jit(solution)/shard_map/ppermute | solution.py:730
Sparse Core Ops, SparseCore 0:
  17.5 80.2 all-gather.2
  198.3 122.7 reduce-scatter.1

commit v4 on v3

--- a/solution.py
+++ b/solution.py
@@ -63,10 +63,14 @@
 STATES = 256
 CHUNK = 512
 ATT = 6144
+ALL_TOKENS = (BATCHES * TOKENS, WIDE)
+ALL_STATES = (BATCHES * STATES, WIDE)
+HIDDEN = (BATCHES * TOKENS, FF)
 VMEM_BYTES = 60 * 1024 * 1024
 FULL = (PARTS, ROWS_OWN, WIDE)
 GATED = (PARTS, ROWS_OWN, FF)
 DOWN = (PARTS, FF // PARTS, WIDE)
+RING = 4
 DOWN_PIECES = [(piece, block) for piece in range(GROUPS) for block in range(8)]
 
 
@@ -314,73 +318,68 @@
     )
 
 
-def backward_kernel(
-    c_ref,
-    x_ref,
-    gains_ref,
-    q_ref,
-    k_ref,
-    v_ref,
-    p_ref,
-    a2_ref,
-    cq_ref,
-    ck_ref,
-    cv_ref,
-    cp_ref,
-    a3_ref,
-    gate_ref,
-    up_ref,
-    weight,
-    da_ref,
-    dgate_ref,
-    dup_ref,
-    dc_ref,
-    dcq_ref,
-    dck_ref,
-    dcv_ref,
-    dself_ref,
-    dq_ref,
-    dk_ref,
-    dv_ref,
-    dgain_ref,
-    dscore_ref,
-    wq,
-    wk,
-    wv,
-    wo,
-    wcq,
-    wco,
-    wg,
-    wu,
-    wd,
-    sems,
-):
-    slots = dict(q=wq, k=wk, v=wv, o=wo, cq=wcq, co=wco, gate=wg, up=wu, down=wd)
-    copies = weight_copies(weight, slots, sems)
-    begin(copies, ("down", "gate", "up", "co", "cq", "o", "q", "k", "v"))
-    own = same_head()
-    own_low = low(own)
-    finish(copies, "down")
-    finish(copies, "gate")
-    finish(copies, "up")
-
+def core_is(part):
+    return lax.axis_index("section") == part
+
+
+def push(source, keep, send, part, window, sem):
+    @pl.when(core_is(part))
+    def _():
+        pltpu.make_async_copy(source, keep.at[window], sem).start()
+
+    @pl.when(jnp.logical_not(core_is(part)))
+    def _():
+        pltpu.make_async_copy(source, send.at[window], sem).start()
+
+    return pltpu.make_async_copy(source, keep.at[window], sem)
+
+
+def columns(start, width):
+    return (slice(None), slice(None), slice(None), pl.ds(start, width))
+
+
+def put_square(slot, part, lanes, value):
+    value = value.reshape(RING, RING, ROWS_OWN, value.shape[-1])
+    if part == 1:
+        slot[:, :, :, lanes] = value
+    else:
+        for place in range(RING):
+            slot[:, place, :, lanes] = value[place]
+
+
+def hidden_back(with_grads, c_ref, a3_ref, gains_ref, gate_ref, up_ref, wg, wu, wd, extra):
     def step(index, total):
         lanes = pl.ds(pl.multiple_of(index * CHUNK, CHUNK), CHUNK)
         grad = product(c_ref[...], wd[pl.ds(4 * index, 4)].reshape(CHUNK, WIDE), 1, 1)
         bent, slope = gelu_parts(gate_ref[:, lanes])
         dgate = low(grad * up_ref[:, lanes] * slope)
         dup = low(grad * bent)
-        dgate_ref[:, lanes] = dgate
-        dup_ref[:, lanes] = dup
         total = total + product(dgate, wg[:, :, lanes].reshape(WIDE, CHUNK), 1, 1)
-        return total + product(dup, wu[:, :, lanes].reshape(WIDE, CHUNK), 1, 1)
-
-    grad = lax.fori_loop(0, FF // CHUNK, step, jnp.zeros((BATCHES * TOKENS, WIDE), jnp.float32))
+        total = total + product(dup, wu[:, :, lanes].reshape(WIDE, CHUNK), 1, 1)
+        if with_grads:
+            n3_ref, hid_ref, gg, gu, gd0, gd1 = extra
+            rows = n3_ref[...]
+            put_square(gg, 0, lanes, low(product(rows, dgate, 0, 0)))
+            put_square(gu, 1, lanes, low(product(rows, dup, 0, 0)))
+            grad = low(product(hid_ref[:, lanes], c_ref[...], 0, 0))
+            grad = grad.reshape(RING, FF // PARTS, WIDE)
+            gd0[:, pl.ds(index, 1)] = grad[:, : FF // PARTS // 2][:, None]
+            gd1[pl.ds(index, 1)] = grad[:, FF // PARTS // 2 :][None]
+        return total
+
+    grad = lax.fori_loop(0, FF // CHUNK, step, jnp.zeros(ALL_TOKENS, jnp.float32))
     back, dgain = norm_back(grad, a3_ref[...], gains_ref[2:3])
-    dgain_ref[2:3] = dgain
-    stream = c_ref[...].astype(jnp.float32) + back
+    return c_ref[...].astype(jnp.float32) + back, dgain
+
+
+def cross_back(
+    stream, finish_weight, gains_ref, a2_ref, cq_ref, ck_ref, cv_ref, cp_ref, wcq, wco,
+    dc_ref, dcq_ref, dck_ref, dcv_ref,
+):
+    own = same_head()
+    own_low = low(own)
     dc_ref[...] = low(stream)
-    finish(copies, "co")
+    finish_weight("co")
     datt = low(product(dc_ref[...], square(wco), 1, 1))
     for row in range(BATCHES):
         part = pl.ds(TOKENS * row, TOKENS)
@@ -399,13 +398,20 @@
             dscore = low(chance * (dchance - inner))
             dcq_ref[part, lanes] = low(fold_heads(product(dscore, ck_ref[keys, lanes]), own))
             dck_ref[keys, lanes] = low(product(dscore, spread, 0, 0))
-    finish(copies, "cq")
+    finish_weight("cq")
     grad = product(dcq_ref[...], square(wcq), 1, 1)
     back, dgain = norm_back(grad, a2_ref[...], gains_ref[1:2])
-    dgain_ref[1:2] = dgain
-    stream = stream + back
+    return stream + back, dgain
+
+
+def self_back(
+    stream, finish_weight, gains_ref, x_ref, q_ref, k_ref, v_ref, p_ref, wq, wk, wv, wo,
+    dself_ref, dq_ref, dk_ref, dv_ref, dscore_ref,
+):
+    own = same_head()
+    own_low = low(own)
     dself_ref[...] = low(stream)
-    finish(copies, "o")
+    finish_weight("o")
     datt = low(product(dself_ref[...], square(wo), 1, 1))
     for row in range(BATCHES):
         part = pl.ds(TOKENS * row, TOKENS)
@@ -421,115 +427,138 @@
             dv_ref[part, lanes] = low(product(low(chance), dout, 0, 0))
             inner = jnp.sum(chance * dchance, axis=-1, keepdims=True)
             dscore = low(chance * (dchance - inner))
-            if row == 0:
-                dscore_ref[lanes] = dscore.astype(jnp.float32)
-            else:
-                dscore_ref[lanes] += dscore.astype(jnp.float32)
+            if dscore_ref is not None:
+                if row == 0:
+                    dscore_ref[lanes] = dscore.astype(jnp.float32)
+                else:
+                    dscore_ref[lanes] += dscore.astype(jnp.float32)
             dq_ref[part, lanes] = low(fold_heads(product(dscore, k_ref[part, lanes]), own))
             dk_ref[part, lanes] = low(product(dscore, spread, 0, 0))
-    finish(copies, "q")
+    finish_weight("q")
     grad = product(dq_ref[...], square(wq), 1, 1)
-    finish(copies, "k")
+    finish_weight("k")
     grad = grad + product(dk_ref[...], square(wk), 1, 1)
-    finish(copies, "v")
+    finish_weight("v")
     grad = grad + product(dv_ref[...], square(wv), 1, 1)
     back, dgain = norm_back(grad, x_ref[...].astype(jnp.float32), gains_ref[0:1])
-    dgain_ref[0:1] = dgain
-    da_ref[...] = low(stream + back)
-
-
-def weight_kernel(
-    c_ref,
-    enc_ref,
-    n1_ref,
-    o_ref,
-    n2_ref,
-    co_ref,
-    n3_ref,
-    hid_ref,
-    dgate_ref,
-    dup_ref,
-    dc_ref,
-    dcq_ref,
-    dck_ref,
-    dcv_ref,
-    dself_ref,
-    dq_ref,
-    dk_ref,
-    dv_ref,
-    weight,
-    grads,
-    denc_ref,
-    wck,
-    wcv,
-    gq,
-    gk,
-    gv,
-    go,
-    gcq,
-    gck,
-    gcv,
-    gco,
-    gg,
-    gu,
-    gd,
-    sems,
-    out_sems,
+    return stream + back, dgain
+
+
+def chain_kernel(
+    c_ref, x_ref, gains_ref, q_ref, k_ref, v_ref, p_ref, a2_ref, cq_ref, ck_ref, cv_ref, cp_ref,
+    a3_ref, gate_ref, up_ref, weight,
+    da_ref,
+    dc_ref, dcq_ref, dck_ref, dcv_ref, dself_ref, dq_ref, dk_ref, dv_ref,
+    wq, wk, wv, wo, wcq, wco, wg, wu, wd, sems,
 ):
-    copies = weight_copies(weight, dict(ck=wck, cv=wcv), sems)
-    begin(copies, ("ck", "cv"))
-    slots = dict(q=gq, k=gk, v=gv, o=go, cq=gcq, ck=gck, cv=gcv, co=gco, gate=gg, up=gu, down=gd)
-    outward = {
-        name: [
-            pltpu.make_async_copy(
-                slots[name], grads.at[:, 0, :, pl.ds(WIDE * place, WIDE)], out_sems.at[place]
-            )
-        ]
-        for place, name in enumerate(("q", "k", "v", "o", "cq", "ck", "cv", "co"))
-    }
-    for place, name in enumerate(("gate", "up")):
-        target = grads.at[:, 1, :, pl.ds(FF * place, FF)]
-        outward[name] = [pltpu.make_async_copy(slots[name], target, out_sems.at[8 + place])]
-    outward["down"] = [
-        pltpu.make_async_copy(
-            rows_at(gd, piece, block),
-            down_at(grads, piece, block),
-            out_sems.at[10 + place],
-        )
-        for place, (piece, block) in enumerate(DOWN_PIECES)
-    ]
-
-    def down_step(index, carry):
-        lanes = pl.ds(pl.multiple_of(index * CHUNK, CHUNK), CHUNK)
-        grad = low(product(hid_ref[:, lanes], c_ref[...], 0, 0))
-        gd[pl.ds(4 * index, 4)] = grad.reshape(4, FF // PARTS, WIDE)
-        return carry
-
-    lax.fori_loop(0, FF // CHUNK, down_step, 0)
-    begin(outward, ("down",))
-
-    def up_step(index, carry):
-        lanes = pl.ds(pl.multiple_of(index * CHUNK, CHUNK), CHUNK)
-        rows = n3_ref[...]
-        shape = (PARTS, ROWS_OWN, CHUNK)
-        gg[:, :, lanes] = low(product(rows, dgate_ref[:, lanes], 0, 0)).reshape(shape)
-        gu[:, :, lanes] = low(product(rows, dup_ref[:, lanes], 0, 0)).reshape(shape)
-        return carry
-
-    lax.fori_loop(0, FF // CHUNK, up_step, 0)
-    begin(outward, ("gate", "up"))
-    for name, left, right in (
-        ("co", co_ref, dc_ref),
-        ("cq", n2_ref, dcq_ref),
-        ("ck", enc_ref, dck_ref),
-        ("cv", enc_ref, dcv_ref),
-        ("o", o_ref, dself_ref),
-        ("q", n1_ref, dq_ref),
-        ("k", n1_ref, dk_ref),
-        ("v", n1_ref, dv_ref),
-    ):
-        slots[name][...] = low(product(left[...], right[...], 0, 0)).reshape(FULL)
-        begin(outward, (name,))
+    slots = dict(q=wq, k=wk, v=wv, o=wo, cq=wcq, co=wco, gate=wg, up=wu, down=wd)
+    copies = weight_copies(weight, slots, sems)
+    begin(copies, ("down", "gate", "up", "co", "cq", "o", "q", "k", "v"))
+    for name in ("down", "gate", "up"):
+        finish(copies, name)
+
+    def finish_weight(name):
+        finish(copies, name)
+
+    stream, _ = hidden_back(False, c_ref, a3_ref, gains_ref, gate_ref, up_ref, wg, wu, wd, None)
+    stream, _ = cross_back(
+        stream, finish_weight, gains_ref, a2_ref, cq_ref, ck_ref, cv_ref, cp_ref, wcq, wco,
+        dc_ref, dcq_ref, dck_ref, dcv_ref,
+    )
+    stream, _ = self_back(
+        stream, finish_weight, gains_ref, x_ref, q_ref, k_ref, v_ref, p_ref, wq, wk, wv, wo,
+        dself_ref, dq_ref, dk_ref, dv_ref, None,
+    )
+    da_ref[...] = low(stream)
+
+
+def hidden_kernel(
+    c_ref, a3_ref, gains_ref, gate_ref, up_ref, n3_ref, hid_ref, weight,
+    stream_ref, dgain_ref, keep, send,
+    wg, wu, wd, gg, gu, gd0, gd1, sems, out_sems,
+):
+    copies = weight_copies(weight, dict(gate=wg, up=wu, down=wd), sems)
+    begin(copies, ("down", "gate", "up"))
+    for name in ("down", "gate", "up"):
+        finish(copies, name)
+    stream, dgain = hidden_back(
+        True, c_ref, a3_ref, gains_ref, gate_ref, up_ref, wg, wu, wd,
+        (n3_ref, hid_ref, gg, gu, gd0, gd1),
+    )
+    sent = []
+    for part, (wide, tall) in enumerate(((gg, gd0), (gu, gd1))):
+        sent.append(push(wide, keep, send, part, columns(0, FF), out_sems.at[part]))
+        for piece in range(GROUPS):
+            for block in range(4):
+                source = tall.at[:, :, pl.ds(16 * block, 16), pl.ds(GROUP * piece, GROUP)]
+                window = (
+                    slice(None),
+                    slice(None),
+                    pl.ds(16 * piece, 16),
+                    pl.ds(FF + GROUP * block, GROUP),
+                )
+                place = 2 + 12 * part + 4 * piece + block
+                sent.append(push(source, keep, send, part, window, out_sems.at[place]))
+    stream_ref[...] = stream
+    dgain_ref[...] = dgain
+    for copy in sent:
+        copy.wait()
+
+
+def cross_kernel(
+    stream_ref, gains_ref, a2_ref, cq_ref, ck_ref, cv_ref, cp_ref, weight,
+    next_ref, dgain_ref, dc_ref, dcq_ref, dck_ref, dcv_ref,
+    wcq, wco, sems,
+):
+    copies = weight_copies(weight, dict(cq=wcq, co=wco), sems)
+    begin(copies, ("co", "cq"))
+
+    def finish_weight(name):
+        finish(copies, name)
+
+    stream, dgain = cross_back(
+        stream_ref[...], finish_weight, gains_ref, a2_ref, cq_ref, ck_ref, cv_ref, cp_ref,
+        wcq, wco, dc_ref, dcq_ref, dck_ref, dcv_ref,
+    )
+    next_ref[...] = stream
+    dgain_ref[...] = dgain
+
+
+def self_kernel(
+    stream_ref, x_ref, gains_ref, q_ref, k_ref, v_ref, p_ref,
+    enc_ref, n1_ref, o_ref, n2_ref, co_ref, dc_ref, dcq_ref, dck_ref, dcv_ref, weight,
+    da_ref, dgain_ref, dscore_ref, denc_ref, keep, send,
+    dself_ref, dq_ref, dk_ref, dv_ref,
+    wq, wk, wv, wo, wck, wcv, g0, g1, g2, g3, g4, g5, g6, g7, sems, out_sems,
+):
+    slots = dict(q=wq, k=wk, v=wv, o=wo, ck=wck, cv=wcv)
+    copies = weight_copies(weight, slots, sems)
+    begin(copies, ("o", "q", "k", "v", "ck", "cv"))
+
+    def finish_weight(name):
+        finish(copies, name)
+
+    sent = []
+
+    def emit(slot, part, column, left, right):
+        put_square(slot, part, slice(None), low(product(left[...], right[...], 0, 0)))
+        window = columns(WIDE * column, WIDE)
+        sent.append(push(slot, keep, send, part, window, out_sems.at[len(sent)]))
+
+    emit(g0, 0, 0, co_ref, dc_ref)
+    emit(g1, 0, 1, n2_ref, dcq_ref)
+    emit(g2, 1, 0, enc_ref, dck_ref)
+    emit(g3, 1, 1, enc_ref, dcv_ref)
+    stream, dgain = self_back(
+        stream_ref[...], finish_weight, gains_ref, x_ref, q_ref, k_ref, v_ref, p_ref,
+        wq, wk, wv, wo, dself_ref, dq_ref, dk_ref, dv_ref, dscore_ref,
+    )
+    da_ref[...] = low(stream)
+    dgain_ref[...] = dgain
+    emit(g4, 0, 2, o_ref, dself_ref)
+    emit(g5, 0, 3, n1_ref, dq_ref)
+    emit(g6, 1, 2, n1_ref, dk_ref)
+    emit(g7, 1, 3, n1_ref, dv_ref)
     finish(copies, "ck")
     finish(copies, "cv")
     for row in range(BATCHES):
@@ -537,8 +566,8 @@
         denc_ref[keys] = low(
             product(dck_ref[keys], square(wck), 1, 1) + product(dcv_ref[keys], square(wcv), 1, 1)
         )
-    for name in ("down", "gate", "up", "co", "cq", "ck", "cv", "o", "q", "k", "v"):
-        finish(outward, name)
+    for copy in sent:
+        copy.wait()
 
 
 def in_vmem(count):
@@ -553,9 +582,6 @@
     return jax.ShapeDtypeStruct(dims, kind)
 
 
-ALL_TOKENS = (BATCHES * TOKENS, WIDE)
-ALL_STATES = (BATCHES * STATES, WIDE)
-HIDDEN = (BATCHES * TOKENS, FF)
 params = pltpu.CompilerParams(vmem_limit_bytes=VMEM_BYTES)
 
 
@@ -607,49 +633,90 @@
     )(x, ck, cv, self_add, cross_add, gains, weight)
 
 
-def run_backward(cotangent, x, gains, saved, weight):
+HALF = (RING, RING, ROWS_OWN, ATT // 2)
+RINGED = (RING, RING, ROWS_OWN, WIDE)
+RINGED_WIDE = (RING, RING, ROWS_OWN, FF)
+RINGED_TALL = (RING, RING, FF // PARTS // 2, WIDE)
+ANYWHERE = pl.BlockSpec(memory_space=pl.ANY)
+DMAS = pltpu.SemaphoreType.DMA((34,))
+
+
+def run_chain(cotangent, x, gains, saved, weight):
     (ck, cv, n1, q, k, v, p, o, a2, n2, cq, cp, co, a3, n3, gate, up, hid) = saved
-    outs = [
-        shape_of(ALL_TOKENS),
-        shape_of(HIDDEN),
-        shape_of(HIDDEN),
-        shape_of(ALL_TOKENS),
-        shape_of(ALL_TOKENS),
-        shape_of(ALL_STATES),
-        shape_of(ALL_STATES),
-        shape_of(ALL_TOKENS),
-        shape_of(ALL_TOKENS),
-        shape_of(ALL_TOKENS),
-        shape_of(ALL_TOKENS),
-        shape_of((3, WIDE), jnp.float32),
-        shape_of((WIDE, TOKENS), jnp.float32),
-    ]
     return pl.pallas_call(
-        backward_kernel,
-        out_shape=outs,
-        in_specs=in_vmem(15) + [pl.BlockSpec(memory_space=pl.ANY)],
-        out_specs=in_vmem(len(outs)),
-        scratch_shapes=held(*[FULL] * 6, GATED, GATED, DOWN) + [pltpu.SemaphoreType.DMA((34,))],
+        chain_kernel,
+        out_shape=shape_of(ALL_TOKENS),
+        in_specs=in_vmem(15) + [ANYWHERE],
+        out_specs=in_vmem(1)[0],
+        scratch_shapes=held(
+            ALL_TOKENS, ALL_TOKENS, ALL_STATES, ALL_STATES, *[ALL_TOKENS] * 4,
+            *[FULL] * 6, GATED, GATED, DOWN,
+        )
+        + [DMAS],
         compiler_params=params,
-        name="layer_backward",
+        name="backward_chain",
     )(cotangent, x, gains, q, k, v, p, a2, cq, ck, cv, cp, a3, gate, up, weight)
 
 
-def run_weights(cotangent, enc, saved, records, weight):
+def run_hidden(cotangent, gains, saved, weight):
     (ck, cv, n1, q, k, v, p, o, a2, n2, cq, cp, co, a3, n3, gate, up, hid) = saved
-    (dgate, dup, dc, dcq, dck, dcv, dself, dq, dk, dv) = records
     return pl.pallas_call(
-        weight_kernel,
-        out_shape=[shape_of((PARTS, 2, ROWS_OWN, ATT)), shape_of(ALL_STATES)],
-        in_specs=in_vmem(18) + [pl.BlockSpec(memory_space=pl.ANY)],
-        out_specs=[pl.BlockSpec(memory_space=pl.ANY)] + in_vmem(1),
-        scratch_shapes=held(FULL, FULL, *[FULL] * 8, GATED, GATED, DOWN)
-        + [pltpu.SemaphoreType.DMA((34,)), pltpu.SemaphoreType.DMA((34,))],
+        hidden_kernel,
+        out_shape=[
+            shape_of(ALL_TOKENS, jnp.float32),
+            shape_of((1, WIDE), jnp.float32),
+            shape_of(HALF),
+            shape_of(HALF),
+        ],
+        in_specs=in_vmem(7) + [ANYWHERE],
+        out_specs=in_vmem(2) + [ANYWHERE, ANYWHERE],
+        scratch_shapes=held(
+            GATED, GATED, DOWN, RINGED_WIDE, RINGED_WIDE, RINGED_TALL, RINGED_TALL
+        )
+        + [DMAS, DMAS],
         compiler_params=params,
-        name="weight_gradients",
-    )(
-        cotangent, enc, n1, o, n2, co, n3, hid, dgate, dup, dc, dcq, dck, dcv, dself, dq, dk, dv, weight
-    )
+        name="hidden_backward",
+    )(cotangent, a3, gains, gate, up, n3, hid, weight)
+
+
+def run_cross(stream, gains, saved, weight):
+    (ck, cv, n1, q, k, v, p, o, a2, n2, cq, cp, co, a3, n3, gate, up, hid) = saved
+    return pl.pallas_call(
+        cross_kernel,
+        out_shape=[
+            shape_of(ALL_TOKENS, jnp.float32),
+            shape_of((1, WIDE), jnp.float32),
+            shape_of(ALL_TOKENS),
+            shape_of(ALL_TOKENS),
+            shape_of(ALL_STATES),
+            shape_of(ALL_STATES),
+        ],
+        in_specs=in_vmem(7) + [ANYWHERE],
+        out_specs=in_vmem(6),
+        scratch_shapes=held(FULL, FULL) + [DMAS],
+        compiler_params=params,
+        name="cross_backward",
+    )(stream, gains, a2, cq, ck, cv, cp, weight)
+
+
+def run_self(stream, x, gains, enc, saved, records, weight):
+    (ck, cv, n1, q, k, v, p, o, a2, n2, cq, cp, co, a3, n3, gate, up, hid) = saved
+    return pl.pallas_call(
+        self_kernel,
+        out_shape=[
+            shape_of(ALL_TOKENS),
+            shape_of((1, WIDE), jnp.float32),
+            shape_of((WIDE, TOKENS), jnp.float32),
+            shape_of(ALL_STATES),
+            shape_of(HALF),
+            shape_of(HALF),
+        ],
+        in_specs=in_vmem(16) + [ANYWHERE],
+        out_specs=in_vmem(4) + [ANYWHERE, ANYWHERE],
+        scratch_shapes=held(*[ALL_TOKENS] * 4, *[FULL] * 6, *[RINGED] * 8) + [DMAS, DMAS],
+        compiler_params=params,
+        name="self_backward",
+    )(stream, x, gains, q, k, v, p, enc, n1, o, n2, co, *records, weight)
 
 
 def pack_attention(query, kv, out, c_query, c_kv, c_out):
@@ -665,24 +732,28 @@
     return jnp.concatenate([w_in.reshape(rows, -1), pieces.reshape(rows, FF)], axis=1)
 
 
-def unpack(attention, hidden):
-    rows = attention.shape[0]
-    start = 0
-    pieces = []
-    for width in (768, 1536, 768, 768, 1536, 768):
-        pieces.append(attention[:, start : start + width])
-        start += width
-    query, kv, out, c_query, c_kv, c_out = pieces
-    w_ffn = hidden[:, 2 * FF :].reshape(GROUPS, 16, 8, GROUP).transpose(2, 1, 0, 3)
+def unpack(first, second):
+    rows = first.shape[0]
+    squares = [
+        part[:, ATT // 2 + WIDE * place : ATT // 2 + WIDE * (place + 1)]
+        for part in (first, second)
+        for place in range(4)
+    ]
+    c_out, c_query, out, query, c_key, c_value, key, value = squares
+    tall = [
+        part[:, FF : FF + 1024].reshape(GROUPS, 16, 4, GROUP).transpose(2, 1, 0, 3)
+        for part in (first, second)
+    ]
+    tall = [part.reshape(FF // PARTS // 2, WIDE) for part in tall]
     return (
         query,
-        kv.reshape(rows, 2, WIDE),
+        jnp.stack([key, value], axis=1),
         out,
         c_query,
-        c_kv.reshape(rows, 2, WIDE),
+        jnp.stack([c_key, c_value], axis=1),
         c_out,
-        hidden[:, : 2 * FF].reshape(rows, 2, FF),
-        w_ffn.reshape(FF // PARTS, WIDE),
+        jnp.stack([first[:, :FF], second[:, :FF]], axis=1),
+        jnp.concatenate(tall, axis=0),
     )
 
 
@@ -748,6 +819,20 @@
         pairs = [(p, p + steps) for p in range(planes) if p % 2 == (steps < 0)]
         return lax.ppermute(value, "rep", pairs)
 
+    along_z = [[RING * x + z for z in range(RING)] for x in range(RING)]
+    along_x = [[RING * x + z for x in range(RING)] for z in range(RING)]
+    first_rings = along_z + [[PARTS + d for d in ring] for ring in along_x]
+    second_rings = along_x + [[PARTS + d for d in ring] for ring in along_z]
+
+    def add_halves(keep, received):
+        total = low(keep.astype(jnp.float32) + received.astype(jnp.float32))
+        return total.reshape(WIDE, ATT // 2)
+
+    def scatter(value, rings):
+        return lax.psum_scatter(
+            value, ("section", "fsdp"), scatter_dimension=0, axis_index_groups=rings, tiled=True
+        )
+
     attention = pack_attention(
         self_query[0], self_kv[0], self_out[0], cross_query[0], cross_kv[0], cross_out[0]
     )
@@ -777,15 +862,20 @@
     current = jnp.where(layer == 0, rows_in, between_layers(first, 1))
     result, *saved = run_second(current, ck, cv, self_add, cross_add, gains, weight)
     saved = [ck, cv] + saved
-    grad_first = run_backward(given, current, gains, saved, weight)[0]
+    grad_first = run_chain(given, current, gains, saved, weight)
     incoming = jnp.where(layer == 1, given, between_layers(grad_first, -1))
-    grad_input, *records, grad_gains, grad_scores = run_backward(
-        incoming, current, gains, saved, weight
-    )
-    grads, grad_enc = run_weights(incoming, enc, saved, records, weight)
-    partial = lax.psum_scatter(
-        grads.reshape(2 * WIDE, ATT), ("fsdp", "section"), scatter_dimension=0, tiled=True
-    )
+    stream, gain_three, keep, send = run_hidden(incoming, gains, saved, weight)
+    received = flip_core(send)
+    stream, gain_two, *records = run_cross(stream, gains, saved, weight)
+    wide_sum = add_halves(keep, received)
+    wide_sum, stream = lax.optimization_barrier((wide_sum, stream))
+    wide_part = scatter(wide_sum, first_rings)
+    grad_input, gain_one, grad_scores, grad_enc, keep, send = run_self(
+        stream, current, gains, enc, saved, records, weight
+    )
+    square_part = scatter(add_halves(keep, flip_core(send)), first_rings)
+    partial = scatter(jnp.concatenate([wide_part, square_part], axis=1), second_rings)
+    grad_gains = jnp.concatenate([gain_one, gain_two, gain_three], axis=0)
     outs = rows_back(jnp.stack([result, grad_input]))
     encoder_total = grad_enc.astype(jnp.float32) + beside(grad_enc).astype(jnp.float32)
     encoder_total = from_home(encoder_total)
@@ -801,9 +891,15 @@
     little = jnp.where(at_home, little, beside(little))
     own_gains = lax.dynamic_slice(little, (0, part_index * ROWS_OWN), (3, ROWS_OWN))
     own_table = lax.dynamic_slice(little, (3, part_index * 2 * HEADS), (1, 2 * HEADS))
-    partial, own_gains, own_table, encoder_total, outs = lax.optimization_barrier(
-        (partial, own_gains, own_table, encoder_total, outs)
-    )
+    own_table = own_table.reshape(2, HEADS)
+    results = (
+        outs[0].reshape(1, BATCHES, 1, TOKENS, WIDE),
+        outs[1].reshape(1, BATCHES, 1, TOKENS, WIDE),
+        encoder_total.reshape(BATCHES, 1, STATES, WIDE),
+        own_gains[None],
+        own_table[None],
+    )
+    partial, results = lax.optimization_barrier((partial, results))
     up = [(p, (p + 1) % planes) for p in range(planes)]
     down = [(p, (p - 1) % planes) for p in range(planes)]
     above = lax.ppermute(partial, "rep", down).astype(jnp.float32)
@@ -819,26 +915,10 @@
     )
     mine = jnp.where(at_home, own_layer, other_layer)
     theirs = flip_core(jnp.where(at_home, other_layer, own_layer))
-    attention = jnp.where(first_core, mine, theirs).astype(jnp.float32)
-    hidden = jnp.where(first_core, theirs, mine).astype(jnp.float32)
-    query, kv, out, c_query, c_kv, c_out, w_in, w_ffn = unpack(attention, hidden)
-    ordered = (
-        own_gains,
-        query,
-        kv,
-        out,
-        own_table.reshape(2, HEADS),
-        c_query,
-        c_kv,
-        c_out,
-        w_in,
-        w_ffn,
-    )
-    return (
-        outs[0].reshape(1, BATCHES, 1, TOKENS, WIDE),
-        outs[1].reshape(1, BATCHES, 1, TOKENS, WIDE),
-        encoder_total.reshape(BATCHES, 1, STATES, WIDE),
-    ) + tuple(member[None] for member in ordered)
+    first_part = jnp.where(first_core, mine, theirs).astype(jnp.float32)
+    second_part = jnp.where(first_core, theirs, mine).astype(jnp.float32)
+    query, kv, out, *others = [member[None] for member in unpack(first_part, second_part)]
+    return (*results[:4], query, kv, out, results[4], *others)
 
 
 def solution(mesh):

time: 373 us -> 376 us (level)
  other arithmetic: 12.6 us -> 30.7 us
  waiting for transfers between devices: 170 us -> 158 us
    reduce_scatter x1 -> x3, waiting for transfers between devices: 58.6 us -> 37.7 us  [scatter(): lax.psum_scatter(value, ('section', 'fsdp'), scatter_dimension=0, axis_in...]
    convert_element_type x1 -> x3, other arithmetic: 0.14 us -> 14.7 us  [low(): return value.astype(jnp.bfloat16)]
    ppermute x2 -> x4, waiting for transfers between devices: 1.84 us -> 11.3 us  [flip_core(): return lax.ppermute(value, 'section', [(0, 1), (1, 0)])]
    ppermute x1, waiting for transfers between devices: 5.67 us -> 0.01 us  [rows_back(): lax.ppermute(value, ('section', 'rep'), pairs)]
    another operation x6 -> x3, local copies, waits for them, and re-layouts: 5.13 us -> 0.81 us  [the longest x1 0.65 us: shards(): own_table[None]]
    unnamed x57 -> x62, local copies, waits for them, and re-layouts: 6.84 us -> 9.21 us
    pallas_call x3 -> x4, Pallas kernels: 58 us -> 59.4 us  [the longest x1 20.4 us: run_chain(): pl.pallas_call(chain_kernel, out_shape=shape_of(ALL_TOKENS), in_specs=in_...]
  transfers between devices with their start and end apart: 24 -> 28, of which waited for: 18 -> 19; matrix products, arithmetic and copies ran while one was open for 4% -> 6% of each run, Pallas kernels for 0% -> 6%
where the time goes in v4:
time: 376 us; the launch traced here: 369 us
  waiting for transfers between devices  158 us (42%)
  Pallas kernels  85.3 us (23%)
  starting transfers between devices  42.2 us (11%)
  other arithmetic  30.7 us (8%)
  blocking collectives  20.7 us (6%)
  local copies, waits for them, and re-layouts  16.8 us (4%)
  between operations  14.9 us (4%)
    all_gather x1, waiting for transfers between devices, shards(): weight = lax.all_gather(half, ('fsdp', 'section'), axis=0, tiled=True)  46.9 us
    reduce_scatter x3, waiting for transfers between devices, scatter(): lax.psum_scatter(value, ('section', 'fsdp'), scatter_dimension=0, axis_in...  37.7 us
    all_gather x1, blocking collectives, shards(): small = lax.all_gather(from_home(small), 'fsdp', axis=0, tiled=False)  20.7 us
    pallas_call x1, Pallas kernels, run_chain(): pl.pallas_call(chain_kernel, out_shape=shape_of(ALL_TOKENS), in_specs=in_...  20.4 us
    ppermute x2, waiting for transfers between devices, beside(): return lax.ppermute(value, 'rep', [(p, p ^ 1) for p in range(planes)])  19.6 us
    pallas_call x1, Pallas kernels, run_hidden(): pl.pallas_call(hidden_kernel, out_shape=[shape_of(ALL_TOKENS, jnp.float32...  17.9 us
    convert_element_type x3, other arithmetic, low(): return value.astype(jnp.bfloat16)  14.7 us
    ppermute x1, waiting for transfers between devices, shards(): above = lax.ppermute(partial, 'rep', down).astype(jnp.float32)  14.1 us
  transfers between devices with their start and end apart: 28, of which 19 were waited for; matrix products, arithmetic and copies ran while one was open for 6% of the time, Pallas kernels for 6%

profile of v4, /device:TPU:1, one launch (start us, length us, event | category | flops | bytes accessed | tf_op | source)
XLA Modules:
  0.0 368.9 jit_solution(4687974861457696259)
XLA Ops:
  7.3 1.0 bitcast_dynamic-update-slice_fusion.3
  8.3 0.9 copy.63
  9.2 0.9 copy.64
  10.1 1.1 copy.65
  11.8 0.9 broadcast_select_fusion.2
  12.7 1.4 collective-permute-start
  14.1 1.8 collective-permute-done
  16.0 1.0 select_select_fusion
  17.1 1.3 collective-permute-start.3
  18.7 1.3 collective-permute-start.4
  20.1 1.3 collective-permute-start.1
  21.4 1.3 collective-permute-start.2
  23.3 20.7 %all-gather = bf16[128,128]{1,0:T(8,128)(2,1)S(1)} all-gather(bf16[8,128]{1,0:T(8,128)(2,1)S(1)} %broadcast_select_fusion.11), channel_id=2, replica_groups=mesh['section'=2,'fsdp'=16,'rep'=4] {'fsdp'}, dimensions={0}, use_global_device_ids=true | all-gather | bytes 34816 | tf_op jit(solution)/shard_map/all_gather | solution.py:848
  46.0 1.0 bitcast_select_fusion.self_add_ref
  47.7 1.0 broadcast_select_fusion.6
  49.5 1.0 broadcast_select_fusion.1.enc_ref
  50.5 46.9 %all-gather.3.cloned.1.call-done = bf16[1536,6144]{1,0:T(8,128)(2,1)} async-done(((bf16[48,6144]{1,0:T(8,128)(2,1)}), bf16[1536,6144]{1,0:T(8,128)(2,1)}) %all-gather.3.cloned.1.call-update) | async-done | bytes 18874384 | tf_op jit(solution)/shard_map/all_gather | solution.py:843
  97.4 12.7 %first_forward.1 = (bf16[128,768]{1,0:T(8,128)(2,1)}, bf16[512,768]{1,0:T(8,128)(2,1)}, bf16[512,768]{1,0:T(8,128)(2,1)}) custom-call(bf16[128,768]{1,0:T(8,128)(2,1)} %get-tuple-element.113.x_ref, bf16[512,768]{1,0:T(8,128)(2,1)} %broadcast_select_fusion.1.enc_ref, f32[2,768,64]{2,1,0:T(8,128)} %bitcast_select_fusion.self_add_ref, ...), custom_call_target="tpu_custom_call" | custom-call | tf_op jit(solution)/shard_map/first_forward/pallas_call | solution.py:610
  110.1 3.4 collective-permute-start.5
  113.5 4.1 %collective-permute-done.5 = bf16[128,768]{1,0:T(8,128)(2,1)S(1)} collective-permute-done((bf16[128,768]{1,0:T(8,128)(2,1)}, bf16[128,768]{1,0:T(8,128)(2,1)S(1)}, u32[]{:S(2)}, u32[]{:S(2)}) %collective-permute-start.5) | collective-permute-done | bytes 196640 | tf_op jit(solution)/shard_map/ppermute | solution.py:820
  118.3 13.3 %second_forward.1 = (bf16[128,768]{1,0:T(8,128)(2,1)}, bf16[128,768]{1,0:T(8,128)(2,1)}, bf16[128,768]{1,0:T(8,128)(2,1)}, bf16[128,768]{1,0:T(8,128)(2,1)}, bf1...) custom-call(bf16[128,768]{1,0:T(8,128)(2,1)} %broadcast_select_fusio, ...), custom_call_target="tpu_custom_call" | custom-call | tf_op jit(solution)/shard_map/second_forward/pallas_call | solution.py:625
  131.6 20.4 %backward_chain.1 = bf16[128,768]{1,0:T(8,128)(2,1)} custom-call(bf16[128,768]{1,0:T(8,128)(2,1)} %get-tuple-element.112.c_ref, bf16[128,768]{1,0:T(8,128)(2,1)} %broadcast_select_fusion.7.x_ref, f32[3,768]{1,0:T(4,128)} %reshape.229.gains_ref, bf16[128,768]{1,0:T(8,128)(2,1)} %get-tuple-element.122.q_ref, bf16[128,768]{1,0:T(8,128)(2,1)} %get-tuple-element.123.k_ref, ...), custom_call_target="tpu_custom_call" | custom-call | tf_op jit(solution)/shard_map/backward_chain/pallas_call | solution.py:646
  152.0 1.8 collective-permute-start.6
  153.8 5.7 %collective-permute-done.6 = bf16[128,768]{1,0:T(8,128)(2,1)S(1)} collective-permute-done((bf16[128,768]{1,0:T(8,128)(2,1)}, bf16[128,768]{1,0:T(8,128)(2,1)S(1)}, u32[]{:S(2)}, u32[]{:S(2)}) %collective-permute-start.6) | collective-permute-done | bytes 196640 | tf_op jit(solution)/shard_map/ppermute | solution.py:820
  160.2 17.9 %hidden_backward.1 = (f32[128,768]{1,0:T(8,128)}, f32[1,768]{1,0:T(1,128)}, bf16[4,4,48,3072]{3,2,1,0:T(8,128)(2,1)}, bf16[4,4,48,3072]{3,2,1,0:T(8,128)(2,1)}) custom-call(bf16[128,768]{1,0:T(8,128)(2,1)} %broadcast_select_fusion.8.c_ref, f32[128,768]{1,0:T(8,128)} %get-tuple-element.129.a3_ref, f32[3,768]{1,0:T(4,128)} %reshape.229.gains_ref, ...), custom_call_target="tpu_custom_call" | custom-call | tf_op jit(solution)/shard_map/hidden_backward/pallas_call | solution.py:663
  178.0 2.0 collective-permute-start.7
  180.1 7.8 %cross_backward.1 = (f32[128,768]{1,0:T(8,128)}, f32[1,768]{1,0:T(1,128)}, bf16[128,768]{1,0:T(8,128)(2,1)}, bf16[128,768]{1,0:T(8,128)(2,1)}, bf16[512,768]{1,0:T(8,128)(2,1)}, /*index=5*/bf16[512,768]{1,0:T(8,128)(2,1)}) custom-call(f32[128,768]{1,0:T(8,128)} %get-tuple-element.136.stream_ref, f32[3,768]{1,0:T(4,128)} %reshape.229.gains_ref, ...), custom_call_target="tpu_custom_call" | custom-call | tf_op jit(solution)/shard_map/cross_backward/pallas_call | solution.py:684
  188.0 8.0 %add_convert_fusion.1 = bf16[4,4,48,3072]{3,2,1,0:T(8,128)(2,1)} fusion(bf16[4,4,48,3072]{3,2,1,0:T(8,128)(2,1)} %collective-permute-done.7, bf16[4,4,48,3072]{3,2,1,0:T(8,128)(2,1)} %get-tuple-element.134), kind=kLoop, calls=%fused_computation.1 | loop fusion | flops 9437184 | bytes 14155776 | tf_op jit(solution)/shard_map/convert_element_type | solution.py:87
  196.2 13.3 %self_backward.1 = (bf16[128,768]{1,0:T(8,128)(2,1)}, f32[1,768]{1,0:T(1,128)}, f32[768,64]{1,0:T(8,128)}, bf16[512,768]{1,0:T(8,128)(2,1)}, bf16[4,4,48,3072]{3...) custom-call(f32[128,768]{1,0:T(8,128)} %get-tuple-element.139.stream_ref, bf16[128,768]{1,0:T(8,128)(2,1)} %broadcast_select_fusion.7.x_ref, ...), custom_call_target="tpu_custom_call" | custom-call | tf_op jit(solution)/shard_map/self_backward/pallas_call | solution.py:704
  210.0 7.7 %collective-permute-done.8 = bf16[4,4,48,3072]{3,2,1,0:T(8,128)(2,1)S(1)} collective-permute-done((bf16[4,4,48,3072]{3,2,1,0:T(8,128)(2,1)}, bf16[4,4,48,3072]{3,2,1,0:T(8,128)(2,1)S(1)}, u32[]{:S(2)}, u32[]{:S(2)}) %collective-permute-start.8) | collective-permute-done | bytes 4718624 | tf_op jit(solution)/shard_map/ppermute | solution.py:801
  217.7 6.6 %add_convert_fusion = bf16[4,4,48,3072]{3,2,1,0:T(8,128)(2,1)} fusion(bf16[4,4,48,3072]{3,2,1,0:T(8,128)(2,1)S(1)} %collective-permute-done.8, bf16[4,4,48,3072]{3,2,1,0:T(8,128)(2,1)} %get-tuple-element.148), kind=kLoop, calls=%fused_computation | loop fusion | flops 9437184 | bytes 14155776 | tf_op jit(solution)/shard_map/convert_element_type | solution.py:87
  224.4 2.9 reduce-scatter.4.cloned.1.call-done
  227.3 34.8 %reduce-scatter.6.cloned.1.call-done = bf16[192,3072]{1,0:T(8,128)(2,1)} async-done(((bf16[768,3072]{1,0:T(8,128)(2,1)}), bf16[192,3072]{1,0:T(8,128)(2,1)}) %reduce-scatter.6.cloned.1.call-update) | async-done | bytes 1179664 | tf_op jit(solution)/shard_map/reduce_scatter | solution.py:832
  262.1 3.3 pad_maximum_fusion
  265.4 1.1 copy-done
  266.5 1.2 collective-permute-start.10
  267.7 16.9 %collective-permute-done.10 = bf16[512,768]{1,0:T(8,128)(2,1)S(1)} collective-permute-done((bf16[512,768]{1,0:T(8,128)(2,1)S(1)}, bf16[512,768]{1,0:T(8,128)(2,1)S(1)}, u32[]{:S(2)}, u32[]{:S(2)}) %collective-permute-start.10) | collective-permute-done | bytes 786464 | tf_op jit(solution)/shard_map/ppermute | solution.py:808
  284.6 1.3 convert_add_fusion
  285.9 1.3 collective-permute-start.11
  289.3 3.3 collective-permute-start.12
  292.6 0.8 collective-permute-done.12
  293.4 1.5 collective-permute-start.13
  294.9 1.2 collective-permute-done.13
  296.1 3.3 collective-permute-start.14
  299.4 1.2 collective-permute-done.14
  300.6 2.7 collective-permute-done.15
  303.3 0.9 collective-permute-start.16
  304.2 7.9 %collective-permute-start.9 = (bf16[2,128,768]{2,1,0:T(8,128)(2,1)S(1)}, bf16[2,128,768]{2,1,0:T(8,128)(2,1)S(1)}, u32[]{:S(2)}, u32[]{:S(2)}) collective-permute-start(bf16[2,128,768]{2,1,0:T(8,128)(2,1)S(1)} %pad_maximum_fusion.2), channel_id=1, source_target_pairs={{64,1},{1,64},{66,3},{3,66},{68,5},{5,68},{70,7},{7,70},{72,9},{9,... | collective-permute-start | bytes 1179656 | tf_op jit(solution)/shard_map/ppermute | solution.py:816
  312.1 2.5 collective-permute-start.17
  314.6 5.6 %collective-permute-done.17 = f32[8,768]{1,0:T(8,128)S(1)} collective-permute-done((f32[8,768]{1,0:T(8,128)S(1)}, f32[8,768]{1,0:T(8,128)S(1)}, u32[]{:S(2)}, u32[]{:S(2)}) %collective-permute-start.17) | collective-permute-done | bytes 24608 | tf_op jit(solution)/shard_map/ppermute | solution.py:890
  320.2 2.7 collective-permute-done.18
  325.1 2.8 broadcast_select_fusion
  327.8 1.5 collective-permute-start.20
  329.3 14.1 %collective-permute-done.19 = bf16[48,6144]{1,0:T(8,128)(2,1)S(1)} collective-permute-done((bf16[48,6144]{1,0:T(8,128)(2,1)}, bf16[48,6144]{1,0:T(8,128)(2,1)S(1)}, u32[]{:S(2)}, u32[]{:S(2)}) %collective-permute-start.19) | collective-permute-done | bytes 589856 | tf_op jit(solution)/shard_map/ppermute | solution.py:905
  343.6 1.5 collective-permute-start.22
  345.1 5.4 %collective-permute-done.21 = bf16[48,3072]{1,0:T(8,128)(2,1)S(1)} collective-permute-done((bf16[48,3072]{1,0:T(8,128)(2,1)S(1)}, bf16[48,3072]{1,0:T(8,128)(2,1)S(1)}, u32[]{:S(2)}, u32[]{:S(2)}) %collective-permute-start.21) | collective-permute-done | bytes 294944 | tf_op jit(solution)/shard_map/ppermute | solution.py:911
  350.5 1.1 collective-permute-done.22
  351.7 2.8 collective-permute-start.23
  354.5 1.6 collective-permute-done.23
  356.4 0.9 slice_bitcast_fusion.4
  357.9 1.5 copy.59
  359.4 0.9 copy.58
  360.4 0.9 copy.57
  361.3 0.8 maximum_bitcast_fusion.1
  (143 shorter events, 12.6 us)
Async XLA Ops:
  7.2 4.1 %copy-start.9 = (bf16[1,128,768]{2,1,0:T(8,128)(2,1)S(1)}, bf16[1,128,768]{2,1,0:T(8,128)(2,1)}, u32[]{:S(2)}) copy-start(bf16[1,128,768]{2,1,0:T(8,128)(2,1)} %param.39) | copy-start | bytes 589828
  7.2 4.4 %copy-start.10 = (bf16[1,48,768]{2,1,0:T(8,128)(2,1)S(1)}, bf16[1,48,768]{2,1,0:T(8,128)(2,1)}, u32[]{:S(2)}) copy-start(bf16[1,48,768]{2,1,0:T(8,128)(2,1)} %param.33) | copy-start | bytes 221188
  7.2 4.4 %copy-start.11 = (bf16[1,48,768]{2,1,0:T(8,128)(2,1)S(1)}, bf16[1,48,768]{2,1,0:T(8,128)(2,1)}, u32[]{:S(2)}) copy-start(bf16[1,48,768]{2,1,0:T(8,128)(2,1)} %param.35) | copy-start | bytes 221188
  7.2 4.5 %copy-start.12 = (bf16[1,48,768]{2,1,0:T(8,128)(2,1)S(1)}, bf16[1,48,768]{2,1,0:T(8,128)(2,1)}, u32[]{:S(2)}) copy-start(bf16[1,48,768]{2,1,0:T(8,128)(2,1)} %param.37) | copy-start | bytes 221188
  7.2 90.2 %all-gather.3.cloned.1.call-start = ((), (), s32[]{:S(2)}) async-start(), calls=%async_computation.3 | async-start | bytes 19464192 | tf_op jit(solution)/shard_map/all_gather | solution.py:843
  11.7 5.3 %copy-start.18 = (s32[2,1,256]{2,1,0:T(1,128)S(1)}, s32[2,1,256]{2,1,0:T(1,128)}, u32[]{:S(2)}) copy-start(s32[2,1,256]{2,1,0:T(1,128)} %param.29) | copy-start | bytes 6148
  11.7 5.3 %copy-start.14 = (s32[2,1,64]{2,1,0:T(1,128)S(1)}, s32[2,1,64]{2,1,0:T(1,128)}, u32[]{:S(2)}) copy-start(s32[2,1,64]{2,1,0:T(1,128)} %param.28) | copy-start | bytes 1540
  11.8 6.7 %copy-start.19 = (bf16[1,3,48]{2,1,0:T(4,128)(2,1)S(1)}, bf16[1,3,48]{2,1,0:T(4,128)(2,1)}, u32[]{:S(2)}) copy-start(bf16[1,3,48]{2,1,0:T(4,128)(2,1)} %param.30) | copy-start | bytes 868
  11.8 6.7 %copy-start.20 = (bf16[1,2,12]{2,1,0:T(2,128)(2,1)S(1)}, bf16[1,2,12]{2,1,0:T(2,128)(2,1)}, u32[]{:S(2)}) copy-start(bf16[1,2,12]{2,1,0:T(2,128)(2,1)} %param.34) | copy-start | bytes 148
  11.8 8.3 %copy-start.4 = (bf16[2,1,64,768]{3,2,1,0:T(8,128)(2,1)S(1)}, bf16[2,1,64,768]{3,2,1,0:T(8,128)(2,1)}, u32[]{:S(2)}) copy-start(bf16[2,1,64,768]{3,2,1,0:T(8,128)(2,1)} %param.26) | copy-start | bytes 589828
  11.8 8.3 %copy-start.5 = (bf16[2,1,64,768]{3,2,1,0:T(8,128)(2,1)S(1)}, bf16[2,1,64,768]{3,2,1,0:T(8,128)(2,1)}, u32[]{:S(2)}) copy-start(bf16[2,1,64,768]{3,2,1,0:T(8,128)(2,1)} %param.25) | copy-start | bytes 589828
  11.8 9.6 %copy-start.3 = (bf16[2,1,256,768]{3,2,1,0:T(8,128)(2,1)S(1)}, bf16[2,1,256,768]{3,2,1,0:T(8,128)(2,1)}, u32[]{:S(2)}) copy-start(bf16[2,1,256,768]{3,2,1,0:T(8,128)(2,1)} %param.27) | copy-start | bytes 2359300
  12.7 31.4 %copy-start.13 = (f32[32,64]{1,0:T(8,128)S(1)}, f32[32,64]{1,0:T(8,128)}, u32[]{:S(2)}) copy-start(f32[32,64]{1,0:T(8,128)} %constant.142.clone) | copy-start | bytes 24580
  12.7 3.3 collective-permute-start
  17.0 210.3 %reduce-scatter.4.cloned.1.call-start = ((), (), s32[]{:S(2)}) async-start(), calls=%async_computation.4 | async-start | bytes 5898240 | tf_op jit(solution)/shard_map/reduce_scatter | solution.py:832
  17.1 28.6 %collective-permute-start.3 = (s32[2,320]{1,0:T(2,128)S(1)}, s32[2,320]{1,0:T(2,128)S(1)}, u32[]{:S(2)}, u32[]{:S(2)}) collective-permute-start(s32[2,320]{1,0:T(2,128)S(1)} %pad_add_fusion), channel_id=1, source_target_pairs={{0,1},{65,64},{2,3},{67,66},{4,5},{69,68},{6,7},{71,70},{8,9},{73,... | collective-permute-start | bytes 7688 | tf_op jit(solution)/shard_map/ppermute | solution.py:812
  18.7 4.6 %collective-permute-start.4 = (bf16[8,128]{1,0:T(8,128)(2,1)S(1)}, bf16[8,128]{1,0:T(8,128)(2,1)S(1)}, u32[]{:S(2)}, u32[]{:S(2)}) collective-permute-start(bf16[8,128]{1,0:T(8,128)(2,1)S(1)} %scatter.15), channel_id=1, source_target_pairs={{0,64},{65,1},{2,66},{67,3},{4,68},{69,5},{6,70},{71,7},{8,72},{73... | collective-permute-start | bytes 6152 | tf_op jit(solution)/shard_map/ppermute | solution.py:805
  20.1 27.6 %collective-permute-start.1 = (bf16[2,128,768]{2,1,0:T(8,128)(2,1)S(1)}, bf16[2,128,768]{2,1,0:T(8,128)(2,1)}, u32[]{:S(2)}, u32[]{:S(2)}) collective-permute-start(bf16[2,128,768]{2,1,0:T(8,128)(2,1)S(1)} %pad_maximum_fusion.1), channel_id=1, source_target_pairs={{0,1},{65,64},{2,3},{67,66},{4,5},{69,68},{6,7},{71,70},{8,9},{73,... | collective-permute-start | bytes 1179656 | tf_op jit(solution)/shard_map/ppermute | solution.py:812
  21.4 28.1 %collective-permute-start.2 = (bf16[512,768]{1,0:T(8,128)(2,1)S(1)}, bf16[512,768]{1,0:T(8,128)(2,1)S(1)}, u32[]{:S(2)}, u32[]{:S(2)}) collective-permute-start(bf16[512,768]{1,0:T(8,128)(2,1)S(1)} %bitcast.118), channel_id=1, source_target_pairs={{0,1},{65,64},{2,3},{67,66},{4,5},{69,68},{6,7},{71,70},{8,9},{73,... | collective-permute-start | bytes 2359304 | tf_op jit(solution)/shard_map/ppermute | solution.py:812
  97.4 20.2 %copy-start.2 = (bf16[128,768]{1,0:T(8,128)(2,1)S(1)}, bf16[128,768]{1,0:T(8,128)(2,1)}, u32[]{:S(2)}) copy-start(bf16[128,768]{1,0:T(8,128)(2,1)} %get-tuple-element.113.x_ref) | copy-start | bytes 589828
  110.1 7.5 %collective-permute-start.5 = (bf16[128,768]{1,0:T(8,128)(2,1)}, bf16[128,768]{1,0:T(8,128)(2,1)S(1)}, u32[]{:S(2)}, u32[]{:S(2)}) collective-permute-start(bf16[128,768]{1,0:T(8,128)(2,1)} %get-tuple-element.119), channel_id=1, source_target_pairs={{0,1},{2,3},{4,5},{6,7},{8,9},{10,11},{12,13},{14,15},{16,17},{18,... | collective-permute-start | bytes 589832 | tf_op jit(solution)/shard_map/ppermute | solution.py:820
  131.6 27.9 %copy-start.1 = (bf16[128,768]{1,0:T(8,128)(2,1)S(1)}, bf16[128,768]{1,0:T(8,128)(2,1)}, u32[]{:S(2)}) copy-start(bf16[128,768]{1,0:T(8,128)(2,1)} %get-tuple-element.112.c_ref) | copy-start | bytes 589828
  152.0 7.5 %collective-permute-start.6 = (bf16[128,768]{1,0:T(8,128)(2,1)}, bf16[128,768]{1,0:T(8,128)(2,1)S(1)}, u32[]{:S(2)}, u32[]{:S(2)}) collective-permute-start(bf16[128,768]{1,0:T(8,128)(2,1)} %backward_chain.1), channel_id=1, source_target_pairs={{1,0},{3,2},{5,4},{7,6},{9,8},{11,10},{13,12},{15,14},{17,16},{19,... | collective-permute-start | bytes 589832 | tf_op jit(solution)/shard_map/ppermute | solution.py:820
  178.0 9.9 %collective-permute-start.7 = (bf16[4,4,48,3072]{3,2,1,0:T(8,128)(2,1)}, bf16[4,4,48,3072]{3,2,1,0:T(8,128)(2,1)}, u32[]{:S(2)}, u32[]{:S(2)}) collective-permute-start(bf16[4,4,48,3072]{3,2,1,0:T(8,128)(2,1)} %get-tuple-element.135), channel_id=1, source_target_pairs={{0,64},{64,0},{1,65},{65,1},{2,66},{66,2},{3,67},{67,3},{4,68},{68... | collective-permute-start | bytes 14155784 | tf_op jit(solution)/shard_map/ppermute | solution.py:801
  196.0 66.1 %reduce-scatter.6.cloned.1.call-start = ((), (), s32[]{:S(2)}) async-start(), calls=%async_computation.5 | async-start | bytes 5898240 | tf_op jit(solution)/shard_map/reduce_scatter | solution.py:832
  209.5 8.2 %collective-permute-start.8 = (bf16[4,4,48,3072]{3,2,1,0:T(8,128)(2,1)}, bf16[4,4,48,3072]{3,2,1,0:T(8,128)(2,1)S(1)}, u32[]{:S(2)}, u32[]{:S(2)}) collective-permute-start(bf16[4,4,48,3072]{3,2,1,0:T(8,128)(2,1)} %get-tuple-element.149), channel_id=1, source_target_pairs={{0,64},{64,0},{1,65},{65,1},{2,66},{66,2},{3,67},{67,3},{4,68},{68... | collective-permute-start | bytes 14155784 | tf_op jit(solution)/shard_map/ppermute | solution.py:801
  224.4 103.5 %reduce-scatter.8.cloned.1.call-start = ((), (), s32[]{:S(2)}) async-start(), calls=%async_computation.6 | async-start | bytes 2949120 | tf_op jit(solution)/shard_map/reduce_scatter | solution.py:832
  265.4 1.1 copy-start
  265.4 21.8 %copy-start.8 = (f32[768,64]{1,0:T(8,128)S(1)}, f32[768,64]{1,0:T(8,128)}, u32[]{:S(2)}) copy-start(f32[768,64]{1,0:T(8,128)} %get-tuple-element.156) | copy-start | bytes 589828
  266.5 18.1 %collective-permute-start.10 = (bf16[512,768]{1,0:T(8,128)(2,1)S(1)}, bf16[512,768]{1,0:T(8,128)(2,1)S(1)}, u32[]{:S(2)}, u32[]{:S(2)}) collective-permute-start(bf16[512,768]{1,0:T(8,128)(2,1)S(1)} %copy-done), channel_id=1, source_target_pairs={{0,1},{1,0},{2,3},{3,2},{4,5},{5,4},{6,7},{7,6},{8,9},{9,8},{10,11... | collective-permute-start | bytes 2359304 | tf_op jit(solution)/shard_map/ppermute | solution.py:808
  285.9 39.1 %collective-permute-start.11 = (f32[512,768]{1,0:T(8,128)}, f32[512,768]{1,0:T(8,128)}, u32[]{:S(2)}, u32[]{:S(2)}) collective-permute-start(f32[512,768]{1,0:T(8,128)} %convert_add_fusion), channel_id=1, source_target_pairs={{0,64},{65,1},{2,66},{67,3},{4,68},{69,5},{6,70},{71,7},{8,72},{73... | collective-permute-start | bytes 4718600 | tf_op jit(solution)/shard_map/ppermute | solution.py:805
  287.2 1.7 copy-start.15
  287.2 1.7 copy-start.16
  287.2 1.7 copy-start.17
  287.4 16.7 %copy-start.6 = (bf16[128,768]{1,0:T(8,128)(2,1)S(1)}, bf16[128,768]{1,0:T(8,128)(2,1)}, u32[]{:S(2)}) copy-start(bf16[128,768]{1,0:T(8,128)(2,1)} %get-tuple-element.150) | copy-start | bytes 589828
  287.4 16.7 %copy-start.7 = (bf16[128,768]{1,0:T(8,128)(2,1)S(1)}, bf16[128,768]{1,0:T(8,128)(2,1)}, u32[]{:S(2)}) copy-start(bf16[128,768]{1,0:T(8,128)(2,1)} %get-tuple-element.151) | copy-start | bytes 589828
  289.3 4.1 %collective-permute-start.12 = (f32[8,768]{1,0:T(8,128)S(1)}, f32[8,768]{1,0:T(8,128)S(1)}, u32[]{:S(2)}, u32[]{:S(2)}) collective-permute-start(f32[8,768]{1,0:T(8,128)S(1)} %scatter.19), channel_id=1, source_target_pairs={{0,64},{64,0},{1,65},{65,1},{2,66},{66,2},{3,67},{67,3},{4,68},{68... | collective-permute-start | bytes 73736 | tf_op jit(solution)/shard_map/ppermute | solution.py:890
  293.4 2.7 collective-permute-start.13
  296.1 4.5 %collective-permute-start.14 = (f32[8,768]{1,0:T(8,128)S(1)}, f32[8,768]{1,0:T(8,128)S(1)}, u32[]{:S(2)}, u32[]{:S(2)}) collective-permute-start(f32[8,768]{1,0:T(8,128)S(1)} %add.64), channel_id=1, source_target_pairs={{0,8},{4,12},{8,0},{12,4},{16,24},{20,28},{24,16},{28,20},{32,40},... | collective-permute-start | bytes 73736 | tf_op jit(solution)/shard_map/ppermute | solution.py:890
  300.6 2.7 collective-permute-start.15
  303.3 8.8 %collective-permute-start.16 = (f32[8,768]{1,0:T(8,128)S(1)}, f32[8,768]{1,0:T(8,128)S(1)}, u32[]{:S(2)}, u32[]{:S(2)}) collective-permute-start(f32[8,768]{1,0:T(8,128)S(1)} %add.66), channel_id=1, source_target_pairs={{0,32},{4,36},{8,40},{12,44},{16,48},{20,52},{24,56},{28,60},{32,0... | collective-permute-start | bytes 73736 | tf_op jit(solution)/shard_map/ppermute | solution.py:890
  304.2 20.0 %collective-permute-start.9 = (bf16[2,128,768]{2,1,0:T(8,128)(2,1)S(1)}, bf16[2,128,768]{2,1,0:T(8,128)(2,1)S(1)}, u32[]{:S(2)}, u32[]{:S(2)}) collective-permute-start(bf16[2,128,768]{2,1,0:T(8,128)(2,1)S(1)} %pad_maximum_fusion.2), channel_id=1, source_target_pairs={{64,1},{1,64},{66,3},{3,66},{68,5},{5,68},{70,7},{7,70},{72,9},{9,... | collective-permute-start | bytes 1179656 | tf_op jit(solution)/shard_map/ppermute | solution.py:816
  312.1 8.1 %collective-permute-start.17 = (f32[8,768]{1,0:T(8,128)S(1)}, f32[8,768]{1,0:T(8,128)S(1)}, u32[]{:S(2)}, u32[]{:S(2)}) collective-permute-start(f32[8,768]{1,0:T(8,128)S(1)} %add.67), channel_id=1, source_target_pairs={{0,2},{1,3},{2,0},{3,1},{4,6},{5,7},{6,4},{7,5},{8,10},{9,11},{10,... | collective-permute-start | bytes 73736 | tf_op jit(solution)/shard_map/ppermute | solution.py:890
  320.2 2.7 collective-permute-start.18
  327.8 15.6 %collective-permute-start.19 = (bf16[48,6144]{1,0:T(8,128)(2,1)}, bf16[48,6144]{1,0:T(8,128)(2,1)S(1)}, u32[]{:S(2)}, u32[]{:S(2)}) collective-permute-start(bf16[48,6144]{1,0:T(8,128)(2,1)} %reduce-scatter.8.cloned.1.call-done), channel_id=1, source_target_pairs={{0,3},{1,0},{2,1},{3,2},{4,7},{5,4},{6,5},{7,6},{8,11},{9,8},{10,9... | collective-permute-start | bytes 1769480 | tf_op jit(solution)/shard_map/ppermute | solution.py:905
  327.8 15.6 %collective-permute-start.20 = (bf16[48,6144]{1,0:T(8,128)(2,1)}, bf16[48,6144]{1,0:T(8,128)(2,1)S(1)}, u32[]{:S(2)}, u32[]{:S(2)}) collective-permute-start(bf16[48,6144]{1,0:T(8,128)(2,1)} %reduce-scatter.8.cloned.1.call-done), channel_id=1, source_target_pairs={{0,1},{1,2},{2,3},{3,0},{4,5},{5,6},{6,7},{7,4},{8,9},{9,10},{10,1... | collective-permute-start | bytes 1769480 | tf_op jit(solution)/shard_map/ppermute | solution.py:906
  343.6 7.0 %collective-permute-start.21 = (bf16[48,3072]{1,0:T(8,128)(2,1)S(1)}, bf16[48,3072]{1,0:T(8,128)(2,1)S(1)}, u32[]{:S(2)}, u32[]{:S(2)}) collective-permute-start(bf16[48,3072]{1,0:T(8,128)(2,1)S(1)} %get-tuple-element.213), channel_id=1, source_target_pairs={{0,3},{1,0},{2,1},{3,2},{4,7},{5,4},{6,5},{7,6},{8,11},{9,8},{10,9... | collective-permute-start | bytes 884744 | tf_op jit(solution)/shard_map/ppermute | solution.py:911
  343.6 8.0 %collective-permute-start.22 = (bf16[48,3072]{1,0:T(8,128)(2,1)S(1)}, bf16[48,3072]{1,0:T(8,128)(2,1)S(1)}, u32[]{:S(2)}, u32[]{:S(2)}) collective-permute-start(bf16[48,3072]{1,0:T(8,128)(2,1)S(1)} %get-tuple-element.212), channel_id=1, source_target_pairs={{0,1},{1,2},{2,3},{3,0},{4,5},{5,6},{6,7},{7,4},{8,9},{9,10},{10,1... | collective-permute-start | bytes 884744 | tf_op jit(solution)/shard_map/ppermute | solution.py:912
  351.7 4.4 %collective-permute-start.23 = (bf16[48,6144]{1,0:T(8,128)(2,1)S(1)}, bf16[48,6144]{1,0:T(8,128)(2,1)S(1)}, u32[]{:S(2)}, u32[]{:S(2)}) collective-permute-start(bf16[48,6144]{1,0:T(8,128)(2,1)S(1)} %broadcast_select_fusion.3), channel_id=1, source_target_pairs={{0,64},{64,0},{1,65},{65,1},{2,66},{66,2},{3,67},{67,3},{4,68},{68... | collective-permute-start | bytes 1769480 | tf_op jit(solution)/shard_map/ppermute | solution.py:801
Sparse Core Ops, SparseCore 0:
  17.1 80.2 all-gather.2
  196.1 31.1 reduce-scatter.3
  229.7 32.3 reduce-scatter.5
  265.5 23.8 reduce-scatter.7
